TPU v7x, 128 devices: a whole 4x4x4 slice. The times are simulated.
128 devices in a mesh: dp: 32 (over z, x, core), ep: 4 (over y).
Axes of the slice: x: 4, y: 4, z: 4, core: 2. Of those that a mesh axis runs over, the one named last changes fastest.
Arguments:
- query_rows: bfloat16 [128, 128, 576], P(('dp', 'ep')), may hold values from -65 to 65, as said below
- cache_latent: bfloat16 [524288, 576], P(('dp', 'ep')), may hold values from -6 to 6, as said below
- lengths: int32 [128], replicated, may hold values from 2 to 4096, as said below
- moe_input: bfloat16 [1024, 7168], P(('dp', 'ep')), may hold values from -6 to 6
- expert_ids: int32 [1024, 8], P(('dp', 'ep')), may hold values from 0 to 31, all different within a row; in each aligned block of 8 rows (0 to 7, 8 to 15, ...) at most 4 rows name the same one
- gate_weights: float32 [1024, 8], P(('dp', 'ep')), may hold values from 0.05 to 0.5
- expert_gate: bfloat16 [32, 7168, 1024], P('dp', None, 'ep'), may hold values from -0.0625 to 0.0625
- expert_up: bfloat16 [32, 7168, 1024], P('dp', None, 'ep'), may hold values from -0.0625 to 0.0625
- expert_down: bfloat16 [32, 1024, 7168], P('dp', 'ep'), may hold values from -0.1875 to 0.1875
Outputs:
- attn_out: bfloat16 [128, 128, 512], P(('dp', 'ep'))
- moe_out: bfloat16 [1024, 7168], P(('dp', 'ep'))
Inputs may be any that keep to these rules, and one draw needn't show every extreme that they name: `lengths`: some request has exactly 4096 cached tokens in every draw. `expert_ids`: each row names 8 different experts. Among the rows of one device no expert is named more than 4 times, a bound that some block reaches. `cache_latent`: finite latent entries. `query_rows`: finite query entries.
All inputs are finite; a program needn't handle non-finite values.
Results may differ from a plain program's by a relative error of at most 0.008.
Values may be sent and summed in bfloat16 or wider, within the bound.
No kernel may reach another device: no remote copies, remote signals or barrier semaphores. Data moves between devices by JAX's collectives and lax.ppermute only.
A program may use at most 128 MiB of HBM per device.

v0:
```python
import jax
import jax.numpy as jnp
from jax import lax
from jax.sharding import PartitionSpec as P

WIDTH = 7168
LATENT = 512
TOPK = 8


qk_scale = 192.0 ** (-0.5)
far_low = -1e30
attend_rows = 512


def exchange_in_groups(shard, axis, split_dim, concat_dim, work, item_dim, out_dim):

    def moved(group):
        return lax.all_to_all(group, axis, split_axis=split_dim, concat_axis=concat_dim, tiled=True)

    items = jax.tree.leaves(shard)[0].shape[item_dim]
    ends = [items * k // 2 for k in range(2 + 1)] if items % 2 == 0 else [0, items]
    groups = [
        jax.tree.map(lambda a: lax.slice_in_dim(a, low, high, axis=item_dim), shard)
        for low, high in zip(ends, ends[1:])
    ]
    arrived = [moved(group) for group in groups]
    made = [work(group) for group in arrived]
    return jax.tree.map(lambda *parts: jnp.concatenate(parts, axis=out_dim), *made)


def partial_attend(query_row, key_rows, live_mask):
    scores = qk_scale * lax.dot_general(
        query_row, key_rows, (((1,), (1,)), ((), ())), preferred_element_type=jnp.float32
    )
    scores = jnp.where(live_mask[None, :], scores, far_low)
    score_top = jnp.max(scores, axis=1)
    exponent = jnp.where(live_mask[None, :], jnp.exp(scores - score_top[:, None]), 0.0)
    weight_sum = jnp.sum(exponent, axis=1)
    mixed_values = jnp.dot(
        exponent.astype(jnp.bfloat16), key_rows[:, :LATENT], preferred_element_type=jnp.float32
    )
    return (score_top, weight_sum, mixed_values)


def merge_parts(first, second):
    top_first, sum_first, mix_first = first
    top_second, sum_second, mix_second = second
    score_top = jnp.maximum(top_first, top_second)
    scale_first = jnp.exp(top_first - score_top)
    scale_second = jnp.exp(top_second - score_top)
    return (
        score_top,
        sum_first * scale_first + sum_second * scale_second,
        mix_first * scale_first[:, None] + mix_second * scale_second[:, None],
    )


def local_attend(query_row, cache_rows, keep_end):
    head_count = query_row.shape[0]
    block_total = (keep_end + attend_rows - 1) // attend_rows
    initial = (
        jnp.full((head_count,), far_low, jnp.float32),
        jnp.zeros((head_count,), jnp.float32),
        jnp.zeros((head_count, LATENT), jnp.float32),
    )

    def block_step(block_index, carry):
        start_row = block_index * attend_rows
        key_rows = lax.dynamic_slice_in_dim(cache_rows, start_row, attend_rows, 0)
        live_mask = start_row + jnp.arange(attend_rows, dtype=jnp.int32) < keep_end
        return merge_parts(carry, partial_attend(query_row, key_rows, live_mask))

    return lax.fori_loop(0, block_total, block_step, initial)


def per_device(
    query_rows,
    cache_latent,
    lengths,
    moe_input,
    expert_ids,
    gate_weights,
    expert_gate,
    expert_up,
    expert_down,
):
    ranks_dp = lax.axis_size("dp")
    ranks_ep = lax.axis_size("ep")
    here_dp = lax.axis_index("dp")
    here_ep = lax.axis_index("ep")
    own_rank = here_dp * ranks_ep + here_ep
    own_length = lengths[own_rank]
    query_row = query_rows[0]
    score_top, weight_sum, mixed_values = local_attend(query_row, cache_latent, own_length)
    attn_out = (mixed_values / weight_sum[:, None]).astype(jnp.bfloat16)[None]
    tok_count = moe_input.shape[0]
    slot_count = tok_count * TOPK
    capacity = max(tok_count // 2, tok_count * TOPK // ranks_dp)
    flat_ids = expert_ids.reshape(slot_count)
    onehot = (flat_ids[:, None] == jnp.arange(ranks_dp, dtype=jnp.int32)[None, :]).astype(jnp.int32)
    before = jnp.cumsum(onehot, axis=0) - onehot
    position = jnp.sum(before * onehot, axis=1)
    slot_index = flat_ids * capacity + position
    row_numbers = jnp.arange(ranks_dp * capacity, dtype=jnp.int32)
    dispatch_table = jnp.any(
        row_numbers[:, None, None] == slot_index.reshape(tok_count, TOPK)[None], axis=2
    ).astype(jnp.bfloat16)
    packed = jnp.dot(dispatch_table, moe_input, preferred_element_type=jnp.float32).astype(
        jnp.bfloat16
    )
    packed = packed.reshape(ranks_dp, capacity, WIDTH)
    gate_proj = expert_gate[0]
    up_proj = expert_up[0]
    down_proj = expert_down[0]

    def expert_hidden(row_block):
        gate_act = jnp.dot(row_block, gate_proj, preferred_element_type=jnp.float32)
        up_act = jnp.dot(row_block, up_proj, preferred_element_type=jnp.float32)
        return (jax.nn.silu(gate_act) * up_act).astype(jnp.bfloat16)

    ranks_all = ranks_dp * ranks_ep
    spread = jnp.broadcast_to(packed[:, None], (ranks_dp, ranks_ep, capacity, WIDTH)).reshape(
        ranks_all, capacity, WIDTH
    )

    def direct_work(shard_rows):
        item_count = shard_rows.shape[1]
        flat_rows = shard_rows.reshape(ranks_all * item_count, WIDTH)
        partial_sum = jnp.dot(
            expert_hidden(flat_rows), down_proj, preferred_element_type=jnp.float32
        )
        partial_sum = partial_sum.astype(jnp.bfloat16).reshape(ranks_all, item_count, WIDTH)
        returned = lax.all_to_all(
            partial_sum, ("dp", "ep"), split_axis=0, concat_axis=0, tiled=True
        )
        grouped = returned.reshape(ranks_dp, ranks_ep, item_count, WIDTH)
        running_sum = grouped[:, 0].astype(jnp.float32)
        for group_number in range(1, ranks_ep):
            running_sum = running_sum + grouped[:, group_number].astype(jnp.float32)
        return running_sum.astype(jnp.bfloat16)

    expert_out = exchange_in_groups(spread, ("dp", "ep"), 0, 0, direct_work, 1, 1)
    gathered = expert_out.reshape(ranks_dp * capacity, WIDTH)[slot_index].reshape(
        tok_count, TOPK, WIDTH
    )
    moe_sum = jnp.einsum("tk,tkd->td", gate_weights, gathered.astype(jnp.float32))
    return (attn_out, moe_sum.astype(jnp.bfloat16))


def solution(mesh):
    placed = (
        P(("dp", "ep"), None, None),
        P(("dp", "ep"), None),
        P(),
        P(("dp", "ep"), None),
        P(("dp", "ep"), None),
        P(("dp", "ep"), None),
        P("dp", None, "ep"),
        P("dp", None, "ep"),
        P("dp", "ep", None),
    )
    return jax.shard_map(
        per_device,
        mesh=mesh,
        in_specs=placed,
        out_specs=(P(("dp", "ep"), None, None), P(("dp", "ep"), None)),
        check_vma=False,
    )
```

profile of v0, /device:TPU:6, one launch (start us, length us, event | category | flops | bytes accessed | tf_op | source)
XLA Modules:
  0.0 244.6 jit_solution(14059672276770615462)
XLA Ops:
  3.4 1.7 broadcast_in_dim.52
  5.0 6.7 %broadcast_in_dim.53 = bf16[32,4,4,7168]{3,2,1,0:T(4,128)(2,1)} broadcast(bf16[32,4,7168]{2,1,0:T(4,128)(2,1)} %broadcast_in_dim.52), dimensions={0,2,3} | broadcast | bytes 9175040 | tf_op jit(solution)/shard_map/broadcast_in_dim | solution.py:123
  11.8 9.0 %fusion.63 = (bf16[128,2,7168]{2,1,0:T(2,128)(2,1)}, bf16[128,2,7168]{2,1,0:T(2,128)(2,1)S(1)}) fusion(bf16[128,4,7168]{2,1,0:T(4,128)(2,1)} %bitcast.111), kind=kLoop, calls=%fused_computation.81 | loop fusion | bytes 14680064 | tf_op jit(solution)/shard_map/slice | solution.py:24
  20.8 56.4 %all_to_all.20 = bf16[128,2,7168]{2,1,0:T(2,128)(2,1)} all-to-all(bf16[128,2,7168]{2,1,0:T(2,128)(2,1)S(1)} %get-tuple-element.71), channel_id=1, replica_groups=mesh['dp'=32,'ep'=4] {'dp','ep'}, dimensions={0} | all-to-all | bytes 7340032 | tf_op jit(solution)/shard_map/all_to_all | solution.py:19
  77.2 5.9 %all-to-all-start = ((bf16[128,2,7168]{2,1,0:T(2,128)(2,1)}), bf16[128,2,7168]{2,1,0:T(2,128)(2,1)}, u32[]{:S(2)}, u32[]{:S(2)}) async-start(bf16[128,2,7168]{2,1,0:T(2,128)(2,1)} %get-tuple-element.70), calls=%async_computation | async-start | bytes 7340032 | tf_op jit(solution)/shard_map/all_to_all | solution.py:19
  83.2 8.4 %reshape.97 = bf16[256,7168]{1,0:T(8,128)(2,1)} reshape(bf16[128,2,7168]{2,1,0:T(2,128)(2,1)} %all_to_all.20) | data formatting | bytes 7340032 | tf_op jit(solution)/shard_map/reshape | solution.py:129
  91.6 4.3 %fusion.19 = f32[256,256]{1,0:T(8,128)S(1)} fusion(bf16[256,7168]{1,0:T(8,128)(2,1)} %reshape.97, bf16[1,7168,256]{2,1,0:T(8,128)(2,1)} %param.17), kind=kOutput, calls=%fused_computation.29 | convolution fusion | flops 939524096 | bytes 7602176 | tf_op jit(solution)/shard_map/dot_general | solution.py:118
  95.8 10.0 %convolution_convert_fusion = bf16[256,7168]{1,0:T(8,128)(2,1)} fusion(bf16[1,256,7168]{2,1,0:T(8,128)(2,1)} %param.19, bf16[256,7168]{1,0:T(8,128)(2,1)} %reshape.97, bf16[1,7168,256]{2,1,0:T(8,128)(2,1)} %param.18, f32[256,256]{1,0:T(8,128)S(1)} %fusion.19), kind=kOutput, calls=%fused_computation.20 | convolution fusion | flops 1881276416 | bytes 14942208 | tf_op jit(solution)/shard_map/dot_general | solution.py:130
  105.8 8.1 %reshape.98 = bf16[128,2,7168]{2,1,0:T(2,128)(2,1)} reshape(bf16[256,7168]{1,0:T(8,128)(2,1)} %convolution_convert_fusion) | data formatting | bytes 7340032 | tf_op jit(solution)/shard_map/reshape | solution.py:133
  114.0 15.1 %all-to-all-done = bf16[128,2,7168]{2,1,0:T(2,128)(2,1)} async-done(((bf16[128,2,7168]{2,1,0:T(2,128)(2,1)}), bf16[128,2,7168]{2,1,0:T(2,128)(2,1)}, u32[]{:S(2)}, u32[]{:S(2)}) %all-to-all-start) | async-done | bytes 3670048 | tf_op jit(solution)/shard_map/all_to_all | solution.py:19
  129.0 5.9 %all-to-all-start.3 = ((bf16[128,2,7168]{2,1,0:T(2,128)(2,1)}), bf16[128,2,7168]{2,1,0:T(2,128)(2,1)}, u32[]{:S(2)}, u32[]{:S(2)}) async-start(bf16[128,2,7168]{2,1,0:T(2,128)(2,1)} %reshape.98), calls=%async_computation.3 | async-start | bytes 7340032 | tf_op jit(solution)/shard_map/all_to_all | solution.py:134
  136.4 8.4 %reshape.94 = bf16[256,7168]{1,0:T(8,128)(2,1)} reshape(bf16[128,2,7168]{2,1,0:T(2,128)(2,1)} %all-to-all-done) | data formatting | bytes 7340032 | tf_op jit(solution)/shard_map/reshape | solution.py:129
  144.8 4.3 %fusion.21 = f32[256,256]{1,0:T(8,128)S(1)} fusion(bf16[256,7168]{1,0:T(8,128)(2,1)} %reshape.94, bf16[1,7168,256]{2,1,0:T(8,128)(2,1)} %param.17), kind=kOutput, calls=%fused_computation.31 | convolution fusion | flops 939524096 | bytes 7602176 | tf_op jit(solution)/shard_map/dot_general | solution.py:118
  149.1 10.0 %convolution_convert_fusion.1 = bf16[256,7168]{1,0:T(8,128)(2,1)} fusion(bf16[1,256,7168]{2,1,0:T(8,128)(2,1)} %param.19, bf16[256,7168]{1,0:T(8,128)(2,1)} %reshape.94, bf16[1,7168,256]{2,1,0:T(8,128)(2,1)} %param.18, f32[256,256]{1,0:T(8,128)S(1)} %fusion.21), kind=kOutput, calls=%fused_computation.21 | convolution fusion | flops 1881276416 | bytes 14942208 | tf_op jit(solution)/shard_map/dot_general | solution.py:130
  159.1 8.1 %reshape.95 = bf16[128,2,7168]{2,1,0:T(2,128)(2,1)} reshape(bf16[256,7168]{1,0:T(8,128)(2,1)} %convolution_convert_fusion.1) | data formatting | bytes 7340032 | tf_op jit(solution)/shard_map/reshape | solution.py:133
  167.2 13.6 %all-to-all-done.3 = bf16[128,2,7168]{2,1,0:T(2,128)(2,1)} async-done(((bf16[128,2,7168]{2,1,0:T(2,128)(2,1)}), bf16[128,2,7168]{2,1,0:T(2,128)(2,1)}, u32[]{:S(2)}, u32[]{:S(2)}) %all-to-all-start.3) | async-done | bytes 3670048 | tf_op jit(solution)/shard_map/all_to_all | solution.py:134
  180.8 5.9 %all-to-all-start.1 = ((bf16[128,2,7168]{2,1,0:T(2,128)(2,1)}), bf16[128,2,7168]{2,1,0:T(2,128)(2,1)}, u32[]{:S(2)}, u32[]{:S(2)}) async-start(bf16[128,2,7168]{2,1,0:T(2,128)(2,1)} %reshape.95), calls=%async_computation.1 | async-start | bytes 7340032 | tf_op jit(solution)/shard_map/all_to_all | solution.py:134
  186.8 15.7 %while.14 = (s32[]{:T(128)}, f32[128]{0:T(128)S(1)}, f32[128]{0:T(128)S(1)}, f32[128,512]{1,0:T(8,128)S(1)}, s32[]{:T(128)}, /*index=5*/s32[]{:T(128)}, bf16[409...) while((s32[]{:T(128)}, f32[128]{0:T(128)S(1)}, ...), condition=%wide.region_3.4_spmd, body=%wide.region_0.3_spmd.sunk | while | flops 143394304 | bytes 2581683 | solution.py:74
  193.0 1.5 fusion.83
  203.3 3.4 %fusion.42 = bf16[32,2,7168]{2,1,0:T(2,128)(2,1)S(1)} fusion(bf16[32,4,2,7168]{3,2,1,0:T(2,128)(2,1)} %bitcast.9), kind=kLoop, calls=%fused_computation.51 | loop fusion | flops 3670016 | bytes 4587520 | tf_op jit(solution)/shard_map/add | solution.py:140
  206.7 25.9 %all-to-all-done.1 = bf16[128,2,7168]{2,1,0:T(2,128)(2,1)} async-done(((bf16[128,2,7168]{2,1,0:T(2,128)(2,1)}), bf16[128,2,7168]{2,1,0:T(2,128)(2,1)}, u32[]{:S(2)}, u32[]{:S(2)}) %all-to-all-start.1) | async-done | bytes 3670048 | tf_op jit(solution)/shard_map/all_to_all | solution.py:134
  232.6 3.4 %fusion.41 = bf16[32,2,7168]{2,1,0:T(2,128)(2,1)S(1)} fusion(bf16[32,4,2,7168]{3,2,1,0:T(2,128)(2,1)} %bitcast.7), kind=kLoop, calls=%fused_computation.50 | loop fusion | flops 3670016 | bytes 4587520 | tf_op jit(solution)/shard_map/add | solution.py:140
  236.0 3.4 %pad_maximum_fusion = bf16[32,4,7168]{2,1,0:T(4,128)(2,1)} fusion(bf16[32,2,7168]{2,1,0:T(2,128)(2,1)S(1)} %fusion.42, bf16[32,2,7168]{2,1,0:T(2,128)(2,1)S(1)} %fusion.41), kind=kLoop, calls=%fused_computation.33 | loop fusion | flops 3670016 | bytes 3670016 | tf_op jit(solution)/shard_map/concatenate | solution.py:29
  239.4 3.0 %reshape.100 = bf16[128,7168]{1,0:T(8,128)(2,1)S(1)} reshape(bf16[32,4,7168]{2,1,0:T(4,128)(2,1)} %pad_maximum_fusion) | data formatting | bytes 3670016 | tf_op jit(solution)/shard_map/reshape | solution.py:144
  (49 shorter events, 20.3 us)
Async XLA Ops:
  0.6 2.1 copy-start
  77.2 51.8 %all-to-all-start = ((bf16[128,2,7168]{2,1,0:T(2,128)(2,1)}), bf16[128,2,7168]{2,1,0:T(2,128)(2,1)}, u32[]{:S(2)}, u32[]{:S(2)}) async-start(bf16[128,2,7168]{2,1,0:T(2,128)(2,1)} %get-tuple-element.70), calls=%async_computation | async-start | bytes 7340032 | tf_op jit(solution)/shard_map/all_to_all | solution.py:19
  114.0 21.0 %copy-start.4 = (s32[128]{0:T(128)S(1)}, s32[128]{0:T(128)}, u32[]{:S(2)}) copy-start(s32[128]{0:T(128)} %param.13) | copy-start | bytes 1540
  114.0 22.3 %copy-start.2 = (bf16[1,128,576]{1,2,0:T(8,128)(2,1)S(1)}, bf16[1,128,576]{1,2,0:T(8,128)(2,1)}, u32[]{:S(2)}) copy-start(bf16[1,128,576]{1,2,0:T(8,128)(2,1)} %param.11) | copy-start | bytes 442372
  129.0 51.8 %all-to-all-start.3 = ((bf16[128,2,7168]{2,1,0:T(2,128)(2,1)}), bf16[128,2,7168]{2,1,0:T(2,128)(2,1)}, u32[]{:S(2)}, u32[]{:S(2)}) async-start(bf16[128,2,7168]{2,1,0:T(2,128)(2,1)} %reshape.98), calls=%async_computation.3 | async-start | bytes 7340032 | tf_op jit(solution)/shard_map/all_to_all | solution.py:134
  180.8 51.8 %all-to-all-start.1 = ((bf16[128,2,7168]{2,1,0:T(2,128)(2,1)}), bf16[128,2,7168]{2,1,0:T(2,128)(2,1)}, u32[]{:S(2)}, u32[]{:S(2)}) async-start(bf16[128,2,7168]{2,1,0:T(2,128)(2,1)} %reshape.95), calls=%async_computation.1 | async-start | bytes 7340032 | tf_op jit(solution)/shard_map/all_to_all | solution.py:134
  239.4 5.2 %copy-start.1 = (bf16[8,7168]{1,0:T(8,128)(2,1)S(1)}, bf16[8,7168]{1,0:T(8,128)(2,1)}, u32[]{:S(2)}) copy-start(bf16[8,7168]{1,0:T(8,128)(2,1)} %param.14) | copy-start | bytes 344068
  242.4 1.1 copy-start.3
where the time goes:
time: 249 us; the launch traced here: 245 us
  local copies, waits for them, and re-layouts  57 us (23%)
  blocking collectives  56.4 us (23%)
  waiting for transfers between devices  54.6 us (22%)
  matrix products  41.5 us (17%)
  starting transfers between devices  17.8 us (7%)
  other arithmetic  15.4 us (6%)
    all_to_all x1, blocking collectives, moved(): lax.all_to_all(group, axis, split_axis=split_dim, concat_axis=concat_dim,...  56.4 us
    all_to_all x2, waiting for transfers between devices, direct_work(): lax.all_to_all(partial_sum, ('dp', 'ep'), split_axis=0, concat_axis=0, ti...  39.5 us
    dot_general x2, matrix products, direct_work(): jnp.dot(expert_hidden(flat_rows), down_proj, preferred_element_type=jnp.f...  20 us
    reshape x2, local copies, waits for them, and re-layouts, direct_work(): flat_rows = shard_rows.reshape(ranks_all * item_count, WIDTH)  16.8 us
    reshape x2, local copies, waits for them, and re-layouts, direct_work(): partial_sum.astype(jnp.bfloat16).reshape(ranks_all, item_count, WIDTH)  16.2 us
    all_to_all x1, waiting for transfers between devices, moved(): lax.all_to_all(group, axis, split_axis=split_dim, concat_axis=concat_dim,...  15.1 us
    all_to_all x2, starting transfers between devices, direct_work(): lax.all_to_all(partial_sum, ('dp', 'ep'), split_axis=0, concat_axis=0, ti...  11.8 us
    slice x1, local copies, waits for them, and re-layouts, exchange_in_groups(): lax.slice_in_dim(a, low, high, axis=item_dim)  9.04 us
  transfers between devices with their start and end apart: 3, of which 3 were waited for; matrix products, arithmetic and copies ran while one was open for 33% of the time, Pallas kernels for 0%

commit v1 on v0

v1 whole, which is shorter than its diff:
```python
import jax
import jax.numpy as jnp
from jax import lax
from jax.experimental import pallas as pl
from jax.experimental.pallas import tpu as pltpu
from jax.sharding import Mesh, PartitionSpec as P

WIDTH = 7168
LATENT = 512
KEY_DIM = 576
HEADS = 128
EXPERTS = 32
CTX = 4096
UNITS = 256
TOK = 8
CHIPS = 64
ROWS = CHIPS * TOK
PAY = WIDTH + 128
QK_SCALE = 192.0 ** (-0.5)
FAR_LOW = -1e30
ATT_ROWS = 1024
K_STEP = 512
N_TILE = 896
RET_CUTS = (0, 3584, 7168)
BF = jnp.bfloat16
F32 = jnp.float32
CHIP_AXES = ("z", "x", "y")


def attend_kernel(length_ref, query_ref, cache_ref, out_ref, top_ref, sum_ref, mix_ref):
    step = pl.program_id(0)
    length = length_ref[0]

    @pl.when(step == 0)
    def _():
        top_ref[...] = jnp.full_like(top_ref, FAR_LOW)
        sum_ref[...] = jnp.zeros_like(sum_ref)
        mix_ref[...] = jnp.zeros_like(mix_ref)

    @pl.when(step * ATT_ROWS < length)
    def _():
        rows = cache_ref[...]
        scores = QK_SCALE * lax.dot_general(
            query_ref[0], rows, (((1,), (1,)), ((), ())), preferred_element_type=F32
        )
        place = step * ATT_ROWS + lax.broadcasted_iota(jnp.int32, scores.shape, 1)
        scores = jnp.where(place < length, scores, FAR_LOW)
        top_old = top_ref[...]
        top_new = jnp.maximum(top_old, jnp.max(scores, axis=1, keepdims=True))
        weights = jnp.exp(scores - top_new)
        scale = jnp.exp(top_old - top_new)
        top_ref[...] = top_new
        sum_ref[...] = sum_ref[...] * scale + jnp.sum(weights, axis=1, keepdims=True)
        mix_ref[...] = mix_ref[...] * scale + jnp.dot(
            weights.astype(BF), rows[:, :LATENT], preferred_element_type=F32
        )

    @pl.when(step == pl.num_programs(0) - 1)
    def _():
        out_ref[0] = (mix_ref[...] / sum_ref[...]).astype(BF)


def attend(length, query_rows, cache_latent):
    def cache_block(step, length_ref):
        return jnp.minimum(step, (length_ref[0] - 1) // ATT_ROWS), 0

    return pl.pallas_call(
        attend_kernel,
        grid_spec=pltpu.PrefetchScalarGridSpec(
            num_scalar_prefetch=1,
            grid=(CTX // ATT_ROWS,),
            in_specs=[
                pl.BlockSpec((1, HEADS, KEY_DIM), lambda step, length_ref: (0, 0, 0)),
                pl.BlockSpec((ATT_ROWS, KEY_DIM), cache_block),
            ],
            out_specs=pl.BlockSpec((1, HEADS, LATENT), lambda step, length_ref: (0, 0, 0)),
            scratch_shapes=[
                pltpu.VMEM((HEADS, 1), F32),
                pltpu.VMEM((HEADS, 1), F32),
                pltpu.VMEM((HEADS, LATENT), F32),
            ],
        ),
        out_shape=jax.ShapeDtypeStruct((1, HEADS, LATENT), BF),
        compiler_params=pltpu.CompilerParams(vmem_limit_bytes=24 * 2**20),
        cost_estimate=pl.CostEstimate(
            flops=2 * HEADS * CTX * (KEY_DIM + LATENT),
            bytes_accessed=CTX * KEY_DIM * 2,
            transcendentals=HEADS * CTX,
        ),
        name="attend",
    )(length, query_rows, cache_latent)


def hidden_kernel(x_ref, tail_ref, pick_ref, g0, u0, g1, u1, out_ref, acc_ref):
    step = pl.program_id(0)
    x = x_ref[...]

    @pl.when(step == 0)
    def _():
        acc_ref[...] = jnp.zeros_like(acc_ref)

    for place, weight in enumerate((g0, g1, u0, u1)):
        acc_ref[:, place * UNITS : (place + 1) * UNITS] += jnp.dot(
            x, weight[...], preferred_element_type=F32
        )

    @pl.when(step == pl.num_programs(0) - 1)
    def _():
        share = jnp.dot(tail_ref[...], pick_ref[...], preferred_element_type=F32)
        gate = acc_ref[:, : 2 * UNITS]
        up = acc_ref[:, 2 * UNITS :]
        out_ref[...] = (gate / (1.0 + jnp.exp(-gate)) * up * share).astype(BF)


def hidden_of(payload, pick, gate_own, up_own, gate_other, up_other):
    weight = pl.BlockSpec((K_STEP, UNITS), lambda step: (step, 0))
    return pl.pallas_call(
        hidden_kernel,
        grid=(WIDTH // K_STEP,),
        in_specs=[
            pl.BlockSpec((ROWS, K_STEP), lambda step: (0, step)),
            pl.BlockSpec((ROWS, 128), lambda step: (0, WIDTH // 128)),
            pl.BlockSpec((128, 2 * UNITS), lambda step: (0, 0)),
            weight,
            weight,
            weight,
            weight,
        ],
        out_specs=pl.BlockSpec((ROWS, 2 * UNITS), lambda step: (0, 0)),
        out_shape=jax.ShapeDtypeStruct((ROWS, 2 * UNITS), BF),
        scratch_shapes=[pltpu.VMEM((ROWS, 4 * UNITS), F32)],
        compiler_params=pltpu.CompilerParams(vmem_limit_bytes=32 * 2**20),
        cost_estimate=pl.CostEstimate(
            flops=2 * ROWS * WIDTH * 4 * UNITS,
            bytes_accessed=2 * (ROWS * PAY + 4 * UNITS * WIDTH),
            transcendentals=ROWS * 2 * UNITS,
        ),
        name="hidden",
    )(payload, payload, pick, gate_own, up_own, gate_other, up_other)


def down_kernel(h_ref, d0, d1, out_ref):
    out_ref[...] = (
        jnp.dot(h_ref[:, :UNITS], d0[...], preferred_element_type=F32)
        + jnp.dot(h_ref[:, UNITS:], d1[...], preferred_element_type=F32)
    ).astype(BF)


def down_of(hidden, down_own, down_other, low, high):
    first = low // N_TILE
    weight = pl.BlockSpec((UNITS, N_TILE), lambda step: (0, step + first))
    return pl.pallas_call(
        down_kernel,
        grid=((high - low) // N_TILE,),
        in_specs=[pl.BlockSpec((ROWS, 2 * UNITS), lambda step: (0, 0)), weight, weight],
        out_specs=pl.BlockSpec((ROWS, N_TILE), lambda step: (0, step)),
        out_shape=jax.ShapeDtypeStruct((ROWS, high - low), BF),
        compiler_params=pltpu.CompilerParams(vmem_limit_bytes=24 * 2**20),
        cost_estimate=pl.CostEstimate(
            flops=2 * ROWS * 2 * UNITS * (high - low),
            bytes_accessed=2 * (ROWS * 2 * UNITS + (ROWS + 2 * UNITS) * (high - low)),
            transcendentals=0,
        ),
        name="down",
    )(hidden, down_own, down_other)


def swap(array):
    return lax.ppermute(array, "core", [(0, 1), (1, 0)])


def payload_of(moe_input, expert_ids, gate_weights):
    chosen = expert_ids[:, :, None] == jnp.arange(EXPERTS, dtype=jnp.int32)
    shares = jnp.sum(jnp.where(chosen, gate_weights[:, :, None], 0.0), axis=1)
    high = lax.reduce_precision(shares, 8, 7)
    middle = lax.reduce_precision(shares - high, 8, 7)
    low = lax.reduce_precision(shares - high - middle, 8, 7)
    blank = jnp.zeros((TOK, 128 - 3 * EXPERTS), F32)
    tail = jnp.concatenate([high, middle, low, blank], axis=1).astype(BF)
    return jnp.concatenate([moe_input, tail], axis=1)


def per_device(
    query_rows,
    cache_latent,
    lengths,
    moe_input,
    expert_ids,
    gate_weights,
    expert_gate,
    expert_up,
    expert_down,
):
    chip = (lax.axis_index("z") * 4 + lax.axis_index("x")) * 2
    own = chip + lax.axis_index("core")
    other = chip + 1 - lax.axis_index("core")
    length = lax.dynamic_slice_in_dim(lengths, own * 4 + lax.axis_index("y"), 1)

    payload = payload_of(moe_input, expert_ids, gate_weights)
    arrived = lax.all_gather(payload, CHIP_AXES, axis=0, tiled=True)

    gate_own, up_own, down_own = expert_gate[0], expert_up[0], expert_down[0]
    gate_other, up_other, down_other = swap(gate_own), swap(up_own), swap(down_own)
    attn_out = attend(length, query_rows, cache_latent)

    row = lax.broadcasted_iota(jnp.int32, (128, 2 * UNITS), 0)
    column = lax.broadcasted_iota(jnp.int32, (128, 2 * UNITS), 1)
    wanted = jnp.where(column < UNITS, own, other)
    pick = ((row % EXPERTS == wanted) & (row < 3 * EXPERTS)).astype(BF)

    hidden = hidden_of(arrived, pick, gate_own, up_own, gate_other, up_other)
    sums = []
    for low, high in zip(RET_CUTS, RET_CUTS[1:]):
        made = down_of(hidden, down_own, down_other, low, high).reshape(CHIPS, TOK, high - low)
        back = lax.all_to_all(made, CHIP_AXES, split_axis=0, concat_axis=0, tiled=True)
        sums.append(jnp.sum(back.astype(F32), axis=0).astype(BF))
    return attn_out, jnp.concatenate(sums, axis=1)


def solution(mesh):
    fine = Mesh(mesh.devices.reshape(4, 4, 2, 4), ("z", "x", "core", "y"))
    dp = ("z", "x", "core")
    both = ("z", "x", "core", "y")
    return jax.shard_map(
        per_device,
        mesh=fine,
        in_specs=(
            P(both, None, None),
            P(both, None),
            P(),
            P(both, None),
            P(both, None),
            P(both, None),
            P(dp, None, "y"),
            P(dp, None, "y"),
            P(dp, "y", None),
        ),
        out_specs=(P(both, None, None), P(both, None)),
        check_vma=False,
    )
```

time: 249 us -> 238 us (0.956); the launches traced: 245 us -> 237 us
  waiting for transfers between devices: 54.6 us -> 144 us
  blocking collectives: 56.4 us -> 0 us
  matrix products: 41.5 us -> 0 us
  local copies, waits for them, and re-layouts: 57 us -> 25.6 us
  Pallas kernels: 0 us -> 29.3 us
  between operations: 1.5 us -> 14.2 us
  other arithmetic: 15.4 us -> 6.72 us
    all_gather x0 -> x1, waiting for transfers between devices: none -> 67.6 us  [per_device(): arrived = lax.all_gather(payload, CHIP_AXES, axis=0, tiled=True)]
    all_to_all x1 -> x0, blocking collectives: 56.4 us -> none  [moved(): lax.all_to_all(group, axis, split_axis=split_dim, concat_axis=concat_dim,...]
    dot_general x14 -> x0, matrix products: 41.5 us -> none  [the longest x2 20 us: direct_work(): jnp.dot(expert_hidden(flat_rows), down_proj, preferred_element_type=jnp.f...]
    reshape x5 -> x0, local copies, waits for them, and re-layouts: 36 us -> none  [the longest x2 16.8 us: direct_work(): flat_rows = shard_rows.reshape(ranks_all * item_count, WIDTH)]
    pallas_call x0 -> x4, Pallas kernels: none -> 29.3 us  [the longest x1 14.6 us: hidden_of(): pl.pallas_call(hidden_kernel, grid=(WIDTH // K_STEP,), in_specs=[pl.Block...]
    unnamed x11 -> x22, local copies, waits for them, and re-layouts: 0.19 us -> 23.4 us
    ppermute x0 -> x3, waiting for transfers between devices: none -> 11.2 us  [swap(): return lax.ppermute(array, 'core', [(0, 1), (1, 0)])]
    all_to_all x3 -> x2, waiting for transfers between devices: 54.6 us -> 65.1 us  [per_device(): lax.all_to_all(made, CHIP_AXES, split_axis=0, concat_axis=0, tiled=True)]
  transfers between devices with their start and end apart: 3 -> 6, of which waited for: 3 -> 5; matrix products, arithmetic and copies ran while one was open for 33% -> 5% of each run, Pallas kernels for 0% -> 10%
where the time goes in v1:
time: 238 us; the launch traced here: 237 us
  waiting for transfers between devices  144 us (61%)
  Pallas kernels  29.3 us (12%)
  local copies, waits for them, and re-layouts  25.6 us (11%)
  starting transfers between devices  17 us (7%)
  between operations  14.2 us (6%)
  other arithmetic  6.72 us (3%)
    all_gather x1, waiting for transfers between devices, per_device(): arrived = lax.all_gather(payload, CHIP_AXES, axis=0, tiled=True)  67.6 us
    all_to_all x2, waiting for transfers between devices, per_device(): lax.all_to_all(made, CHIP_AXES, split_axis=0, concat_axis=0, tiled=True)  65.1 us
    unnamed x22, local copies, waits for them, and re-layouts  23.4 us
    all_to_all x2, starting transfers between devices, per_device(): lax.all_to_all(made, CHIP_AXES, split_axis=0, concat_axis=0, tiled=True)  16.3 us
    pallas_call x1, Pallas kernels, hidden_of(): pl.pallas_call(hidden_kernel, grid=(WIDTH // K_STEP,), in_specs=[pl.Block...  14.6 us
    ppermute x3, waiting for transfers between devices, swap(): return lax.ppermute(array, 'core', [(0, 1), (1, 0)])  11.2 us
    pallas_call x2, Pallas kernels, down_of(): pl.pallas_call(down_kernel, grid=((high - low) // N_TILE,), in_specs=[pl....  9.09 us
    pallas_call x1, Pallas kernels, attend(): pl.pallas_call(attend_kernel, grid_spec=pltpu.PrefetchScalarGridSpec(num_...  5.59 us
  transfers between devices with their start and end apart: 6, of which 5 were waited for; matrix products, arithmetic and copies ran while one was open for 5% of the time, Pallas kernels for 10%

profile of v1, /device:TPU:6, one launch (start us, length us, event | category | flops | bytes accessed | tf_op | source)
XLA Modules:
  0.0 236.8 jit_solution(16015135396733113267)
XLA Ops:
  7.2 0.8 select_reduce_fusion
  8.0 1.6 concatenate.9
  10.5 6.0 %collective-permute-done.g1 = bf16[7168,256]{1,0:T(8,128)(2,1)} collective-permute-done((bf16[7168,256]{1,0:T(8,128)(2,1)}, bf16[7168,256]{1,0:T(8,128)(2,1)}, u32[]{:S(2)}, u32[]{:S(2)}) %collective-permute-start) | collective-permute-done | bytes 3670048 | tf_op jit(solution)/shard_map/ppermute | solution.py:169
  16.5 5.2 %collective-permute-done.1.u1 = bf16[7168,256]{1,0:T(8,128)(2,1)} collective-permute-done((bf16[7168,256]{1,0:T(8,128)(2,1)}, bf16[7168,256]{1,0:T(8,128)(2,1)}, u32[]{:S(2)}, u32[]{:S(2)}) %collective-permute-start.1) | collective-permute-done | bytes 3670048 | tf_op jit(solution)/shard_map/ppermute | solution.py:169
  21.8 67.6 %all-gather.2.cloned.1.call-done.x_ref.tail_ref = bf16[512,7296]{1,0:T(8,128)(2,1)} async-done(((bf16[8,7296]{1,0:T(8,128)(2,1)}), bf16[512,7296]{1,0:T(8,128)(2,1)}) %all-gather.2.cloned.1.call-update) | async-done | bytes 7471120 | tf_op jit(solution)/shard_map/all_gather | solution.py:200
  89.4 3.1 %copy-done = bf16[512,7296]{1,0:T(8,128)(2,1)S(1)} copy-done((bf16[512,7296]{1,0:T(8,128)(2,1)S(1)}, bf16[512,7296]{1,0:T(8,128)(2,1)}, u32[]{:S(2)}) %copy-start) | copy-done | bytes 7471128
  92.5 2.0 copy-done.6
  94.5 2.0 copy-done.7
  96.6 14.6 %hidden.1.h_ref = bf16[512,512]{1,0:T(8,128)(2,1)S(1)} custom-call(bf16[512,7296]{1,0:T(8,128)(2,1)S(1)} %copy-done, bf16[512,7296]{1,0:T(8,128)(2,1)S(1)} %copy-done, bf16[128,512]{1,0:T(8,128)(2,1)S(1)} %fusion.1.pick_ref, bf16[7168,256]{1,0:T(8,128)(2,1)S(1)} %bitcast.11, bf16[7168,256]{1,0:T(8,128)(2,1)S(1)} %bitcast.13, ...), custom_call_target="tpu_custom_call" | custom-call | flops 7516192768 | bytes 22151168 | tf_op jit(solution)/shard_map/hidden/pallas_call | solution.py:117
  111.2 4.5 %down.2 = bf16[512,3584]{1,0:T(8,128)(2,1)S(1)} custom-call(bf16[512,512]{1,0:T(8,128)(2,1)S(1)} %hidden.1.h_ref, bf16[256,7168]{1,0:T(8,128)(2,1)S(1)} %bitcast.8, bf16[256,7168]{1,0:T(8,128)(2,1)} %collective-permute-done.2.d1), custom_call_target="tpu_custom_call" | custom-call | flops 1879048192 | bytes 7864320 | tf_op jit(solution)/shard_map/down/pallas_call | solution.py:152
  115.8 1.9 copy-done.3
  117.7 8.9 %all-to-all-start = ((bf16[64,8,3584]{2,1,0:T(8,128)(2,1)}), bf16[64,8,3584]{2,1,0:T(8,128)(2,1)}, u32[]{:S(2)}, u32[]{:S(2)}) async-start(bf16[64,8,3584]{2,1,0:T(8,128)(2,1)} %bitcast.6), calls=%async_computation | async-start | bytes 7340032 | tf_op jit(solution)/shard_map/all_to_all | solution.py:215
  126.5 2.0 copy-done.5
  128.6 4.5 %down.3 = bf16[512,3584]{1,0:T(8,128)(2,1)S(1)} custom-call(bf16[512,512]{1,0:T(8,128)(2,1)S(1)} %hidden.1.h_ref, bf16[256,7168]{1,0:T(8,128)(2,1)S(1)} %bitcast.9, bf16[256,7168]{1,0:T(8,128)(2,1)} %collective-permute-done.2.d1), custom_call_target="tpu_custom_call" | custom-call | flops 1879048192 | bytes 7864320 | tf_op jit(solution)/shard_map/down/pallas_call | solution.py:152
  133.1 1.8 copy-done.2
  135.0 38.4 %all-to-all-done = bf16[64,8,3584]{2,1,0:T(8,128)(2,1)} async-done(((bf16[64,8,3584]{2,1,0:T(8,128)(2,1)}), bf16[64,8,3584]{2,1,0:T(8,128)(2,1)}, u32[]{:S(2)}, u32[]{:S(2)}) %all-to-all-start) | async-done | bytes 3670048 | tf_op jit(solution)/shard_map/all_to_all | solution.py:215
  173.3 7.4 %all-to-all-start.1 = ((bf16[64,8,3584]{2,1,0:T(8,128)(2,1)}), bf16[64,8,3584]{2,1,0:T(8,128)(2,1)}, u32[]{:S(2)}, u32[]{:S(2)}) async-start(bf16[64,8,3584]{2,1,0:T(8,128)(2,1)} %bitcast.5), calls=%async_computation.1 | async-start | bytes 7340032 | tf_op jit(solution)/shard_map/all_to_all | solution.py:215
  180.8 7.7 %copy.14.cache_ref = bf16[4096,576]{1,0:T(8,128)(2,1)} copy(bf16[4096,576]{0,1:T(8,128)(2,1)} %param.10) | data formatting | bytes 9437184 | tf_op args[1]
  189.3 2.5 %copy-done.1 = bf16[4096,576]{1,0:T(8,128)(2,1)S(1)} copy-done((bf16[4096,576]{1,0:T(8,128)(2,1)S(1)}, bf16[4096,576]{1,0:T(8,128)(2,1)}, u32[]{:S(2)}) %copy-start.1) | copy-done | bytes 4718616
  191.8 5.6 %attend.1 = bf16[1,128,512]{2,1,0:T(8,128)(2,1)} custom-call(s32[1]{0:T(128)} %dynamic_slice.3.length_ref, bf16[1,128,576]{2,1,0:T(8,128)(2,1)S(1)} %copy.13.query_ref, bf16[4096,576]{1,0:T(8,128)(2,1)S(1)} %copy-done.1), custom_call_target="tpu_custom_call" | custom-call | flops 1140850688 | bytes 4718592 | tf_op jit(solution)/shard_map/attend/pallas_call | solution.py:67
  197.4 2.6 %reduce_sum.34 = bf16[8,3584]{1,0:T(8,128)(2,1)S(1)} reduce(bf16[64,8,3584]{2,1,0:T(8,128)(2,1)} %all-to-all-done, bf16[]{:T(256)} %constant.46.clone.1), dimensions={0}, to_apply=%region_1.2 | reduce | flops 1806336 | bytes 3727362 | tf_op jit(solution)/shard_map/reduce_sum | solution.py:216
  199.9 26.8 %all-to-all-done.1 = bf16[64,8,3584]{2,1,0:T(8,128)(2,1)} async-done(((bf16[64,8,3584]{2,1,0:T(8,128)(2,1)}), bf16[64,8,3584]{2,1,0:T(8,128)(2,1)}, u32[]{:S(2)}, u32[]{:S(2)}) %all-to-all-start.1) | async-done | bytes 3670048 | tf_op jit(solution)/shard_map/all_to_all | solution.py:215
  226.7 2.6 %reduce_sum.35 = bf16[8,3584]{1,0:T(8,128)(2,1)S(1)} reduce(bf16[64,8,3584]{2,1,0:T(8,128)(2,1)} %all-to-all-done.1, bf16[]{:T(256)} %constant.46.clone.1), dimensions={0}, to_apply=%region_2.3 | reduce | flops 1806336 | bytes 3727362 | tf_op jit(solution)/shard_map/reduce_sum | solution.py:216
  229.3 0.7 pad_maximum_fusion
  (27 shorter events, 1.7 us)
Async XLA Ops:
  7.2 82.2 %all-gather.2.cloned.1.call-start = ((), (), s32[]{:S(2)}) async-start(), calls=%async_computation.2 | async-start | bytes 7587840 | tf_op jit(solution)/shard_map/all_gather | solution.py:200
  9.7 6.8 %collective-permute-start = (bf16[7168,256]{1,0:T(8,128)(2,1)}, bf16[7168,256]{1,0:T(8,128)(2,1)}, u32[]{:S(2)}, u32[]{:S(2)}) collective-permute-start(bf16[7168,256]{1,0:T(8,128)(2,1)} %bitcast.10), channel_id=1, source_target_pairs={{0,4},{4,0},{1,5},{5,1},{2,6},{6,2},{3,7},{7,3},{8,12},{12,8},{9,1... | collective-permute-start | bytes 11010056 | tf_op jit(solution)/shard_map/ppermute | solution.py:169
  9.8 12.0 %collective-permute-start.1 = (bf16[7168,256]{1,0:T(8,128)(2,1)}, bf16[7168,256]{1,0:T(8,128)(2,1)}, u32[]{:S(2)}, u32[]{:S(2)}) collective-permute-start(bf16[7168,256]{1,0:T(8,128)(2,1)} %bitcast.12), channel_id=1, source_target_pairs={{0,4},{4,0},{1,5},{5,1},{2,6},{6,2},{3,7},{7,3},{8,12},{12,8},{9,1... | collective-permute-start | bytes 11010056 | tf_op jit(solution)/shard_map/ppermute | solution.py:169
  10.3 100.9 %collective-permute-start.2 = (bf16[256,7168]{1,0:T(8,128)(2,1)}, bf16[256,7168]{1,0:T(8,128)(2,1)}, u32[]{:S(2)}, u32[]{:S(2)}) collective-permute-start(bf16[256,7168]{1,0:T(8,128)(2,1)} %bitcast.7), channel_id=1, source_target_pairs={{0,4},{4,0},{1,5},{5,1},{2,6},{6,2},{3,7},{7,3},{8,12},{12,8},{9,1... | collective-permute-start | bytes 11010056 | tf_op jit(solution)/shard_map/ppermute | solution.py:169
  89.4 3.1 %copy-start = (bf16[512,7296]{1,0:T(8,128)(2,1)S(1)}, bf16[512,7296]{1,0:T(8,128)(2,1)}, u32[]{:S(2)}) copy-start(bf16[512,7296]{1,0:T(8,128)(2,1)} %all-gather.2.cloned.1.call-done.x_ref.tail_ref) | copy-start | bytes 22413316
  92.5 2.0 copy-start.6
  94.5 2.0 copy-start.7
  96.6 14.6 %copy-start.4 = (bf16[1,256,7168]{2,1,0:T(8,128)(2,1)S(1)}, bf16[1,256,7168]{2,1,0:T(8,128)(2,1)}, u32[]{:S(2)}) copy-start(bf16[1,256,7168]{2,1,0:T(8,128)(2,1)} %param.17) | copy-start | bytes 11010052
  115.7 1.9 copy-start.3
  117.7 55.7 %all-to-all-start = ((bf16[64,8,3584]{2,1,0:T(8,128)(2,1)}), bf16[64,8,3584]{2,1,0:T(8,128)(2,1)}, u32[]{:S(2)}, u32[]{:S(2)}) async-start(bf16[64,8,3584]{2,1,0:T(8,128)(2,1)} %bitcast.6), calls=%async_computation | async-start | bytes 7340032 | tf_op jit(solution)/shard_map/all_to_all | solution.py:215
  126.5 2.0 copy-start.5
  133.1 1.9 copy-start.2
  173.3 53.4 %all-to-all-start.1 = ((bf16[64,8,3584]{2,1,0:T(8,128)(2,1)}), bf16[64,8,3584]{2,1,0:T(8,128)(2,1)}, u32[]{:S(2)}, u32[]{:S(2)}) async-start(bf16[64,8,3584]{2,1,0:T(8,128)(2,1)} %bitcast.5), calls=%async_computation.1 | async-start | bytes 7340032 | tf_op jit(solution)/shard_map/all_to_all | solution.py:215
  180.8 7.8 %copy-start.8 = (bf16[1,128,576]{1,2,0:T(8,128)(2,1)S(1)}, bf16[1,128,576]{1,2,0:T(8,128)(2,1)}, u32[]{:S(2)}) copy-start(bf16[1,128,576]{1,2,0:T(8,128)(2,1)} %param.9) | copy-start | bytes 442372
  180.8 7.9 %copy-start.9 = (s32[128]{0:T(128)S(1)}, s32[128]{0:T(128)}, u32[]{:S(2)}) copy-start(s32[128]{0:T(128)} %param.11) | copy-start | bytes 1540
  189.3 2.5 %copy-start.1 = (bf16[4096,576]{1,0:T(8,128)(2,1)S(1)}, bf16[4096,576]{1,0:T(8,128)(2,1)}, u32[]{:S(2)}) copy-start(bf16[4096,576]{1,0:T(8,128)(2,1)} %copy.14.cache_ref) | copy-start | bytes 14155780
Sparse Core Ops, SparseCore 0:
  11.4 77.8 all-gather.1

commit v2 on v1

v2 whole, which is shorter than its diff:
```python
import jax
import jax.numpy as jnp
from jax import lax
from jax.experimental import pallas as pl
from jax.experimental.pallas import tpu as pltpu
from jax.sharding import Mesh, PartitionSpec as P

WIDTH = 7168
LATENT = 512
KEY_DIM = 576
HEADS = 128
EXPERTS = 32
CTX = 4096
UNITS = 256
TOK = 8
CHIPS = 64
ROWS = CHIPS * TOK
PAY = WIDTH + 128
QK_SCALE = 192.0 ** (-0.5)
FAR_LOW = -1e30
ATT_ROWS = 1024
HALF = WIDTH // 2
K_STEP = 512
N_TILE = 512
STEPS = HALF // K_STEP
PART = ROWS // 4
GROUP = ROWS // 16
BF = jnp.bfloat16
F32 = jnp.float32


def attend_kernel(length_ref, query_ref, cache_ref, out_ref, top_ref, sum_ref, mix_ref):
    step = pl.program_id(0)
    length = length_ref[0]

    @pl.when(step == 0)
    def _():
        top_ref[...] = jnp.full_like(top_ref, FAR_LOW)
        sum_ref[...] = jnp.zeros_like(sum_ref)
        mix_ref[...] = jnp.zeros_like(mix_ref)

    @pl.when(step * ATT_ROWS < length)
    def _():
        rows = cache_ref[...]
        scores = QK_SCALE * lax.dot_general(
            query_ref[0], rows, (((1,), (0,)), ((), ())), preferred_element_type=F32
        )
        place = step * ATT_ROWS + lax.broadcasted_iota(jnp.int32, scores.shape, 1)
        scores = jnp.where(place < length, scores, FAR_LOW)
        top_old = top_ref[...]
        top_new = jnp.maximum(top_old, jnp.max(scores, axis=1, keepdims=True))
        weights = jnp.exp(scores - top_new)
        scale = jnp.exp(top_old - top_new)
        top_ref[...] = top_new
        sum_ref[...] = sum_ref[...] * scale + jnp.sum(weights, axis=1, keepdims=True)
        mix_ref[...] = mix_ref[...] * scale + lax.dot_general(
            weights.astype(BF), rows[:LATENT], (((1,), (1,)), ((), ())), preferred_element_type=F32
        )

    @pl.when(step == pl.num_programs(0) - 1)
    def _():
        out_ref[0] = (mix_ref[...] / sum_ref[...]).astype(BF)


def attend(length, query_rows, cache_latent):
    def cache_block(step, length_ref):
        return 0, jnp.minimum(step, (length_ref[0] - 1) // ATT_ROWS)

    return pl.pallas_call(
        attend_kernel,
        grid_spec=pltpu.PrefetchScalarGridSpec(
            num_scalar_prefetch=1,
            grid=(CTX // ATT_ROWS,),
            in_specs=[
                pl.BlockSpec((1, HEADS, KEY_DIM), lambda step, length_ref: (0, 0, 0)),
                pl.BlockSpec((KEY_DIM, ATT_ROWS), cache_block),
            ],
            out_specs=pl.BlockSpec((1, HEADS, LATENT), lambda step, length_ref: (0, 0, 0)),
            scratch_shapes=[
                pltpu.VMEM((HEADS, 1), F32),
                pltpu.VMEM((HEADS, 1), F32),
                pltpu.VMEM((HEADS, LATENT), F32),
            ],
        ),
        out_shape=jax.ShapeDtypeStruct((1, HEADS, LATENT), BF),
        compiler_params=pltpu.CompilerParams(vmem_limit_bytes=24 * 2**20),
        cost_estimate=pl.CostEstimate(
            flops=2 * HEADS * CTX * (KEY_DIM + LATENT),
            bytes_accessed=CTX * KEY_DIM * 2,
            transcendentals=HEADS * CTX,
        ),
        name="attend",
    )(length, query_rows, cache_latent.T)


def dots(xs, weights):
    stacked = xs[0] if len(xs) == 1 else jnp.concatenate(xs, axis=0)
    return [jnp.dot(stacked, weight[...], preferred_element_type=F32) for weight in weights]


def early_kernel(*refs):
    a_refs, b_refs, weights_a, weights_b = refs[:3], refs[3:6], refs[6:10], refs[10:14]
    outs = refs[14:]
    step = pl.program_id(0)

    @pl.when(step == 0)
    def _():
        for out in outs:
            out[...] = jnp.zeros_like(out)

    for blocks, weights, out in ((a_refs, weights_a, outs[0]), (b_refs, weights_b, outs[1])):
        for place, made in enumerate(dots([block[...] for block in blocks], weights)):
            out[:, place * UNITS : (place + 1) * UNITS] += made


def late_kernel(*refs):
    a_ref, b_ref, weights_a, weights_b = refs[0], refs[1], refs[2:6], refs[6:10]
    tails, pick, early_a, early_b = refs[10:14], refs[14], refs[15], refs[16]
    out_a, out_b, last_a, last_b = refs[17:]
    step = pl.program_id(0)

    @pl.when(step == 0)
    def _():
        last_a[...] = jnp.zeros_like(last_a)
        last_b[...] = jnp.zeros_like(last_b)

    for block, weights, last in ((a_ref, weights_a, last_a), (b_ref, weights_b, last_b)):
        for place, made in enumerate(dots([block[...]], weights)):
            last[:, place * UNITS : (place + 1) * UNITS] += made

    @pl.when(step == pl.num_programs(0) - 1)
    def _():
        def group(early, last, outer, inner):
            low = inner * GROUP
            if outer == 3:
                return last[low : low + GROUP, :]
            return early[outer * PART + low : outer * PART + low + GROUP, :]

        for kx in range(4):
            share = jnp.dot(tails[kx][...], pick[...], preferred_element_type=F32)
            for kz in range(4):
                total = group(early_a, last_a, kz, kx) + group(early_b, last_b, kx, kz)
                gate, up = total[:, : 2 * UNITS], total[:, 2 * UNITS :]
                made = gate / (1.0 + jnp.exp(-gate)) * up * share[kz * GROUP : (kz + 1) * GROUP]
                made = made.astype(BF)
                low_a, low_b = (kz * 4 + kx) * GROUP, (kx * 4 + kz) * GROUP
                out_a[low_a : low_a + GROUP, :] = made
                out_b[low_b : low_b + GROUP, :] = made


def hidden_of(parts, pick, weights):
    a_blocks, b_blocks = parts
    block = pl.BlockSpec((PART, K_STEP), lambda step: (0, step))
    first = pl.BlockSpec((K_STEP, UNITS), lambda step: (step, 0))
    second = pl.BlockSpec((K_STEP, UNITS), lambda step: (step + STEPS, 0))
    tail = pl.BlockSpec((PART, 128), lambda step: (0, HALF // 128))

    def whole(rows, columns):
        return pl.BlockSpec((rows, columns), lambda step: (0, 0))

    def cost(blocks):
        return pl.CostEstimate(
            flops=2 * blocks * PART * WIDTH * 4 * UNITS,
            bytes_accessed=2 * (blocks * PART + 4 * UNITS) * WIDTH,
            transcendentals=0,
        )

    sums = jax.ShapeDtypeStruct((3 * PART, 4 * UNITS), F32)
    early_a, early_b = pl.pallas_call(
        early_kernel,
        grid=(STEPS,),
        in_specs=[block] * 6 + [first] * 4 + [second] * 4,
        out_specs=[whole(3 * PART, 4 * UNITS)] * 2,
        out_shape=[sums] * 2,
        compiler_params=pltpu.CompilerParams(vmem_limit_bytes=32 * 2**20),
        cost_estimate=cost(3),
        name="early",
    )(*a_blocks[:3], *b_blocks[:3], *weights, *weights)
    made = jax.ShapeDtypeStruct((ROWS, 2 * UNITS), BF)
    return pl.pallas_call(
        late_kernel,
        grid=(STEPS,),
        in_specs=[block] * 2
        + [first] * 4
        + [second] * 4
        + [tail] * 4
        + [whole(128, 2 * UNITS)]
        + [whole(3 * PART, 4 * UNITS)] * 2,
        out_specs=[whole(ROWS, 2 * UNITS)] * 2,
        out_shape=[made] * 2,
        scratch_shapes=[pltpu.VMEM((PART, 4 * UNITS), F32)] * 2,
        compiler_params=pltpu.CompilerParams(vmem_limit_bytes=32 * 2**20),
        cost_estimate=cost(1),
        name="late",
    )(a_blocks[3], b_blocks[3], *weights, *weights, *b_blocks, pick, early_a, early_b)


def down_kernel(h_a, h_b, d0_a, d1_a, d0_b, d1_b, out_a, out_b):
    for h, d0, d1, out in ((h_a, d0_a, d1_a, out_a), (h_b, d0_b, d1_b, out_b)):
        out[...] = (
            jnp.dot(h[:, :UNITS], d0[...], preferred_element_type=F32)
            + jnp.dot(h[:, UNITS:], d1[...], preferred_element_type=F32)
        ).astype(BF)


def down_of(hidden, downs, index):
    rows = pl.BlockSpec((PART, 2 * UNITS), lambda step: (index, 0))
    first = pl.BlockSpec((UNITS, N_TILE), lambda step: (0, step))
    second = pl.BlockSpec((UNITS, N_TILE), lambda step: (0, step + HALF // N_TILE))
    return pl.pallas_call(
        down_kernel,
        grid=(HALF // N_TILE,),
        in_specs=[rows, rows, first, first, second, second],
        out_specs=[pl.BlockSpec((PART, N_TILE), lambda step: (0, step))] * 2,
        out_shape=[jax.ShapeDtypeStruct((PART, HALF), BF)] * 2,
        compiler_params=pltpu.CompilerParams(vmem_limit_bytes=24 * 2**20),
        cost_estimate=pl.CostEstimate(
            flops=2 * PART * 2 * UNITS * WIDTH,
            bytes_accessed=2 * (PART + 2 * UNITS) * WIDTH,
            transcendentals=0,
        ),
        name="down",
    )(*hidden, *downs, *downs)


def swap(array):
    return lax.ppermute(array, "core", [(0, 1), (1, 0)])


def move(array, axis, way):
    names = ("core", axis) if axis == "y" else (axis, "core")

    def flat(core, place):
        return core * 4 + place if axis == "y" else place * 2 + core

    pairs = [
        (flat(core, place), flat(core, (place + (way if core == 0 else -way)) % 4))
        for core in range(2)
        for place in range(4)
    ]
    return lax.ppermute(array, names, pairs)


def gather_stage(parts, axes):
    first = [move(part, axis, 1) for part, axis in zip(parts, axes)]
    second = [move(part, axis, -1) for part, axis in zip(parts, axes)]
    third = [move(part, axis, 1) for part, axis in zip(first, axes)]
    return [list(blocks) for blocks in zip(parts, first, second, third)]


def joined(blocks):
    return jnp.concatenate(blocks, axis=0)


def added(*terms):
    total = terms[0].astype(F32)
    for term in terms[1:]:
        total = total + term.astype(F32)
    return total.astype(BF)


def reduce_stage(parts, axes):
    far = [move(blocks[3], axis, -1) for blocks, axis in zip(parts, axes)]
    near = [move(blocks[2], axis, 1) for blocks, axis in zip(parts, axes)]
    last = [
        move(added(blocks[1], relayed), axis, -1)
        for blocks, relayed, axis in zip(parts, far, axes)
    ]
    return [added(blocks[0], n, l) for blocks, n, l in zip(parts, near, last)]


def quarters(array):
    return jnp.split(array, 4, axis=0)


def payload_of(moe_input, expert_ids, gate_weights):
    chosen = expert_ids[:, :, None] == jnp.arange(EXPERTS, dtype=jnp.int32)
    shares = jnp.sum(jnp.where(chosen, gate_weights[:, :, None], 0.0), axis=1)
    high = lax.reduce_precision(shares, 8, 7)
    middle = lax.reduce_precision(shares - high, 8, 7)
    low = lax.reduce_precision(shares - high - middle, 8, 7)
    blank = jnp.zeros((TOK, 128 - 3 * EXPERTS), F32)
    tail = jnp.concatenate([high, middle, low, blank], axis=1).astype(BF)
    return jnp.concatenate([moe_input, tail], axis=1)


def per_device(
    query_rows,
    cache_latent,
    lengths,
    moe_input,
    expert_ids,
    gate_weights,
    expert_gate,
    expert_up,
    expert_down,
):
    chip = (lax.axis_index("z") * 4 + lax.axis_index("x")) * 2
    own = chip + lax.axis_index("core")
    other = chip + 1 - lax.axis_index("core")
    length = lax.dynamic_slice_in_dim(lengths, own * 4 + lax.axis_index("y"), 1)

    payload = payload_of(moe_input, expert_ids, gate_weights)
    column = joined(gather_stage([payload], ["y"])[0])
    plane = gather_stage([column[:, :HALF], column[:, HALF:]], ["x", "z"])
    parts = gather_stage([joined(blocks) for blocks in plane], ["z", "x"])

    gate_own, up_own, down_own = expert_gate[0], expert_up[0], expert_down[0]
    gate_other, up_other, down_other = swap(gate_own), swap(up_own), swap(down_own)
    attn_out = attend(length, query_rows, cache_latent)

    row = lax.broadcasted_iota(jnp.int32, (128, 2 * UNITS), 0)
    lane = lax.broadcasted_iota(jnp.int32, (128, 2 * UNITS), 1)
    wanted = jnp.where(lane < UNITS, own, other)
    pick = ((row % EXPERTS == wanted) & (row < 3 * EXPERTS)).astype(BF)

    hidden = hidden_of(parts, pick, (gate_own, gate_other, up_own, up_other))
    made = [None] * 4
    for index in (3, 2, 1, 0):
        made[index] = down_of(hidden, (down_own, down_other), index)
    sums = reduce_stage([[pair[0] for pair in made], [pair[1] for pair in made]], ["z", "x"])
    sums = reduce_stage([quarters(part) for part in sums], ["x", "z"])
    moe_out = reduce_stage([quarters(jnp.concatenate(sums, axis=1))], ["y"])[0]
    return attn_out, moe_out


def solution(mesh):
    fine = Mesh(mesh.devices.reshape(4, 4, 2, 4), ("z", "x", "core", "y"))
    dp = ("z", "x", "core")
    both = ("z", "x", "core", "y")
    return jax.shard_map(
        per_device,
        mesh=fine,
        in_specs=(
            P(both, None, None),
            P(both, None),
            P(),
            P(both, None),
            P(both, None),
            P(both, None),
            P(dp, None, "y"),
            P(dp, None, "y"),
            P(dp, "y", None),
        ),
        out_specs=(P(both, None, None), P(both, None)),
        check_vma=False,
    )
```

time: 238 us -> 192 us (0.81)
  waiting for transfers between devices: 144 us -> 78.7 us
  starting transfers between devices: 17 us -> 51 us
  Pallas kernels: 29.3 us -> 45.7 us
  local copies, waits for them, and re-layouts: 25.6 us -> 11.6 us
  between operations: 14.2 us -> 0.97 us
  other arithmetic: 6.72 us -> 3.24 us
    ppermute x0 -> x30, waiting for transfers between devices: none -> 78.7 us  [move(): return lax.ppermute(array, names, pairs)]
    all_gather x1 -> x0, waiting for transfers between devices: 67.6 us -> none  [per_device(): arrived = lax.all_gather(payload, CHIP_AXES, axis=0, tiled=True)]
    all_to_all x2 -> x0, waiting for transfers between devices: 65.1 us -> none  [per_device(): lax.all_to_all(made, CHIP_AXES, split_axis=0, concat_axis=0, tiled=True)]
    ppermute x0 -> x30, starting transfers between devices: none -> 50.5 us  [move(): return lax.ppermute(array, names, pairs)]
    all_to_all x2 -> x0, starting transfers between devices: 16.3 us -> none  [per_device(): lax.all_to_all(made, CHIP_AXES, split_axis=0, concat_axis=0, tiled=True)]
    pallas_call x3 -> x6, Pallas kernels: 23.7 us -> 39.9 us  [the longest x4 22.4 us: down_of(): pl.pallas_call(down_kernel, grid=(HALF // N_TILE,), in_specs=[rows, rows,...]
    unnamed x22 -> x23, local copies, waits for them, and re-layouts: 23.4 us -> 9.91 us
    ppermute x3, waiting for transfers between devices: 11.2 us -> 0.01 us  [swap(): return lax.ppermute(array, 'core', [(0, 1), (1, 0)])]
  transfers between devices with their start and end apart: 6 -> 33, of which waited for: 5 -> 14; matrix products, arithmetic and copies ran while one was open for 5% -> 1% of each run, Pallas kernels for 10% -> 21%
where the time goes in v2:
time: 192 us; the launch traced here: 191 us
  waiting for transfers between devices  78.7 us (41%)
  starting transfers between devices  51 us (27%)
  Pallas kernels  45.7 us (24%)
  local copies, waits for them, and re-layouts  11.6 us (6%)
  other arithmetic  3.24 us (2%)
    ppermute x30, waiting for transfers between devices, move(): return lax.ppermute(array, names, pairs)  78.7 us
    ppermute x30, starting transfers between devices, move(): return lax.ppermute(array, names, pairs)  50.5 us
    pallas_call x4, Pallas kernels, down_of(): pl.pallas_call(down_kernel, grid=(HALF // N_TILE,), in_specs=[rows, rows,...  22.4 us
    unnamed x23, local copies, waits for them, and re-layouts  9.91 us
    pallas_call x1, Pallas kernels, hidden_of(): pl.pallas_call(early_kernel, grid=(STEPS,), in_specs=[block] * 6 + [first...  9.67 us
    pallas_call x1, Pallas kernels, hidden_of(): pl.pallas_call(late_kernel, grid=(STEPS,), in_specs=[block] * 2 + [first]...  7.87 us
    pallas_call x1, Pallas kernels, attend(): pl.pallas_call(attend_kernel, grid_spec=pltpu.PrefetchScalarGridSpec(num_...  5.76 us
  transfers between devices with their start and end apart: 33, of which 14 were waited for; matrix products, arithmetic and copies ran while one was open for 1% of the time, Pallas kernels for 21%

profile of v2, /device:TPU:6, one launch (start us, length us, event | category | flops | bytes accessed | tf_op | source)
XLA Modules:
  0.0 191.2 jit_solution(2658556623732233485)
XLA Ops:
  10.3 4.2 %collective-permute-done.2 = bf16[8,7296]{1,0:T(8,128)(2,1)S(1)} collective-permute-done((bf16[8,7296]{1,0:T(8,128)(2,1)S(1)}, bf16[8,7296]{1,0:T(8,128)(2,1)S(1)}, u32[]{:S(2)}, u32[]{:S(2)}) %collective-permute-start.2) | collective-permute-done | bytes 116768 | tf_op jit(solution)/shard_map/ppermute | solution.py:241
  29.0 4.7 %collective-permute-done.9 = bf16[32,3712]{1,0:T(8,128)(2,1)S(1)} collective-permute-done((bf16[32,3712]{1,0:T(8,128)(2,1)S(1)}, bf16[32,3712]{1,0:T(8,128)(2,1)S(1)}, u32[]{:S(2)}, u32[]{:S(2)}) %collective-permute-start.9) | collective-permute-done | bytes 237600 | tf_op jit(solution)/shard_map/ppermute | solution.py:241
  33.7 3.7 %collective-permute-start.16 = (bf16[128,3584]{1,0:T(8,128)(2,1)S(1)}, bf16[128,3584]{1,0:T(8,128)(2,1)S(1)}, u32[]{:S(2)}, u32[]{:S(2)}) collective-permute-start(bf16[128,3584]{1,0:T(8,128)(2,1)S(1)} %pad_maximum_fusion.1.refs_0_), channel_id=1, source_target_pairs={{0,96},{32,0},{64,32},{96,64},{4,36},{36,68},{68,100},{100,4},{1,9... | collective-permute-start | bytes 2752520 | tf_op jit(solution)/shard_map/ppermute | solution.py:241
  37.5 19.8 %collective-permute-done.16.refs_2_ = bf16[128,3584]{1,0:T(8,128)(2,1)S(1)} collective-permute-done((bf16[128,3584]{1,0:T(8,128)(2,1)S(1)}, bf16[128,3584]{1,0:T(8,128)(2,1)S(1)}, u32[]{:S(2)}, u32[]{:S(2)}) %collective-permute-start.16) | collective-permute-done | bytes 917536 | tf_op jit(solution)/shard_map/ppermute | solution.py:241
  60.3 19.2 %collective-permute-done.11.refs_4_.refs_11_ = bf16[128,3712]{1,0:T(8,128)(2,1)S(1)} collective-permute-done((bf16[128,3712]{1,0:T(8,128)(2,1)S(1)}, bf16[128,3712]{1,0:T(8,128)(2,1)S(1)}, u32[]{:S(2)}, u32[]{:S(2)}) %collective-permute-start.11) | collective-permute-done | bytes 950304 | tf_op jit(solution)/shard_map/ppermute | solution.py:241
  88.4 9.7 %early.1 = (f32[384,1024]{1,0:T(8,128)S(1)}, f32[384,1024]{1,0:T(8,128)S(1)}) custom-call(bf16[128,3584]{1,0:T(8,128)(2,1)S(1)} %copy-done.6, bf16[128,3584]{1,0:T(8,128)(2,1)} %collective-permute-done.6.refs_1_, bf16[128,3584]{1,0:T(8,128)(2,1)S(1)} %copy-done.8, bf16[128,3712]{1,0:T(8,128)(2,1)S(1)} %pad_maximum_fusion.refs_3_.refs_10_, ...), custom_call_target="tpu_custom_call" | custom-call | flops 5637144576 | bytes 20185088 | tf_op jit(solution)/shard_map/early/pallas_call | solution.py:169
  98.2 7.9 %late.1 = (bf16[512,512]{1,0:T(8,128)(2,1)S(1)}, bf16[512,512]{1,0:T(8,128)(2,1)S(1)}) custom-call(bf16[128,3584]{1,0:T(8,128)(2,1)} %collective-permute-done.7.refs_0_, bf16[128,3712]{1,0:T(8,128)(2,1)} %collective-permute-done.12.refs_1_.refs_13_, bf16[7168,256]{1,0:T(8,128)(2,1)S(1)} %bitcast.16, ...), custom_call_target="tpu_custom_call" | custom-call | flops 1879048192 | bytes 16515072 | tf_op jit(solution)/shard_map/late/pallas_call | solution.py:180
  106.1 5.6 %down.7 = (bf16[128,3584]{1,0:T(8,128)(2,1)S(1)}, bf16[128,3584]{1,0:T(8,128)(2,1)S(1)}) custom-call(bf16[512,512]{1,0:T(8,128)(2,1)S(1)} %get-tuple-element.16.h_a, bf16[512,512]{1,0:T(8,128)(2,1)S(1)} %get-tuple-element.17.h_b, bf16[256,7168]{1,0:T(8,128)(2,1)S(1)} %bitcast.5, bf16[256,7168]{1,0:T(8,128)(2,1)} %collective-permute-done.17.d1_a.d1_b, ...), custom_call_target="tpu_custom_call" | custom-call | flops 939524096 | bytes 9175040 | tf_op jit(solution)/shard_map/down/pallas_call | solution.py:210
  111.8 5.6 %down.5 = (bf16[128,3584]{1,0:T(8,128)(2,1)S(1)}, bf16[128,3584]{1,0:T(8,128)(2,1)S(1)}) custom-call(bf16[512,512]{1,0:T(8,128)(2,1)S(1)} %get-tuple-element.16.h_a, bf16[512,512]{1,0:T(8,128)(2,1)S(1)} %get-tuple-element.17.h_b, bf16[256,7168]{1,0:T(8,128)(2,1)S(1)} %bitcast.7, bf16[256,7168]{1,0:T(8,128)(2,1)} %collective-permute-done.17.d1_a.d1_b, ...), custom_call_target="tpu_custom_call" | custom-call | flops 939524096 | bytes 9175040 | tf_op jit(solution)/shard_map/down/pallas_call | solution.py:210
  117.4 3.3 %collective-permute-start.24 = (bf16[128,3584]{1,0:T(8,128)(2,1)S(1)}, bf16[128,3584]{1,0:T(8,128)(2,1)S(1)}, u32[]{:S(2)}, u32[]{:S(2)}) collective-permute-start(bf16[128,3584]{1,0:T(8,128)(2,1)S(1)} %get-tuple-element.23), channel_id=1, source_target_pairs={{0,8},{8,16},{16,24},{24,0},{4,28},{12,4},{20,12},{28,20},{1,9},{9... | collective-permute-start | bytes 2752520 | tf_op jit(solution)/shard_map/ppermute | solution.py:241
  123.9 5.6 %down.6 = (bf16[128,3584]{1,0:T(8,128)(2,1)S(1)}, bf16[128,3584]{1,0:T(8,128)(2,1)S(1)}) custom-call(bf16[512,512]{1,0:T(8,128)(2,1)S(1)} %get-tuple-element.16.h_a, bf16[512,512]{1,0:T(8,128)(2,1)S(1)} %get-tuple-element.17.h_b, bf16[256,7168]{1,0:T(8,128)(2,1)S(1)} %bitcast.9, bf16[256,7168]{1,0:T(8,128)(2,1)} %collective-permute-done.17.d1_a.d1_b, ...), custom_call_target="tpu_custom_call" | custom-call | flops 939524096 | bytes 9175040 | tf_op jit(solution)/shard_map/down/pallas_call | solution.py:210
  129.5 5.6 %down.4 = (bf16[128,3584]{1,0:T(8,128)(2,1)S(1)}, bf16[128,3584]{1,0:T(8,128)(2,1)S(1)}) custom-call(bf16[512,512]{1,0:T(8,128)(2,1)S(1)} %get-tuple-element.16.h_a, bf16[512,512]{1,0:T(8,128)(2,1)S(1)} %get-tuple-element.17.h_b, bf16[256,7168]{1,0:T(8,128)(2,1)S(1)} %bitcast.11, bf16[256,7168]{1,0:T(8,128)(2,1)} %collective-permute-done.17.d1_a.d1_b, ...), custom_call_target="tpu_custom_call" | custom-call | flops 939524096 | bytes 9175040 | tf_op jit(solution)/shard_map/down/pallas_call | solution.py:210
  135.4 3.3 %collective-permute-done.19 = bf16[128,3584]{1,0:T(8,128)(2,1)S(1)} collective-permute-done((bf16[128,3584]{1,0:T(8,128)(2,1)S(1)}, bf16[128,3584]{1,0:T(8,128)(2,1)S(1)}, u32[]{:S(2)}, u32[]{:S(2)}) %collective-permute-start.19) | collective-permute-done | bytes 917536 | tf_op jit(solution)/shard_map/ppermute | solution.py:241
  138.9 3.8 %collective-permute-start.20 = (bf16[128,3584]{1,0:T(8,128)(2,1)S(1)}, bf16[128,3584]{1,0:T(8,128)(2,1)S(1)}, u32[]{:S(2)}, u32[]{:S(2)}) collective-permute-start(bf16[128,3584]{1,0:T(8,128)(2,1)S(1)} %add_convert_fusion.3), channel_id=1, source_target_pairs={{0,96},{32,0},{64,32},{96,64},{4,36},{36,68},{68,100},{100,4},{1,9... | collective-permute-start | bytes 2752520 | tf_op jit(solution)/shard_map/ppermute | solution.py:241
  142.7 7.3 %collective-permute-done.26 = bf16[128,3584]{1,0:T(8,128)(2,1)S(1)} collective-permute-done((bf16[128,3584]{1,0:T(8,128)(2,1)S(1)}, bf16[128,3584]{1,0:T(8,128)(2,1)S(1)}, u32[]{:S(2)}, u32[]{:S(2)}) %collective-permute-start.26) | collective-permute-done | bytes 917536 | tf_op jit(solution)/shard_map/ppermute | solution.py:241
  152.4 3.6 %collective-permute-done.20 = bf16[128,3584]{1,0:T(8,128)(2,1)S(1)} collective-permute-done((bf16[128,3584]{1,0:T(8,128)(2,1)S(1)}, bf16[128,3584]{1,0:T(8,128)(2,1)S(1)}, u32[]{:S(2)}, u32[]{:S(2)}) %collective-permute-start.20) | collective-permute-done | bytes 917536 | tf_op jit(solution)/shard_map/ppermute | solution.py:241
  156.5 3.2 %collective-permute-start.21 = (bf16[32,3584]{1,0:T(8,128)(2,1)S(1)}, bf16[32,3584]{1,0:T(8,128)(2,1)S(1)}, u32[]{:S(2)}, u32[]{:S(2)}) collective-permute-start(bf16[32,3584]{1,0:T(8,128)(2,1)S(1)} %get-tuple-element.26), channel_id=1, source_target_pairs={{0,8},{8,16},{16,24},{24,0},{4,28},{12,4},{20,12},{28,20},{1,9},{9... | collective-permute-start | bytes 688136 | tf_op jit(solution)/shard_map/ppermute | solution.py:241
  159.8 3.8 %collective-permute-start.29 = (bf16[32,3584]{1,0:T(8,128)(2,1)S(1)}, bf16[32,3584]{1,0:T(8,128)(2,1)S(1)}, u32[]{:S(2)}, u32[]{:S(2)}) collective-permute-start(bf16[32,3584]{1,0:T(8,128)(2,1)S(1)} %add_convert_fusion.5), channel_id=1, source_target_pairs={{0,96},{32,0},{64,32},{96,64},{4,36},{36,68},{68,100},{100,4},{1,9... | collective-permute-start | bytes 688136 | tf_op jit(solution)/shard_map/ppermute | solution.py:241
  163.9 3.2 %collective-permute-done.29 = bf16[32,3584]{1,0:T(8,128)(2,1)S(1)} collective-permute-done((bf16[32,3584]{1,0:T(8,128)(2,1)S(1)}, bf16[32,3584]{1,0:T(8,128)(2,1)S(1)}, u32[]{:S(2)}, u32[]{:S(2)}) %collective-permute-start.29) | collective-permute-done | bytes 229408 | tf_op jit(solution)/shard_map/ppermute | solution.py:241
  167.2 3.9 %collective-permute-done.23 = bf16[32,3584]{1,0:T(8,128)(2,1)S(1)} collective-permute-done((bf16[32,3584]{1,0:T(8,128)(2,1)S(1)}, bf16[32,3584]{1,0:T(8,128)(2,1)S(1)}, u32[]{:S(2)}, u32[]{:S(2)}) %collective-permute-start.23) | collective-permute-done | bytes 229408 | tf_op jit(solution)/shard_map/ppermute | solution.py:241
  171.2 3.5 %collective-permute-start.31 = (bf16[8,7168]{1,0:T(8,128)(2,1)S(1)}, bf16[8,7168]{1,0:T(8,128)(2,1)S(1)}, u32[]{:S(2)}, u32[]{:S(2)}) collective-permute-start(bf16[8,7168]{1,0:T(8,128)(2,1)S(1)} %get-tuple-element.31), channel_id=1, source_target_pairs={{0,3},{1,0},{2,1},{3,2},{4,5},{5,6},{6,7},{7,4},{8,11},{9,8},{10,9... | collective-permute-start | bytes 344072 | tf_op jit(solution)/shard_map/ppermute | solution.py:241
  174.7 3.1 %collective-permute-done.31 = bf16[8,7168]{1,0:T(8,128)(2,1)S(1)} collective-permute-done((bf16[8,7168]{1,0:T(8,128)(2,1)S(1)}, bf16[8,7168]{1,0:T(8,128)(2,1)S(1)}, u32[]{:S(2)}, u32[]{:S(2)}) %collective-permute-start.31) | collective-permute-done | bytes 114720 | tf_op jit(solution)/shard_map/ppermute | solution.py:241
  177.8 3.8 %collective-permute-start.32 = (bf16[8,7168]{1,0:T(8,128)(2,1)S(1)}, bf16[8,7168]{1,0:T(8,128)(2,1)S(1)}, u32[]{:S(2)}, u32[]{:S(2)}) collective-permute-start(bf16[8,7168]{1,0:T(8,128)(2,1)S(1)} %add_convert_fusion.9), channel_id=1, source_target_pairs={{0,3},{1,0},{2,1},{3,2},{4,5},{5,6},{6,7},{7,4},{8,11},{9,8},{10,9... | collective-permute-start | bytes 344072 | tf_op jit(solution)/shard_map/ppermute | solution.py:241
  184.7 5.8 %attend.1 = bf16[1,128,512]{2,1,0:T(8,128)(2,1)} custom-call(s32[1]{0:T(128)} %dynamic_slice.3.length_ref, bf16[1,128,576]{2,1,0:T(8,128)(2,1)S(1)} %copy.12.query_ref, bf16[576,4096]{1,0:T(8,128)(2,1)S(1)} %bitcast.23), custom_call_target="tpu_custom_call" | custom-call | flops 1140850688 | bytes 4718592 | tf_op jit(solution)/shard_map/attend/pallas_call | solution.py:69
  (98 shorter events, 47.2 us)
Async XLA Ops:
  9.8 72.2 %collective-permute-start.13 = (bf16[7168,256]{1,0:T(8,128)(2,1)}, bf16[7168,256]{1,0:T(8,128)(2,1)}, u32[]{:S(2)}, u32[]{:S(2)}) collective-permute-start(bf16[7168,256]{1,0:T(8,128)(2,1)} %bitcast.13), channel_id=1, source_target_pairs={{0,4},{4,0},{1,5},{5,1},{2,6},{6,2},{3,7},{7,3},{8,12},{12,8},{9,1... | collective-permute-start | bytes 11010056 | tf_op jit(solution)/shard_map/ppermute | solution.py:227
  9.9 72.1 %collective-permute-start.14 = (bf16[7168,256]{1,0:T(8,128)(2,1)}, bf16[7168,256]{1,0:T(8,128)(2,1)}, u32[]{:S(2)}, u32[]{:S(2)}) collective-permute-start(bf16[7168,256]{1,0:T(8,128)(2,1)} %bitcast.18), channel_id=1, source_target_pairs={{0,4},{4,0},{1,5},{5,1},{2,6},{6,2},{3,7},{7,3},{8,12},{12,8},{9,1... | collective-permute-start | bytes 11010056 | tf_op jit(solution)/shard_map/ppermute | solution.py:227
  15.0 8.5 %collective-permute-start.4 = (bf16[32,3584]{1,0:T(8,128)(2,1)S(1)}, bf16[32,3584]{1,0:T(8,128)(2,1)S(1)}, u32[]{:S(2)}, u32[]{:S(2)}) collective-permute-start(bf16[32,3584]{1,0:T(8,128)(2,1)S(1)} %pad_maximum_fusion.5), channel_id=1, source_target_pairs={{0,24},{8,0},{16,8},{24,16},{4,12},{12,20},{20,28},{28,4},{1,25},{... | collective-permute-start | bytes 688136 | tf_op jit(solution)/shard_map/ppermute | solution.py:241
  16.6 8.2 %collective-permute-start.8 = (bf16[32,3712]{1,0:T(8,128)(2,1)S(1)}, bf16[32,3712]{1,0:T(8,128)(2,1)S(1)}, u32[]{:S(2)}, u32[]{:S(2)}) collective-permute-start(bf16[32,3712]{1,0:T(8,128)(2,1)S(1)} %pad_maximum_fusion.2), channel_id=1, source_target_pairs={{0,32},{32,64},{64,96},{96,0},{4,100},{36,4},{68,36},{100,68},{1,3... | collective-permute-start | bytes 712712 | tf_op jit(solution)/shard_map/ppermute | solution.py:241
  23.5 82.6 %collective-permute-start.17 = (bf16[256,7168]{1,0:T(8,128)(2,1)}, bf16[256,7168]{1,0:T(8,128)(2,1)}, u32[]{:S(2)}, u32[]{:S(2)}) collective-permute-start(bf16[256,7168]{1,0:T(8,128)(2,1)} %bitcast.4), channel_id=1, source_target_pairs={{0,4},{4,0},{1,5},{5,1},{2,6},{6,2},{3,7},{7,3},{8,12},{12,8},{9,1... | collective-permute-start | bytes 11010056 | tf_op jit(solution)/shard_map/ppermute | solution.py:227
  24.8 8.9 %collective-permute-start.9 = (bf16[32,3712]{1,0:T(8,128)(2,1)S(1)}, bf16[32,3712]{1,0:T(8,128)(2,1)S(1)}, u32[]{:S(2)}, u32[]{:S(2)}) collective-permute-start(bf16[32,3712]{1,0:T(8,128)(2,1)S(1)} %pad_maximum_fusion.2), channel_id=1, source_target_pairs={{0,96},{32,0},{64,32},{96,64},{4,36},{36,68},{68,100},{100,4},{1,9... | collective-permute-start | bytes 712712 | tf_op jit(solution)/shard_map/ppermute | solution.py:241
  27.6 9.8 %collective-permute-start.10 = (bf16[32,3712]{1,0:T(8,128)(2,1)S(1)}, bf16[32,3712]{1,0:T(8,128)(2,1)S(1)}, u32[]{:S(2)}, u32[]{:S(2)}) collective-permute-start(bf16[32,3712]{1,0:T(8,128)(2,1)S(1)} %collective-permute-done.8), channel_id=1, source_target_pairs={{0,32},{32,64},{64,96},{96,0},{4,100},{36,4},{68,36},{100,68},{1,3... | collective-permute-start | bytes 712712 | tf_op jit(solution)/shard_map/ppermute | solution.py:241
  33.7 23.6 %collective-permute-start.16 = (bf16[128,3584]{1,0:T(8,128)(2,1)S(1)}, bf16[128,3584]{1,0:T(8,128)(2,1)S(1)}, u32[]{:S(2)}, u32[]{:S(2)}) collective-permute-start(bf16[128,3584]{1,0:T(8,128)(2,1)S(1)} %pad_maximum_fusion.1.refs_0_), channel_id=1, source_target_pairs={{0,96},{32,0},{64,32},{96,64},{4,36},{36,68},{68,100},{100,4},{1,9... | collective-permute-start | bytes 2752520 | tf_op jit(solution)/shard_map/ppermute | solution.py:241
  37.4 21.5 %collective-permute-start.6 = (bf16[128,3584]{1,0:T(8,128)(2,1)S(1)}, bf16[128,3584]{1,0:T(8,128)(2,1)}, u32[]{:S(2)}, u32[]{:S(2)}) collective-permute-start(bf16[128,3584]{1,0:T(8,128)(2,1)S(1)} %pad_maximum_fusion.1.refs_0_), channel_id=1, source_target_pairs={{0,32},{32,64},{64,96},{96,0},{4,100},{36,4},{68,36},{100,68},{1,3... | collective-permute-start | bytes 2752520 | tf_op jit(solution)/shard_map/ppermute | solution.py:241
  58.2 21.3 %collective-permute-start.11 = (bf16[128,3712]{1,0:T(8,128)(2,1)S(1)}, bf16[128,3712]{1,0:T(8,128)(2,1)S(1)}, u32[]{:S(2)}, u32[]{:S(2)}) collective-permute-start(bf16[128,3712]{1,0:T(8,128)(2,1)S(1)} %pad_maximum_fusion.refs_3_.refs_10_), channel_id=1, source_target_pairs={{0,8},{8,16},{16,24},{24,0},{4,28},{12,4},{20,12},{28,20},{1,9},{9... | collective-permute-start | bytes 2850824 | tf_op jit(solution)/shard_map/ppermute | solution.py:241
  58.9 20.6 %collective-permute-start.15 = (bf16[128,3712]{1,0:T(8,128)(2,1)S(1)}, bf16[128,3712]{1,0:T(8,128)(2,1)S(1)}, u32[]{:S(2)}, u32[]{:S(2)}) collective-permute-start(bf16[128,3712]{1,0:T(8,128)(2,1)S(1)} %pad_maximum_fusion.refs_3_.refs_10_), channel_id=1, source_target_pairs={{0,24},{8,0},{16,8},{24,16},{4,12},{12,20},{20,28},{28,4},{1,25},{... | collective-permute-start | bytes 2850824 | tf_op jit(solution)/shard_map/ppermute | solution.py:241
  79.5 18.6 %collective-permute-start.7 = (bf16[128,3584]{1,0:T(8,128)(2,1)}, bf16[128,3584]{1,0:T(8,128)(2,1)}, u32[]{:S(2)}, u32[]{:S(2)}) collective-permute-start(bf16[128,3584]{1,0:T(8,128)(2,1)} %collective-permute-done.6.refs_1_), channel_id=1, source_target_pairs={{0,32},{32,64},{64,96},{96,0},{4,100},{36,4},{68,36},{100,68},{1,3... | collective-permute-start | bytes 2752520 | tf_op jit(solution)/shard_map/ppermute | solution.py:241
  79.5 18.6 %collective-permute-start.12 = (bf16[128,3712]{1,0:T(8,128)(2,1)S(1)}, bf16[128,3712]{1,0:T(8,128)(2,1)}, u32[]{:S(2)}, u32[]{:S(2)}) collective-permute-start(bf16[128,3712]{1,0:T(8,128)(2,1)S(1)} %collective-permute-done.11.refs_4_.refs_11_), channel_id=1, source_target_pairs={{0,8},{8,16},{16,24},{24,0},{4,28},{12,4},{20,12},{28,20},{1,9},{9... | collective-permute-start | bytes 2850824 | tf_op jit(solution)/shard_map/ppermute | solution.py:241
  111.7 23.4 %collective-permute-start.25 = (bf16[128,3584]{1,0:T(8,128)(2,1)S(1)}, bf16[128,3584]{1,0:T(8,128)(2,1)S(1)}, u32[]{:S(2)}, u32[]{:S(2)}) collective-permute-start(bf16[128,3584]{1,0:T(8,128)(2,1)S(1)} %get-tuple-element.25), channel_id=1, source_target_pairs={{0,24},{8,0},{16,8},{24,16},{4,12},{12,20},{20,28},{28,4},{1,25},{... | collective-permute-start | bytes 2752520 | tf_op jit(solution)/shard_map/ppermute | solution.py:241
  117.4 25.3 %collective-permute-start.24 = (bf16[128,3584]{1,0:T(8,128)(2,1)S(1)}, bf16[128,3584]{1,0:T(8,128)(2,1)S(1)}, u32[]{:S(2)}, u32[]{:S(2)}) collective-permute-start(bf16[128,3584]{1,0:T(8,128)(2,1)S(1)} %get-tuple-element.23), channel_id=1, source_target_pairs={{0,8},{8,16},{16,24},{24,0},{4,28},{12,4},{20,12},{28,20},{1,9},{9... | collective-permute-start | bytes 2752520 | tf_op jit(solution)/shard_map/ppermute | solution.py:241
  120.6 31.8 %collective-permute-start.18 = (bf16[128,3584]{1,0:T(8,128)(2,1)S(1)}, bf16[128,3584]{1,0:T(8,128)(2,1)S(1)}, u32[]{:S(2)}, u32[]{:S(2)}) collective-permute-start(bf16[128,3584]{1,0:T(8,128)(2,1)S(1)} %get-tuple-element.19), channel_id=1, source_target_pairs={{0,32},{32,64},{64,96},{96,0},{4,100},{36,4},{68,36},{100,68},{1,3... | collective-permute-start | bytes 2752520 | tf_op jit(solution)/shard_map/ppermute | solution.py:241
  122.5 16.3 %collective-permute-start.19 = (bf16[128,3584]{1,0:T(8,128)(2,1)S(1)}, bf16[128,3584]{1,0:T(8,128)(2,1)S(1)}, u32[]{:S(2)}, u32[]{:S(2)}) collective-permute-start(bf16[128,3584]{1,0:T(8,128)(2,1)S(1)} %get-tuple-element.21), channel_id=1, source_target_pairs={{0,96},{32,0},{64,32},{96,64},{4,36},{36,68},{68,100},{100,4},{1,9... | collective-permute-start | bytes 2752520 | tf_op jit(solution)/shard_map/ppermute | solution.py:241
  135.3 14.7 %collective-permute-start.26 = (bf16[128,3584]{1,0:T(8,128)(2,1)S(1)}, bf16[128,3584]{1,0:T(8,128)(2,1)S(1)}, u32[]{:S(2)}, u32[]{:S(2)}) collective-permute-start(bf16[128,3584]{1,0:T(8,128)(2,1)S(1)} %add_convert_fusion.1), channel_id=1, source_target_pairs={{0,24},{8,0},{16,8},{24,16},{4,12},{12,20},{20,28},{28,4},{1,25},{... | collective-permute-start | bytes 2752520 | tf_op jit(solution)/shard_map/ppermute | solution.py:241
  138.9 17.1 %collective-permute-start.20 = (bf16[128,3584]{1,0:T(8,128)(2,1)S(1)}, bf16[128,3584]{1,0:T(8,128)(2,1)S(1)}, u32[]{:S(2)}, u32[]{:S(2)}) collective-permute-start(bf16[128,3584]{1,0:T(8,128)(2,1)S(1)} %add_convert_fusion.3), channel_id=1, source_target_pairs={{0,96},{32,0},{64,32},{96,64},{4,36},{36,68},{68,100},{100,4},{1,9... | collective-permute-start | bytes 2752520 | tf_op jit(solution)/shard_map/ppermute | solution.py:241
  150.3 9.4 %collective-permute-start.28 = (bf16[32,3584]{1,0:T(8,128)(2,1)S(1)}, bf16[32,3584]{1,0:T(8,128)(2,1)S(1)}, u32[]{:S(2)}, u32[]{:S(2)}) collective-permute-start(bf16[32,3584]{1,0:T(8,128)(2,1)S(1)} %get-tuple-element.29), channel_id=1, source_target_pairs={{0,96},{32,0},{64,32},{96,64},{4,36},{36,68},{68,100},{100,4},{1,9... | collective-permute-start | bytes 688136 | tf_op jit(solution)/shard_map/ppermute | solution.py:241
  152.2 11.7 %collective-permute-start.27 = (bf16[32,3584]{1,0:T(8,128)(2,1)S(1)}, bf16[32,3584]{1,0:T(8,128)(2,1)S(1)}, u32[]{:S(2)}, u32[]{:S(2)}) collective-permute-start(bf16[32,3584]{1,0:T(8,128)(2,1)S(1)} %get-tuple-element.28), channel_id=1, source_target_pairs={{0,32},{32,64},{64,96},{96,0},{4,100},{36,4},{68,36},{100,68},{1,3... | collective-permute-start | bytes 688136 | tf_op jit(solution)/shard_map/ppermute | solution.py:241
  156.5 10.7 %collective-permute-start.21 = (bf16[32,3584]{1,0:T(8,128)(2,1)S(1)}, bf16[32,3584]{1,0:T(8,128)(2,1)S(1)}, u32[]{:S(2)}, u32[]{:S(2)}) collective-permute-start(bf16[32,3584]{1,0:T(8,128)(2,1)S(1)} %get-tuple-element.26), channel_id=1, source_target_pairs={{0,8},{8,16},{16,24},{24,0},{4,28},{12,4},{20,12},{28,20},{1,9},{9... | collective-permute-start | bytes 688136 | tf_op jit(solution)/shard_map/ppermute | solution.py:241
  174.7 15.7 %collective-permute-start.30 = (bf16[8,7168]{1,0:T(8,128)(2,1)S(1)}, bf16[8,7168]{1,0:T(8,128)(2,1)S(1)}, u32[]{:S(2)}, u32[]{:S(2)}) collective-permute-start(bf16[8,7168]{1,0:T(8,128)(2,1)S(1)} %get-tuple-element.30), channel_id=1, source_target_pairs={{0,1},{1,2},{2,3},{3,0},{4,7},{5,4},{6,5},{7,6},{8,9},{9,10},{10,1... | collective-permute-start | bytes 344072 | tf_op jit(solution)/shard_map/ppermute | solution.py:241
  177.8 12.6 %collective-permute-start.32 = (bf16[8,7168]{1,0:T(8,128)(2,1)S(1)}, bf16[8,7168]{1,0:T(8,128)(2,1)S(1)}, u32[]{:S(2)}, u32[]{:S(2)}) collective-permute-start(bf16[8,7168]{1,0:T(8,128)(2,1)S(1)} %add_convert_fusion.9), channel_id=1, source_target_pairs={{0,3},{1,0},{2,1},{3,2},{4,5},{5,6},{6,7},{7,4},{8,11},{9,8},{10,9... | collective-permute-start | bytes 344072 | tf_op jit(solution)/shard_map/ppermute | solution.py:241
  (20 other events, 177.5 us)

commit v3 on v2

--- a/solution.py
+++ b/solution.py
@@ -21,7 +21,8 @@
 ATT_ROWS = 1024
 HALF = WIDTH // 2
 K_STEP = 512
-N_TILE = 512
+N_TILE = 896
+VMEM_LIMIT = 48 * 2**20
 STEPS = HALF // K_STEP
 PART = ROWS // 4
 GROUP = ROWS // 16
@@ -115,12 +116,18 @@
 
 def late_kernel(*refs):
     a_ref, b_ref, weights_a, weights_b = refs[0], refs[1], refs[2:6], refs[6:10]
-    tails, pick, early_a, early_b = refs[10:14], refs[14], refs[15], refs[16]
-    out_a, out_b, last_a, last_b = refs[17:]
+    tails, pick, sources = refs[10:14], refs[14], refs[15:17]
+    out_a, out_b, last_a, last_b, early_a, early_b, arrival = refs[17:]
     step = pl.program_id(0)
+    fetches = [
+        pltpu.make_async_copy(source, kept, arrival.at[place])
+        for place, (source, kept) in enumerate(zip(sources, (early_a, early_b)))
+    ]
 
     @pl.when(step == 0)
     def _():
+        for fetch in fetches:
+            fetch.start()
         last_a[...] = jnp.zeros_like(last_a)
         last_b[...] = jnp.zeros_like(last_b)
 
@@ -130,6 +137,9 @@
 
     @pl.when(step == pl.num_programs(0) - 1)
     def _():
+        for fetch in fetches:
+            fetch.wait()
+
         def group(early, last, outer, inner):
             low = inner * GROUP
             if outer == 3:
@@ -172,7 +182,7 @@
         in_specs=[block] * 6 + [first] * 4 + [second] * 4,
         out_specs=[whole(3 * PART, 4 * UNITS)] * 2,
         out_shape=[sums] * 2,
-        compiler_params=pltpu.CompilerParams(vmem_limit_bytes=32 * 2**20),
+        compiler_params=pltpu.CompilerParams(vmem_limit_bytes=VMEM_LIMIT),
         cost_estimate=cost(3),
         name="early",
     )(*a_blocks[:3], *b_blocks[:3], *weights, *weights)
@@ -185,42 +195,44 @@
         + [second] * 4
         + [tail] * 4
         + [whole(128, 2 * UNITS)]
-        + [whole(3 * PART, 4 * UNITS)] * 2,
+        + [pl.BlockSpec(memory_space=pl.ANY)] * 2,
         out_specs=[whole(ROWS, 2 * UNITS)] * 2,
         out_shape=[made] * 2,
-        scratch_shapes=[pltpu.VMEM((PART, 4 * UNITS), F32)] * 2,
-        compiler_params=pltpu.CompilerParams(vmem_limit_bytes=32 * 2**20),
+        scratch_shapes=[pltpu.VMEM((PART, 4 * UNITS), F32)] * 2
+        + [pltpu.VMEM((3 * PART, 4 * UNITS), F32)] * 2
+        + [pltpu.SemaphoreType.DMA((2,))],
+        compiler_params=pltpu.CompilerParams(vmem_limit_bytes=VMEM_LIMIT),
         cost_estimate=cost(1),
         name="late",
     )(a_blocks[3], b_blocks[3], *weights, *weights, *b_blocks, pick, early_a, early_b)
 
 
-def down_kernel(h_a, h_b, d0_a, d1_a, d0_b, d1_b, out_a, out_b):
-    for h, d0, d1, out in ((h_a, d0_a, d1_a, out_a), (h_b, d0_b, d1_b, out_b)):
-        out[...] = (
-            jnp.dot(h[:, :UNITS], d0[...], preferred_element_type=F32)
-            + jnp.dot(h[:, UNITS:], d1[...], preferred_element_type=F32)
-        ).astype(BF)
-
-
-def down_of(hidden, downs, index):
-    rows = pl.BlockSpec((PART, 2 * UNITS), lambda step: (index, 0))
-    first = pl.BlockSpec((UNITS, N_TILE), lambda step: (0, step))
-    second = pl.BlockSpec((UNITS, N_TILE), lambda step: (0, step + HALF // N_TILE))
+def down_kernel(h, d0, d1, *outs):
+    made = (
+        jnp.dot(h[:, :UNITS], d0[...], preferred_element_type=F32)
+        + jnp.dot(h[:, UNITS:], d1[...], preferred_element_type=F32)
+    ).astype(BF)
+    for place, out in enumerate(outs):
+        out[...] = made[place * PART : (place + 1) * PART]
+
+
+def down_of(hidden, downs, half):
+    first = half * (HALF // N_TILE)
+    weight = pl.BlockSpec((UNITS, N_TILE), lambda step: (0, step + first))
     return pl.pallas_call(
         down_kernel,
         grid=(HALF // N_TILE,),
-        in_specs=[rows, rows, first, first, second, second],
-        out_specs=[pl.BlockSpec((PART, N_TILE), lambda step: (0, step))] * 2,
-        out_shape=[jax.ShapeDtypeStruct((PART, HALF), BF)] * 2,
+        in_specs=[pl.BlockSpec((ROWS, 2 * UNITS), lambda step: (0, 0)), weight, weight],
+        out_specs=[pl.BlockSpec((PART, N_TILE), lambda step: (0, step))] * 4,
+        out_shape=[jax.ShapeDtypeStruct((PART, HALF), BF)] * 4,
         compiler_params=pltpu.CompilerParams(vmem_limit_bytes=24 * 2**20),
         cost_estimate=pl.CostEstimate(
-            flops=2 * PART * 2 * UNITS * WIDTH,
-            bytes_accessed=2 * (PART + 2 * UNITS) * WIDTH,
+            flops=2 * ROWS * 2 * UNITS * HALF,
+            bytes_accessed=2 * (ROWS + 2 * UNITS) * HALF,
             transcendentals=0,
         ),
         name="down",
-    )(*hidden, *downs, *downs)
+    )(hidden, *downs)
 
 
 def swap(array):
@@ -242,10 +254,10 @@
 
 
 def gather_stage(parts, axes):
-    first = [move(part, axis, 1) for part, axis in zip(parts, axes)]
-    second = [move(part, axis, -1) for part, axis in zip(parts, axes)]
-    third = [move(part, axis, 1) for part, axis in zip(first, axes)]
-    return [list(blocks) for blocks in zip(parts, first, second, third)]
+    return [
+        [part, move(part, axis, 1), move(part, axis, -1), move(part, axis, 2)]
+        for part, axis in zip(parts, axes)
+    ]
 
 
 def joined(blocks):
@@ -259,7 +271,14 @@
     return total.astype(BF)
 
 
-def reduce_stage(parts, axes):
+def reduce_stage(parts, axes, relay):
+    if not relay:
+        far = [move(blocks[3], axis, 2) for blocks, axis in zip(parts, axes)]
+        near = [move(blocks[2], axis, 1) for blocks, axis in zip(parts, axes)]
+        last = [move(blocks[1], axis, -1) for blocks, axis in zip(parts, axes)]
+        return [
+            added(blocks[0], n, l, f) for blocks, n, l, f in zip(parts, near, last, far)
+        ]
     far = [move(blocks[3], axis, -1) for blocks, axis in zip(parts, axes)]
     near = [move(blocks[2], axis, 1) for blocks, axis in zip(parts, axes)]
     last = [
@@ -301,13 +320,21 @@
     length = lax.dynamic_slice_in_dim(lengths, own * 4 + lax.axis_index("y"), 1)
 
     payload = payload_of(moe_input, expert_ids, gate_weights)
+    gate_own, up_own, down_own = expert_gate[0], expert_up[0], expert_down[0]
     column = joined(gather_stage([payload], ["y"])[0])
+    column, gate_other, up_other = lax.optimization_barrier(
+        (column, swap(gate_own), swap(up_own))
+    )
     plane = gather_stage([column[:, :HALF], column[:, HALF:]], ["x", "z"])
-    parts = gather_stage([joined(blocks) for blocks in plane], ["z", "x"])
-
-    gate_own, up_own, down_own = expert_gate[0], expert_up[0], expert_down[0]
-    gate_other, up_other, down_other = swap(gate_own), swap(up_own), swap(down_own)
+    both = [joined(blocks) for blocks in plane]
+    both, query_rows, down_own = lax.optimization_barrier((both, query_rows, down_own))
+    down_other = swap(down_own)
+    first = [move(part, axis, 1) for part, axis in zip(both, "zx")]
+    second = [move(part, axis, -1) for part, axis in zip(both, "zx")]
     attn_out = attend(length, query_rows, cache_latent)
+    first, attn_out = lax.optimization_barrier((first, attn_out))
+    third = [move(part, axis, 1) for part, axis in zip(first, "zx")]
+    parts = [list(blocks) for blocks in zip(both, first, second, third)]
 
     row = lax.broadcasted_iota(jnp.int32, (128, 2 * UNITS), 0)
     lane = lax.broadcasted_iota(jnp.int32, (128, 2 * UNITS), 1)
@@ -315,12 +342,10 @@
     pick = ((row % EXPERTS == wanted) & (row < 3 * EXPERTS)).astype(BF)
 
     hidden = hidden_of(parts, pick, (gate_own, gate_other, up_own, up_other))
-    made = [None] * 4
-    for index in (3, 2, 1, 0):
-        made[index] = down_of(hidden, (down_own, down_other), index)
-    sums = reduce_stage([[pair[0] for pair in made], [pair[1] for pair in made]], ["z", "x"])
-    sums = reduce_stage([quarters(part) for part in sums], ["x", "z"])
-    moe_out = reduce_stage([quarters(jnp.concatenate(sums, axis=1))], ["y"])[0]
+    made = [down_of(hidden[half], (down_own, down_other), half) for half in range(2)]
+    sums = reduce_stage(made, ["z", "x"], True)
+    sums = reduce_stage([quarters(part) for part in sums], ["x", "z"], True)
+    moe_out = reduce_stage([quarters(jnp.concatenate(sums, axis=1))], ["y"], False)[0]
     return attn_out, moe_out
 
 

time: 192 us -> 160 us (0.83)
  waiting for transfers between devices: 78.7 us -> 65 us
  Pallas kernels: 45.7 us -> 34.2 us
  local copies, waits for them, and re-layouts: 11.6 us -> 4.18 us
    ppermute x30, waiting for transfers between devices: 78.7 us -> 65 us  [move(): return lax.ppermute(array, names, pairs)]
    pallas_call x4 -> x2, Pallas kernels: 22.4 us -> 9.53 us  [down_of(): pl.pallas_call(down_kernel, grid=(HALF // N_TILE,), in_specs=[pl.BlockSpe...]
    unnamed x23 -> x6, local copies, waits for them, and re-layouts: 9.91 us -> 2.35 us
    pallas_call x1, Pallas kernels: 5.76 us -> 2.64 us  [attend(): pl.pallas_call(attend_kernel, grid_spec=pltpu.PrefetchScalarGridSpec(num_...]
    pallas_call x1, Pallas kernels: 9.67 us -> 12.5 us  [hidden_of(): pl.pallas_call(early_kernel, grid=(STEPS,), in_specs=[block] * 6 + [first...]
  transfers between devices with their start and end apart: 33 -> 33, of which waited for: 14 -> 17; matrix products, arithmetic and copies ran while one was open for 1% -> 3% of each run, Pallas kernels for 21% -> 19%
where the time goes in v3:
time: 160 us; the launch traced here: 159 us
  waiting for transfers between devices  65 us (41%)
  starting transfers between devices  50.7 us (32%)
  Pallas kernels  34.2 us (21%)
  other arithmetic  4.19 us (3%)
  local copies, waits for them, and re-layouts  4.18 us (3%)
    ppermute x30, waiting for transfers between devices, move(): return lax.ppermute(array, names, pairs)  65 us
    ppermute x30, starting transfers between devices, move(): return lax.ppermute(array, names, pairs)  50 us
    pallas_call x1, Pallas kernels, hidden_of(): pl.pallas_call(early_kernel, grid=(STEPS,), in_specs=[block] * 6 + [first...  12.5 us
    pallas_call x1, Pallas kernels, hidden_of(): pl.pallas_call(late_kernel, grid=(STEPS,), in_specs=[block] * 2 + [first]...  9.54 us
    pallas_call x2, Pallas kernels, down_of(): pl.pallas_call(down_kernel, grid=(HALF // N_TILE,), in_specs=[pl.BlockSpe...  9.53 us
  transfers between devices with their start and end apart: 33, of which 17 were waited for; matrix products, arithmetic and copies ran while one was open for 3% of the time, Pallas kernels for 19%

profile of v3, /device:TPU:6, one launch (start us, length us, event | category | flops | bytes accessed | tf_op | source)
XLA Modules:
  0.0 159.2 jit_solution(14472950905179697837)
XLA Ops:
  9.4 4.2 %collective-permute-done.2 = bf16[8,7296]{1,0:T(8,128)(2,1)S(1)} collective-permute-done((bf16[8,7296]{1,0:T(8,128)(2,1)S(1)}, bf16[8,7296]{1,0:T(8,128)(2,1)S(1)}, u32[]{:S(2)}, u32[]{:S(2)}) %collective-permute-start.2) | collective-permute-done | bytes 116768 | tf_op jit(solution)/shard_map/ppermute | solution.py:253
  17.3 4.0 %collective-permute-start.10 = (bf16[32,3712]{1,0:T(8,128)(2,1)S(1)}, bf16[32,3712]{1,0:T(8,128)(2,1)S(1)}, u32[]{:S(2)}, u32[]{:S(2)}) collective-permute-start(bf16[32,3712]{1,0:T(8,128)(2,1)S(1)} %slice.7), channel_id=1, source_target_pairs={{0,64},{32,96},{64,0},{96,32},{4,68},{36,100},{68,4},{100,36},{1,6... | collective-permute-start | bytes 712712 | tf_op jit(solution)/shard_map/ppermute | solution.py:253
  22.3 4.0 %collective-permute-start.9 = (bf16[32,3712]{1,0:T(8,128)(2,1)S(1)}, bf16[32,3712]{1,0:T(8,128)(2,1)S(1)}, u32[]{:S(2)}, u32[]{:S(2)}) collective-permute-start(bf16[32,3712]{1,0:T(8,128)(2,1)S(1)} %slice.7), channel_id=1, source_target_pairs={{0,96},{32,0},{64,32},{96,64},{4,36},{36,68},{68,100},{100,4},{1,9... | collective-permute-start | bytes 712712 | tf_op jit(solution)/shard_map/ppermute | solution.py:253
  28.2 3.1 %collective-permute-done.8 = bf16[32,3712]{1,0:T(8,128)(2,1)S(1)} collective-permute-done((bf16[32,3712]{1,0:T(8,128)(2,1)S(1)}, bf16[32,3712]{1,0:T(8,128)(2,1)S(1)}, u32[]{:S(2)}, u32[]{:S(2)}) %collective-permute-start.8) | collective-permute-done | bytes 237600 | tf_op jit(solution)/shard_map/ppermute | solution.py:253
  38.4 2.3 %copy-done = bf16[4096,576]{0,1:T(8,128)(2,1)S(1)} copy-done((bf16[4096,576]{0,1:T(8,128)(2,1)S(1)}, bf16[4096,576]{0,1:T(8,128)(2,1)}, u32[]{:S(2)}) %copy-start) | copy-done | bytes 4718616
  40.7 2.6 %attend.1 = bf16[1,128,512]{2,1,0:T(8,128)(2,1)} custom-call(s32[1]{0:T(128)} %dynamic_slice.3.length_ref, bf16[1,128,576]{2,1,0:T(8,128)(2,1)S(1)} %copy.12.query_ref, bf16[576,4096]{1,0:T(8,128)(2,1)S(1)} %bitcast.4), custom_call_target="tpu_custom_call" | custom-call | flops 1140850688 | bytes 4718592 | tf_op jit(solution)/shard_map/attend/pallas_call | solution.py:70
  43.3 13.2 %collective-permute-done.11.refs_1_ = bf16[128,3584]{1,0:T(8,128)(2,1)} collective-permute-done((bf16[128,3584]{1,0:T(8,128)(2,1)}, bf16[128,3584]{1,0:T(8,128)(2,1)}, u32[]{:S(2)}, u32[]{:S(2)}) %collective-permute-start.11) | collective-permute-done | bytes 917536 | tf_op jit(solution)/shard_map/ppermute | solution.py:253
  56.6 2.7 %collective-permute-start.14 = (bf16[128,3712]{1,0:T(8,128)(2,1)S(1)}, bf16[128,3712]{1,0:T(8,128)(2,1)}, u32[]{:S(2)}, u32[]{:S(2)}) collective-permute-start(bf16[128,3712]{1,0:T(8,128)(2,1)S(1)} %collective-permute-done.12.refs_4_.refs_11_), channel_id=1, source_target_pairs={{0,8},{8,16},{16,24},{24,0},{4,28},{12,4},{20,12},{28,20},{1,9},{9... | collective-permute-start | bytes 2850824 | tf_op jit(solution)/shard_map/ppermute | solution.py:253
  60.1 12.5 %early.1 = (f32[384,1024]{1,0:T(8,128)}, f32[384,1024]{1,0:T(8,128)}) custom-call(bf16[128,3584]{1,0:T(8,128)(2,1)} %pad_maximum_fusion.1.refs_0_, bf16[128,3584]{1,0:T(8,128)(2,1)} %collective-permute-done.11.refs_1_, bf16[128,3584]{1,0:T(8,128)(2,1)} %collective-permute-done.16.refs_2_, bf16[128,3712]{1,0:T(8,128)(2,1)S(1)} %pad_maximum_fusion.refs_3_.refs_10_, ...), custom_call_target="tpu_custom_call" | custom-call | flops 5637144576 | bytes 20185088 | tf_op jit(solution)/shard_map/early/pallas_call | solution.py:179
  74.2 9.5 %late.1 = (bf16[512,512]{1,0:T(8,128)(2,1)S(1)}, bf16[512,512]{1,0:T(8,128)(2,1)S(1)}) custom-call(bf16[128,3584]{1,0:T(8,128)(2,1)} %collective-permute-done.13.refs_0_, bf16[128,3712]{1,0:T(8,128)(2,1)} %collective-permute-done.14.refs_1_.refs_13_, bf16[7168,256]{1,0:T(8,128)(2,1)} %bitcast.8, ...), custom_call_target="tpu_custom_call" | custom-call | flops 1879048192 | bytes 16515072 | tf_op jit(solution)/shard_map/late/pallas_call | solution.py:190
  83.8 4.8 %down.3 = (bf16[128,3584]{1,0:T(8,128)(2,1)S(1)}, bf16[128,3584]{1,0:T(8,128)(2,1)S(1)}, bf16[128,3584]{1,0:T(8,128)(2,1)S(1)}, bf16[128,3584]{1,0:T(8,128)(2,1)S(1)}) custom-call(bf16[512,512]{1,0:T(8,128)(2,1)S(1)} %get-tuple-element.41.h, bf16[256,7168]{1,0:T(8,128)(2,1)} %bitcast.2.d0, bf16[256,7168]{1,0:T(8,128)(2,1)} %collective-permute-done.17.d1), custom_call_target="tpu_custom_call" | custom-call | flops 1879048192 | bytes 7340032 | tf_op jit(solution)/shard_map/down/pallas_call | solution.py:222
  88.7 3.2 %collective-permute-start.24 = (bf16[128,3584]{1,0:T(8,128)(2,1)S(1)}, bf16[128,3584]{1,0:T(8,128)(2,1)S(1)}, u32[]{:S(2)}, u32[]{:S(2)}) collective-permute-start(bf16[128,3584]{1,0:T(8,128)(2,1)S(1)} %get-tuple-element.43), channel_id=1, source_target_pairs={{0,8},{8,16},{16,24},{24,0},{4,28},{12,4},{20,12},{28,20},{1,9},{9... | collective-permute-start | bytes 2752520 | tf_op jit(solution)/shard_map/ppermute | solution.py:253
  91.9 4.7 %down.2 = (bf16[128,3584]{1,0:T(8,128)(2,1)S(1)}, bf16[128,3584]{1,0:T(8,128)(2,1)S(1)}, bf16[128,3584]{1,0:T(8,128)(2,1)S(1)}, bf16[128,3584]{1,0:T(8,128)(2,1)S(1)}) custom-call(bf16[512,512]{1,0:T(8,128)(2,1)S(1)} %get-tuple-element.35.h, bf16[256,7168]{1,0:T(8,128)(2,1)} %bitcast.2.d0, bf16[256,7168]{1,0:T(8,128)(2,1)} %collective-permute-done.17.d1), custom_call_target="tpu_custom_call" | custom-call | flops 1879048192 | bytes 7340032 | tf_op jit(solution)/shard_map/down/pallas_call | solution.py:222
  98.9 11.9 %collective-permute-done.25 = bf16[128,3584]{1,0:T(8,128)(2,1)S(1)} collective-permute-done((bf16[128,3584]{1,0:T(8,128)(2,1)S(1)}, bf16[128,3584]{1,0:T(8,128)(2,1)S(1)}, u32[]{:S(2)}, u32[]{:S(2)}) %collective-permute-start.25) | collective-permute-done | bytes 917536 | tf_op jit(solution)/shard_map/ppermute | solution.py:253
  111.5 4.9 %collective-permute-done.19 = bf16[128,3584]{1,0:T(8,128)(2,1)S(1)} collective-permute-done((bf16[128,3584]{1,0:T(8,128)(2,1)S(1)}, bf16[128,3584]{1,0:T(8,128)(2,1)S(1)}, u32[]{:S(2)}, u32[]{:S(2)}) %collective-permute-start.19) | collective-permute-done | bytes 917536 | tf_op jit(solution)/shard_map/ppermute | solution.py:253
  116.6 3.8 %collective-permute-start.20 = (bf16[128,3584]{1,0:T(8,128)(2,1)S(1)}, bf16[128,3584]{1,0:T(8,128)(2,1)S(1)}, u32[]{:S(2)}, u32[]{:S(2)}) collective-permute-start(bf16[128,3584]{1,0:T(8,128)(2,1)S(1)} %add_convert_fusion.3), channel_id=1, source_target_pairs={{0,96},{32,0},{64,32},{96,64},{4,36},{36,68},{68,100},{100,4},{1,9... | collective-permute-start | bytes 2752520 | tf_op jit(solution)/shard_map/ppermute | solution.py:253
  120.4 5.4 %collective-permute-done.26 = bf16[128,3584]{1,0:T(8,128)(2,1)S(1)} collective-permute-done((bf16[128,3584]{1,0:T(8,128)(2,1)S(1)}, bf16[128,3584]{1,0:T(8,128)(2,1)S(1)}, u32[]{:S(2)}, u32[]{:S(2)}) %collective-permute-start.26) | collective-permute-done | bytes 917536 | tf_op jit(solution)/shard_map/ppermute | solution.py:253
  128.2 5.5 %collective-permute-done.20 = bf16[128,3584]{1,0:T(8,128)(2,1)S(1)} collective-permute-done((bf16[128,3584]{1,0:T(8,128)(2,1)S(1)}, bf16[128,3584]{1,0:T(8,128)(2,1)S(1)}, u32[]{:S(2)}, u32[]{:S(2)}) %collective-permute-start.20) | collective-permute-done | bytes 917536 | tf_op jit(solution)/shard_map/ppermute | solution.py:253
  134.5 3.0 %collective-permute-start.21 = (bf16[32,3584]{1,0:T(8,128)(2,1)S(1)}, bf16[32,3584]{1,0:T(8,128)(2,1)S(1)}, u32[]{:S(2)}, u32[]{:S(2)}) collective-permute-start(bf16[32,3584]{1,0:T(8,128)(2,1)S(1)} %get-tuple-element.46), channel_id=1, source_target_pairs={{0,8},{8,16},{16,24},{24,0},{4,28},{12,4},{20,12},{28,20},{1,9},{9... | collective-permute-start | bytes 688136 | tf_op jit(solution)/shard_map/ppermute | solution.py:253
  137.5 3.8 %collective-permute-start.29 = (bf16[32,3584]{1,0:T(8,128)(2,1)S(1)}, bf16[32,3584]{1,0:T(8,128)(2,1)S(1)}, u32[]{:S(2)}, u32[]{:S(2)}) collective-permute-start(bf16[32,3584]{1,0:T(8,128)(2,1)S(1)} %add_convert_fusion.5), channel_id=1, source_target_pairs={{0,96},{32,0},{64,32},{96,64},{4,36},{36,68},{68,100},{100,4},{1,9... | collective-permute-start | bytes 688136 | tf_op jit(solution)/shard_map/ppermute | solution.py:253
  141.6 3.2 %collective-permute-done.29 = bf16[32,3584]{1,0:T(8,128)(2,1)S(1)} collective-permute-done((bf16[32,3584]{1,0:T(8,128)(2,1)S(1)}, bf16[32,3584]{1,0:T(8,128)(2,1)S(1)}, u32[]{:S(2)}, u32[]{:S(2)}) %collective-permute-start.29) | collective-permute-done | bytes 229408 | tf_op jit(solution)/shard_map/ppermute | solution.py:253
  144.9 3.9 %collective-permute-done.23 = bf16[32,3584]{1,0:T(8,128)(2,1)S(1)} collective-permute-done((bf16[32,3584]{1,0:T(8,128)(2,1)S(1)}, bf16[32,3584]{1,0:T(8,128)(2,1)S(1)}, u32[]{:S(2)}, u32[]{:S(2)}) %collective-permute-start.23) | collective-permute-done | bytes 229408 | tf_op jit(solution)/shard_map/ppermute | solution.py:253
  149.9 2.3 %collective-permute-start.31 = (bf16[8,7168]{1,0:T(8,128)(2,1)S(1)}, bf16[8,7168]{1,0:T(8,128)(2,1)S(1)}, u32[]{:S(2)}, u32[]{:S(2)}) collective-permute-start(bf16[8,7168]{1,0:T(8,128)(2,1)S(1)} %get-tuple-element.52), channel_id=1, source_target_pairs={{0,3},{1,0},{2,1},{3,2},{4,5},{5,6},{6,7},{7,4},{8,11},{9,8},{10,9... | collective-permute-start | bytes 344072 | tf_op jit(solution)/shard_map/ppermute | solution.py:253
  155.0 3.5 %collective-permute-done.32 = bf16[8,7168]{1,0:T(8,128)(2,1)S(1)} collective-permute-done((bf16[8,7168]{1,0:T(8,128)(2,1)S(1)}, bf16[8,7168]{1,0:T(8,128)(2,1)S(1)}, u32[]{:S(2)}, u32[]{:S(2)}) %collective-permute-start.32) | collective-permute-done | bytes 114720 | tf_op jit(solution)/shard_map/ppermute | solution.py:253
  (80 shorter events, 36.1 us)
Async XLA Ops:
  0.6 13.1 %collective-permute-start.3 = (bf16[7168,256]{1,0:T(8,128)(2,1)}, bf16[7168,256]{1,0:T(8,128)(2,1)}, u32[]{:S(2)}, u32[]{:S(2)}) collective-permute-start(bf16[7168,256]{1,0:T(8,128)(2,1)} %bitcast.5), channel_id=1, source_target_pairs={{0,4},{4,0},{1,5},{5,1},{2,6},{6,2},{3,7},{7,3},{8,12},{12,8},{9,1... | collective-permute-start | bytes 11010056 | tf_op jit(solution)/shard_map/ppermute | solution.py:239
  0.7 13.0 %collective-permute-start.4 = (bf16[7168,256]{1,0:T(8,128)(2,1)}, bf16[7168,256]{1,0:T(8,128)(2,1)}, u32[]{:S(2)}, u32[]{:S(2)}) collective-permute-start(bf16[7168,256]{1,0:T(8,128)(2,1)} %bitcast.10), channel_id=1, source_target_pairs={{0,4},{4,0},{1,5},{5,1},{2,6},{6,2},{3,7},{7,3},{8,12},{12,8},{9,1... | collective-permute-start | bytes 11010056 | tf_op jit(solution)/shard_map/ppermute | solution.py:239
  13.7 8.5 %collective-permute-start.5 = (bf16[32,3584]{1,0:T(8,128)(2,1)S(1)}, bf16[32,3584]{1,0:T(8,128)(2,1)S(1)}, u32[]{:S(2)}, u32[]{:S(2)}) collective-permute-start(bf16[32,3584]{1,0:T(8,128)(2,1)S(1)} %slice.6), channel_id=1, source_target_pairs={{0,8},{8,16},{16,24},{24,0},{4,28},{12,4},{20,12},{28,20},{1,9},{9... | collective-permute-start | bytes 688136 | tf_op jit(solution)/shard_map/ppermute | solution.py:253
  14.3 12.9 %collective-permute-start.6 = (bf16[32,3584]{1,0:T(8,128)(2,1)S(1)}, bf16[32,3584]{1,0:T(8,128)(2,1)S(1)}, u32[]{:S(2)}, u32[]{:S(2)}) collective-permute-start(bf16[32,3584]{1,0:T(8,128)(2,1)S(1)} %slice.6), channel_id=1, source_target_pairs={{0,24},{8,0},{16,8},{24,16},{4,12},{12,20},{20,28},{28,4},{1,25},{... | collective-permute-start | bytes 688136 | tf_op jit(solution)/shard_map/ppermute | solution.py:253
  15.8 11.4 %collective-permute-start.7 = (bf16[32,3584]{1,0:T(8,128)(2,1)S(1)}, bf16[32,3584]{1,0:T(8,128)(2,1)S(1)}, u32[]{:S(2)}, u32[]{:S(2)}) collective-permute-start(bf16[32,3584]{1,0:T(8,128)(2,1)S(1)} %slice.6), channel_id=1, source_target_pairs={{0,16},{8,24},{16,0},{24,8},{4,20},{12,28},{20,4},{28,12},{1,17},{... | collective-permute-start | bytes 688136 | tf_op jit(solution)/shard_map/ppermute | solution.py:253
  17.3 11.0 %collective-permute-start.10 = (bf16[32,3712]{1,0:T(8,128)(2,1)S(1)}, bf16[32,3712]{1,0:T(8,128)(2,1)S(1)}, u32[]{:S(2)}, u32[]{:S(2)}) collective-permute-start(bf16[32,3712]{1,0:T(8,128)(2,1)S(1)} %slice.7), channel_id=1, source_target_pairs={{0,64},{32,96},{64,0},{96,32},{4,68},{36,100},{68,4},{100,36},{1,6... | collective-permute-start | bytes 712712 | tf_op jit(solution)/shard_map/ppermute | solution.py:253
  21.2 10.1 %collective-permute-start.8 = (bf16[32,3712]{1,0:T(8,128)(2,1)S(1)}, bf16[32,3712]{1,0:T(8,128)(2,1)S(1)}, u32[]{:S(2)}, u32[]{:S(2)}) collective-permute-start(bf16[32,3712]{1,0:T(8,128)(2,1)S(1)} %slice.7), channel_id=1, source_target_pairs={{0,32},{32,64},{64,96},{96,0},{4,100},{36,4},{68,36},{100,68},{1,3... | collective-permute-start | bytes 712712 | tf_op jit(solution)/shard_map/ppermute | solution.py:253
  22.3 9.8 %collective-permute-start.9 = (bf16[32,3712]{1,0:T(8,128)(2,1)S(1)}, bf16[32,3712]{1,0:T(8,128)(2,1)S(1)}, u32[]{:S(2)}, u32[]{:S(2)}) collective-permute-start(bf16[32,3712]{1,0:T(8,128)(2,1)S(1)} %slice.7), channel_id=1, source_target_pairs={{0,96},{32,0},{64,32},{96,64},{4,36},{36,68},{68,100},{100,4},{1,9... | collective-permute-start | bytes 712712 | tf_op jit(solution)/shard_map/ppermute | solution.py:253
  32.2 51.6 %collective-permute-start.17 = (bf16[256,7168]{1,0:T(8,128)(2,1)}, bf16[256,7168]{1,0:T(8,128)(2,1)}, u32[]{:S(2)}, u32[]{:S(2)}) collective-permute-start(bf16[256,7168]{1,0:T(8,128)(2,1)} %bitcast.2.d0), channel_id=1, source_target_pairs={{0,4},{4,0},{1,5},{5,1},{2,6},{6,2},{3,7},{7,3},{8,12},{12,8},{9,1... | collective-permute-start | bytes 11010056 | tf_op jit(solution)/shard_map/ppermute | solution.py:239
  32.3 24.3 %collective-permute-start.12 = (bf16[128,3712]{1,0:T(8,128)(2,1)S(1)}, bf16[128,3712]{1,0:T(8,128)(2,1)S(1)}, u32[]{:S(2)}, u32[]{:S(2)}) collective-permute-start(bf16[128,3712]{1,0:T(8,128)(2,1)S(1)} %pad_maximum_fusion.refs_3_.refs_10_), channel_id=1, source_target_pairs={{0,8},{8,16},{16,24},{24,0},{4,28},{12,4},{20,12},{28,20},{1,9},{9... | collective-permute-start | bytes 2850824 | tf_op jit(solution)/shard_map/ppermute | solution.py:253
  34.3 22.2 %collective-permute-start.11 = (bf16[128,3584]{1,0:T(8,128)(2,1)}, bf16[128,3584]{1,0:T(8,128)(2,1)}, u32[]{:S(2)}, u32[]{:S(2)}) collective-permute-start(bf16[128,3584]{1,0:T(8,128)(2,1)} %pad_maximum_fusion.1.refs_0_), channel_id=1, source_target_pairs={{0,32},{32,64},{64,96},{96,0},{4,100},{36,4},{68,36},{100,68},{1,3... | collective-permute-start | bytes 2752520 | tf_op jit(solution)/shard_map/ppermute | solution.py:253
  35.3 24.8 %collective-permute-start.15 = (bf16[128,3712]{1,0:T(8,128)(2,1)S(1)}, bf16[128,3712]{1,0:T(8,128)(2,1)S(1)}, u32[]{:S(2)}, u32[]{:S(2)}) collective-permute-start(bf16[128,3712]{1,0:T(8,128)(2,1)S(1)} %pad_maximum_fusion.refs_3_.refs_10_), channel_id=1, source_target_pairs={{0,24},{8,0},{16,8},{24,16},{4,12},{12,20},{20,28},{28,4},{1,25},{... | collective-permute-start | bytes 2850824 | tf_op jit(solution)/shard_map/ppermute | solution.py:253
  35.4 24.8 %collective-permute-start.16 = (bf16[128,3584]{1,0:T(8,128)(2,1)}, bf16[128,3584]{1,0:T(8,128)(2,1)}, u32[]{:S(2)}, u32[]{:S(2)}) collective-permute-start(bf16[128,3584]{1,0:T(8,128)(2,1)} %pad_maximum_fusion.1.refs_0_), channel_id=1, source_target_pairs={{0,96},{32,0},{64,32},{96,64},{4,36},{36,68},{68,100},{100,4},{1,9... | collective-permute-start | bytes 2752520 | tf_op jit(solution)/shard_map/ppermute | solution.py:253
  56.6 17.7 %collective-permute-start.14 = (bf16[128,3712]{1,0:T(8,128)(2,1)S(1)}, bf16[128,3712]{1,0:T(8,128)(2,1)}, u32[]{:S(2)}, u32[]{:S(2)}) collective-permute-start(bf16[128,3712]{1,0:T(8,128)(2,1)S(1)} %collective-permute-done.12.refs_4_.refs_11_), channel_id=1, source_target_pairs={{0,8},{8,16},{16,24},{24,0},{4,28},{12,4},{20,12},{28,20},{1,9},{9... | collective-permute-start | bytes 2850824 | tf_op jit(solution)/shard_map/ppermute | solution.py:253
  59.3 14.9 %collective-permute-start.13 = (bf16[128,3584]{1,0:T(8,128)(2,1)}, bf16[128,3584]{1,0:T(8,128)(2,1)}, u32[]{:S(2)}, u32[]{:S(2)}) collective-permute-start(bf16[128,3584]{1,0:T(8,128)(2,1)} %collective-permute-done.11.refs_1_), channel_id=1, source_target_pairs={{0,32},{32,64},{64,96},{96,0},{4,100},{36,4},{68,36},{100,68},{1,3... | collective-permute-start | bytes 2752520 | tf_op jit(solution)/shard_map/ppermute | solution.py:253
  88.6 22.3 %collective-permute-start.25 = (bf16[128,3584]{1,0:T(8,128)(2,1)S(1)}, bf16[128,3584]{1,0:T(8,128)(2,1)S(1)}, u32[]{:S(2)}, u32[]{:S(2)}) collective-permute-start(bf16[128,3584]{1,0:T(8,128)(2,1)S(1)} %get-tuple-element.45), channel_id=1, source_target_pairs={{0,24},{8,0},{16,8},{24,16},{4,12},{12,20},{20,28},{28,4},{1,25},{... | collective-permute-start | bytes 2752520 | tf_op jit(solution)/shard_map/ppermute | solution.py:253
  88.7 31.7 %collective-permute-start.24 = (bf16[128,3584]{1,0:T(8,128)(2,1)S(1)}, bf16[128,3584]{1,0:T(8,128)(2,1)S(1)}, u32[]{:S(2)}, u32[]{:S(2)}) collective-permute-start(bf16[128,3584]{1,0:T(8,128)(2,1)S(1)} %get-tuple-element.43), channel_id=1, source_target_pairs={{0,8},{8,16},{16,24},{24,0},{4,28},{12,4},{20,12},{28,20},{1,9},{9... | collective-permute-start | bytes 2752520 | tf_op jit(solution)/shard_map/ppermute | solution.py:253
  96.7 19.7 %collective-permute-start.19 = (bf16[128,3584]{1,0:T(8,128)(2,1)S(1)}, bf16[128,3584]{1,0:T(8,128)(2,1)S(1)}, u32[]{:S(2)}, u32[]{:S(2)}) collective-permute-start(bf16[128,3584]{1,0:T(8,128)(2,1)S(1)} %get-tuple-element.40), channel_id=1, source_target_pairs={{0,96},{32,0},{64,32},{96,64},{4,36},{36,68},{68,100},{100,4},{1,9... | collective-permute-start | bytes 2752520 | tf_op jit(solution)/shard_map/ppermute | solution.py:253
  98.1 30.2 %collective-permute-start.18 = (bf16[128,3584]{1,0:T(8,128)(2,1)S(1)}, bf16[128,3584]{1,0:T(8,128)(2,1)S(1)}, u32[]{:S(2)}, u32[]{:S(2)}) collective-permute-start(bf16[128,3584]{1,0:T(8,128)(2,1)S(1)} %get-tuple-element.38), channel_id=1, source_target_pairs={{0,32},{32,64},{64,96},{96,0},{4,100},{36,4},{68,36},{100,68},{1,3... | collective-permute-start | bytes 2752520 | tf_op jit(solution)/shard_map/ppermute | solution.py:253
  111.1 14.7 %collective-permute-start.26 = (bf16[128,3584]{1,0:T(8,128)(2,1)S(1)}, bf16[128,3584]{1,0:T(8,128)(2,1)S(1)}, u32[]{:S(2)}, u32[]{:S(2)}) collective-permute-start(bf16[128,3584]{1,0:T(8,128)(2,1)S(1)} %add_convert_fusion.1), channel_id=1, source_target_pairs={{0,24},{8,0},{16,8},{24,16},{4,12},{12,20},{20,28},{28,4},{1,25},{... | collective-permute-start | bytes 2752520 | tf_op jit(solution)/shard_map/ppermute | solution.py:253
  116.6 17.1 %collective-permute-start.20 = (bf16[128,3584]{1,0:T(8,128)(2,1)S(1)}, bf16[128,3584]{1,0:T(8,128)(2,1)S(1)}, u32[]{:S(2)}, u32[]{:S(2)}) collective-permute-start(bf16[128,3584]{1,0:T(8,128)(2,1)S(1)} %add_convert_fusion.3), channel_id=1, source_target_pairs={{0,96},{32,0},{64,32},{96,64},{4,36},{36,68},{68,100},{100,4},{1,9... | collective-permute-start | bytes 2752520 | tf_op jit(solution)/shard_map/ppermute | solution.py:253
  126.1 11.3 %collective-permute-start.28 = (bf16[32,3584]{1,0:T(8,128)(2,1)S(1)}, bf16[32,3584]{1,0:T(8,128)(2,1)S(1)}, u32[]{:S(2)}, u32[]{:S(2)}) collective-permute-start(bf16[32,3584]{1,0:T(8,128)(2,1)S(1)} %get-tuple-element.49), channel_id=1, source_target_pairs={{0,96},{32,0},{64,32},{96,64},{4,36},{36,68},{68,100},{100,4},{1,9... | collective-permute-start | bytes 688136 | tf_op jit(solution)/shard_map/ppermute | solution.py:253
  127.7 13.9 %collective-permute-start.27 = (bf16[32,3584]{1,0:T(8,128)(2,1)S(1)}, bf16[32,3584]{1,0:T(8,128)(2,1)S(1)}, u32[]{:S(2)}, u32[]{:S(2)}) collective-permute-start(bf16[32,3584]{1,0:T(8,128)(2,1)S(1)} %get-tuple-element.48), channel_id=1, source_target_pairs={{0,32},{32,64},{64,96},{96,0},{4,100},{36,4},{68,36},{100,68},{1,3... | collective-permute-start | bytes 688136 | tf_op jit(solution)/shard_map/ppermute | solution.py:253
  134.5 10.4 %collective-permute-start.21 = (bf16[32,3584]{1,0:T(8,128)(2,1)S(1)}, bf16[32,3584]{1,0:T(8,128)(2,1)S(1)}, u32[]{:S(2)}, u32[]{:S(2)}) collective-permute-start(bf16[32,3584]{1,0:T(8,128)(2,1)S(1)} %get-tuple-element.46), channel_id=1, source_target_pairs={{0,8},{8,16},{16,24},{24,0},{4,28},{12,4},{20,12},{28,20},{1,9},{9... | collective-permute-start | bytes 688136 | tf_op jit(solution)/shard_map/ppermute | solution.py:253
  (12 other events, 101.1 us)

commit v4 on v3

v4 whole, which is shorter than its diff:
```python
import functools

import jax
import jax.numpy as jnp
from jax import lax
from jax.experimental import pallas as pl
from jax.experimental.pallas import tpu as pltpu
from jax.sharding import Mesh, PartitionSpec as P

WIDTH = 7168
LATENT = 512
KEY_DIM = 576
HEADS = 128
EXPERTS = 32
CTX = 4096
UNITS = 256
TOK = 8
CHIPS = 64
ROWS = CHIPS * TOK
PAY = WIDTH + 128
QK_SCALE = 192.0 ** (-0.5)
FAR_LOW = -1e30
ATT_ROWS = 1024
HALF = WIDTH // 2
K_STEP = 512
RETURN = (3584, 3584)
N_TILE = 896
VMEM_LIMIT = 8 * 2**20
STEPS = HALF // K_STEP
D_STEP = WIDTH // STEPS
PART = ROWS // 4
GROUP = ROWS // 16
BF = jnp.bfloat16
F32 = jnp.float32


def attend_kernel(length_ref, query_ref, cache_ref, out_ref, top_ref, sum_ref, mix_ref):
    step = pl.program_id(0)
    length = length_ref[0]

    @pl.when(step == 0)
    def _():
        top_ref[...] = jnp.full_like(top_ref, FAR_LOW)
        sum_ref[...] = jnp.zeros_like(sum_ref)
        mix_ref[...] = jnp.zeros_like(mix_ref)

    @pl.when(step * ATT_ROWS < length)
    def _():
        rows = cache_ref[...]
        scores = QK_SCALE * lax.dot_general(
            query_ref[0], rows, (((1,), (0,)), ((), ())), preferred_element_type=F32
        )
        place = step * ATT_ROWS + lax.broadcasted_iota(jnp.int32, scores.shape, 1)
        scores = jnp.where(place < length, scores, FAR_LOW)
        top_old = top_ref[...]
        top_new = jnp.maximum(top_old, jnp.max(scores, axis=1, keepdims=True))
        weights = jnp.exp(scores - top_new)
        scale = jnp.exp(top_old - top_new)
        top_ref[...] = top_new
        sum_ref[...] = sum_ref[...] * scale + jnp.sum(weights, axis=1, keepdims=True)
        mix_ref[...] = mix_ref[...] * scale + lax.dot_general(
            weights.astype(BF), rows[:LATENT], (((1,), (1,)), ((), ())), preferred_element_type=F32
        )

    @pl.when(step == pl.num_programs(0) - 1)
    def _():
        out_ref[0] = (mix_ref[...] / sum_ref[...]).astype(BF)


def attend(length, query_rows, cache_latent):
    def cache_block(step, length_ref):
        return 0, jnp.minimum(step, (length_ref[0] - 1) // ATT_ROWS)

    return pl.pallas_call(
        attend_kernel,
        grid_spec=pltpu.PrefetchScalarGridSpec(
            num_scalar_prefetch=1,
            grid=(CTX // ATT_ROWS,),
            in_specs=[
                pl.BlockSpec((1, HEADS, KEY_DIM), lambda step, length_ref: (0, 0, 0)),
                pl.BlockSpec((KEY_DIM, ATT_ROWS), cache_block),
            ],
            out_specs=pl.BlockSpec((1, HEADS, LATENT), lambda step, length_ref: (0, 0, 0)),
            scratch_shapes=[
                pltpu.VMEM((HEADS, 1), F32),
                pltpu.VMEM((HEADS, 1), F32),
                pltpu.VMEM((HEADS, LATENT), F32),
            ],
        ),
        out_shape=jax.ShapeDtypeStruct((1, HEADS, LATENT), BF),
        compiler_params=pltpu.CompilerParams(vmem_limit_bytes=VMEM_LIMIT),
        cost_estimate=pl.CostEstimate(
            flops=2 * HEADS * CTX * (KEY_DIM + LATENT),
            bytes_accessed=CTX * KEY_DIM * 2,
            transcendentals=HEADS * CTX,
        ),
        name="attend",
    )(length, query_rows, cache_latent.T)


def own_kernel(*refs):
    a_ref, b_ref, weights_a, weights_b, d_own, d_other = *refs[:2], refs[2:6], refs[6:10], *refs[10:12]
    out_a, out_b, held, down = refs[12:]
    step = pl.program_id(0)

    @pl.when(step == 0)
    def _():
        out_a[...] = jnp.zeros_like(out_a)
        out_b[...] = jnp.zeros_like(out_b)

    for block, weights, out, start in ((a_ref, weights_a, out_a, 0), (b_ref, weights_b, out_b, HALF)):
        rows = pl.ds(pl.multiple_of(start + step * K_STEP, K_STEP), K_STEP)
        for place, weight in enumerate(weights):
            lanes = slice(place * UNITS, (place + 1) * UNITS)
            value = weight[...]
            held[rows, lanes] = value
            out[:, lanes] += jnp.dot(block[...], value, preferred_element_type=F32)
    columns = pl.ds(pl.multiple_of(step * D_STEP, D_STEP), D_STEP)
    down[:UNITS, columns] = d_own[...]
    down[UNITS:, columns] = d_other[...]


def own_part(a_block, b_block, weights, downs):
    block = pl.BlockSpec((PART, K_STEP), lambda step: (0, step))
    first = pl.BlockSpec((K_STEP, UNITS), lambda step: (step, 0))
    second = pl.BlockSpec((K_STEP, UNITS), lambda step: (step + STEPS, 0))
    down = pl.BlockSpec((UNITS, D_STEP), lambda step: (0, step))
    sums = pl.BlockSpec((PART, 4 * UNITS), lambda step: (0, 0))
    return pl.pallas_call(
        own_kernel,
        grid=(STEPS,),
        in_specs=[block] * 2 + [first] * 4 + [second] * 4 + [down] * 2,
        out_specs=[sums] * 2 + [pl.BlockSpec(memory_space=pltpu.VMEM)] * 2,
        out_shape=[jax.ShapeDtypeStruct((PART, 4 * UNITS), F32)] * 2
        + [pltpu.VMEM((WIDTH, 4 * UNITS), BF), pltpu.VMEM((2 * UNITS, WIDTH), BF)],
        compiler_params=pltpu.CompilerParams(vmem_limit_bytes=VMEM_LIMIT),
        cost_estimate=pl.CostEstimate(
            flops=2 * PART * WIDTH * 4 * UNITS,
            bytes_accessed=2 * (PART + 6 * UNITS) * WIDTH,
            transcendentals=0,
        ),
        name="own",
    )(a_block, b_block, *weights, *weights, *downs)


def on_chip(kernel, name, operands, shapes, flops, aliases=()):
    spec = pl.BlockSpec(memory_space=pltpu.VMEM)
    return pl.pallas_call(
        kernel,
        in_specs=[spec] * len(operands),
        out_specs=[spec] * len(shapes),
        out_shape=[pltpu.VMEM(*shape) for shape in shapes],
        compiler_params=pltpu.CompilerParams(vmem_limit_bytes=VMEM_LIMIT),
        cost_estimate=pl.CostEstimate(flops=flops, bytes_accessed=0, transcendentals=0),
        input_output_aliases=dict(aliases),
        name=name,
    )(*operands)


def early_kernel(a1, a2, b1, b2, held, out_a, out_b, _):
    for blocks, out, start in (((a1, a2), out_a, 0), ((b1, b2), out_b, HALF)):
        stacked = jnp.concatenate([block[:, :HALF] for block in blocks], axis=0)
        out[...] = jnp.dot(stacked, held[start : start + HALF], preferred_element_type=F32)


def send_blocks(hidden, down, low, outs):
    width = outs[0].shape[1]
    for start in range(0, width, N_TILE):
        made = jnp.dot(
            hidden[...], down[:, low + start : low + start + N_TILE], preferred_element_type=F32
        ).astype(BF)
        for place, out in enumerate(outs):
            out[:, start : start + N_TILE] = made[place * PART : (place + 1) * PART]


def late_kernel(a3, b0, b1, b2, b3, held, pick, own_a, own_b, early_a, early_b, out_a, out_b):
    last_a = jnp.dot(a3[...], held[:HALF], preferred_element_type=F32)
    last_b = jnp.dot(b3[:, :HALF], held[HALF:], preferred_element_type=F32)

    def group(own, early, last, outer, inner):
        low = inner * GROUP
        if outer == 0:
            return own[low : low + GROUP]
        if outer == 3:
            return last[low : low + GROUP]
        low = low + (outer - 1) * PART
        return early[low : low + GROUP]

    for kx, tail in enumerate((b0, b1, b2, b3)):
        share = jnp.dot(tail[:, HALF:], pick[...], preferred_element_type=F32)
        for kz in range(4):
            total = group(own_a, early_a, last_a, kz, kx) + group(own_b, early_b, last_b, kx, kz)
            gate, up = total[:, : 2 * UNITS], total[:, 2 * UNITS :]
            made = gate / (1.0 + jnp.exp(-gate)) * up * share[kz * GROUP : (kz + 1) * GROUP]
            made = made.astype(BF)
            low_a, low_b = (kz * 4 + kx) * GROUP, (kx * 4 + kz) * GROUP
            out_a[low_a : low_a + GROUP, :] = made
            out_b[low_b : low_b + GROUP, :] = made


def down_kernel(low, hidden, down, *outs):
    send_blocks(hidden, down, low, outs)


def sent_blocks(parts, own_sums, held, down, pick):
    a_blocks, b_blocks = parts
    sums = ((2 * PART, 4 * UNITS), F32)
    *early_sums, held = on_chip(
        early_kernel,
        "early",
        (*a_blocks[1:3], *b_blocks[1:3], held),
        (sums, sums, ((WIDTH, 4 * UNITS), BF)),
        2 * 2 * PART * WIDTH * 4 * UNITS,
        {4: 2},
    )
    made = ((ROWS, 2 * UNITS), BF)
    halves = on_chip(
        late_kernel,
        "late",
        (a_blocks[3], *b_blocks, held, pick, *own_sums, *early_sums),
        (made, made),
        2 * PART * WIDTH * 4 * UNITS,
    )
    def half(place, hidden):
        return on_chip(
            functools.partial(down_kernel, place * RETURN[0]),
            "down",
            (hidden, down),
            [((PART, RETURN[place]), BF)] * 4,
            2 * ROWS * 2 * UNITS * RETURN[place],
        )

    first, hidden = lax.optimization_barrier((half(0, halves[0]), halves[1]))
    return [first, half(1, hidden)]


def swap(array):
    return lax.ppermute(array, "core", [(0, 1), (1, 0)])


def move(array, axis, way):
    names = ("core", axis) if axis == "y" else (axis, "core")

    def flat(core, place):
        return core * 4 + place if axis == "y" else place * 2 + core

    pairs = [
        (flat(core, place), flat(core, (place + (way if core == 0 else -way)) % 4))
        for core in range(2)
        for place in range(4)
    ]
    return lax.ppermute(array, names, pairs)


def gather_stage(parts, axes):
    return [
        [part, move(part, axis, 1), move(part, axis, -1), move(part, axis, 2)]
        for part, axis in zip(parts, axes)
    ]


def joined(blocks):
    return jnp.concatenate(blocks, axis=0)


def added(*terms):
    total = terms[0].astype(F32)
    for term in terms[1:]:
        total = total + term.astype(F32)
    return total.astype(BF)


def reduce_stage(parts, axes, relay):
    if not relay:
        far = [move(blocks[3], axis, 2) for blocks, axis in zip(parts, axes)]
        near = [move(blocks[2], axis, 1) for blocks, axis in zip(parts, axes)]
        last = [move(blocks[1], axis, -1) for blocks, axis in zip(parts, axes)]
        return [
            added(blocks[0], n, l, f) for blocks, n, l, f in zip(parts, near, last, far)
        ]
    far = [move(blocks[3], axis, -1) for blocks, axis in zip(parts, axes)]
    near = [move(blocks[2], axis, 1) for blocks, axis in zip(parts, axes)]
    last = [
        move(added(blocks[1], relayed), axis, -1)
        for blocks, relayed, axis in zip(parts, far, axes)
    ]
    return [added(blocks[0], n, l) for blocks, n, l in zip(parts, near, last)]


def quarters(array):
    return jnp.split(array, 4, axis=0)


def payload_of(moe_input, expert_ids, gate_weights):
    chosen = expert_ids[:, :, None] == jnp.arange(EXPERTS, dtype=jnp.int32)
    shares = jnp.sum(jnp.where(chosen, gate_weights[:, :, None], 0.0), axis=1)
    high = lax.reduce_precision(shares, 8, 7)
    middle = lax.reduce_precision(shares - high, 8, 7)
    low = lax.reduce_precision(shares - high - middle, 8, 7)
    blank = jnp.zeros((TOK, 128 - 3 * EXPERTS), F32)
    tail = jnp.concatenate([high, middle, low, blank], axis=1).astype(BF)
    return jnp.concatenate([moe_input, tail], axis=1)


def per_device(
    query_rows,
    cache_latent,
    lengths,
    moe_input,
    expert_ids,
    gate_weights,
    expert_gate,
    expert_up,
    expert_down,
):
    chip = (lax.axis_index("z") * 4 + lax.axis_index("x")) * 2
    own = chip + lax.axis_index("core")
    other = chip + 1 - lax.axis_index("core")
    length = lax.dynamic_slice_in_dim(lengths, own * 4 + lax.axis_index("y"), 1)

    row = lax.broadcasted_iota(jnp.int32, (128, 2 * UNITS), 0)
    lane = lax.broadcasted_iota(jnp.int32, (128, 2 * UNITS), 1)
    wanted = jnp.where(lane < UNITS, own, other)
    pick = ((row % EXPERTS == wanted) & (row < 3 * EXPERTS)).astype(BF)

    payload = payload_of(moe_input, expert_ids, gate_weights)
    gate_own, up_own, down_own = expert_gate[0], expert_up[0], expert_down[0]
    column = joined(gather_stage([payload], ["y"])[0])
    column, gate_other, up_other = lax.optimization_barrier(
        (column, swap(gate_own), swap(up_own))
    )
    plane = gather_stage([column[:, :HALF], column[:, HALF:]], ["x", "z"])
    both = [joined(blocks) for blocks in plane]
    both, query_rows, down_own, pick, length = lax.optimization_barrier(
        (both, query_rows, down_own, pick, length)
    )
    down_other = swap(down_own)
    first = [move(part, axis, 1) for part, axis in zip(both, "zx")]
    second = [move(part, axis, -1) for part, axis in zip(both, "zx")]
    attn_out = attend(length, query_rows, cache_latent)
    *own_sums, held, down = own_part(
        both[0], both[1], (gate_own, gate_other, up_own, up_other), (down_own, down_other)
    )
    first, attn_out, own_sums = lax.optimization_barrier((first, attn_out, own_sums))
    third = [move(part, axis, 1) for part, axis in zip(first, "zx")]
    parts = [list(blocks) for blocks in zip(both, first, second, third)]

    made = sent_blocks(parts, own_sums, held, down, pick)
    sums = reduce_stage(made, ["z", "x"], True)
    sums = reduce_stage([quarters(part) for part in sums], ["x", "z"], True)
    moe_out = reduce_stage([quarters(jnp.concatenate(sums, axis=1))], ["y"], False)[0]
    return attn_out, moe_out


def solution(mesh):
    fine = Mesh(mesh.devices.reshape(4, 4, 2, 4), ("z", "x", "core", "y"))
    dp = ("z", "x", "core")
    both = ("z", "x", "core", "y")
    return jax.shard_map(
        per_device,
        mesh=fine,
        in_specs=(
            P(both, None, None),
            P(both, None),
            P(),
            P(both, None),
            P(both, None),
            P(both, None),
            P(dp, None, "y"),
            P(dp, None, "y"),
            P(dp, "y", None),
        ),
        out_specs=(P(both, None, None), P(both, None)),
        check_vma=False,
    )
```

time: 160 us -> 148 us (0.925)
  Pallas kernels: 34.2 us -> 24.7 us
  waiting for transfers between devices: 65 us -> 59.5 us
  local copies, waits for them, and re-layouts: 4.18 us -> 6.87 us
    pallas_call x4 -> x5, Pallas kernels: 31.6 us -> 20.9 us  [the longest x4 12.4 us: on_chip(): pl.pallas_call(kernel, in_specs=[spec] * len(operands), out_specs=[spec]...]
    ppermute x30, waiting for transfers between devices: 65 us -> 59.5 us  [move(): return lax.ppermute(array, names, pairs)]
    unnamed x6 -> x8, local copies, waits for them, and re-layouts: 2.35 us -> 4.38 us
  transfers between devices with their start and end apart: 33 -> 33, of which waited for: 17 -> 17; matrix products, arithmetic and copies ran while one was open for 3% -> 4% of each run, Pallas kernels for 19% -> 12%
where the time goes in v4:
time: 148 us; the launch traced here: 147 us
  waiting for transfers between devices  59.5 us (40%)
  starting transfers between devices  50.6 us (34%)
  Pallas kernels  24.7 us (17%)
  local copies, waits for them, and re-layouts  6.87 us (5%)
  other arithmetic  4.19 us (3%)
    ppermute x30, waiting for transfers between devices, move(): return lax.ppermute(array, names, pairs)  59.5 us
    ppermute x30, starting transfers between devices, move(): return lax.ppermute(array, names, pairs)  49.9 us
    pallas_call x4, Pallas kernels, on_chip(): pl.pallas_call(kernel, in_specs=[spec] * len(operands), out_specs=[spec]...  12.4 us
    pallas_call x1, Pallas kernels, own_part(): pl.pallas_call(own_kernel, grid=(STEPS,), in_specs=[block] * 2 + [first]...  8.51 us
    unnamed x8, local copies, waits for them, and re-layouts  4.38 us
    pallas_call x1, Pallas kernels, attend(): pl.pallas_call(attend_kernel, grid_spec=pltpu.PrefetchScalarGridSpec(num_...  3.85 us
  transfers between devices with their start and end apart: 33, of which 17 were waited for; matrix products, arithmetic and copies ran while one was open for 4% of the time, Pallas kernels for 12%

profile of v4, /device:TPU:6, one launch (start us, length us, event | category | flops | bytes accessed | tf_op | source)
XLA Modules:
  0.0 146.8 jit_solution(13487890148834137686)
XLA Ops:
  9.4 4.2 %collective-permute-done.2 = bf16[8,7296]{1,0:T(8,128)(2,1)S(1)} collective-permute-done((bf16[8,7296]{1,0:T(8,128)(2,1)S(1)}, bf16[8,7296]{1,0:T(8,128)(2,1)S(1)}, u32[]{:S(2)}, u32[]{:S(2)}) %collective-permute-start.2) | collective-permute-done | bytes 116768 | tf_op jit(solution)/shard_map/ppermute | solution.py:252
  18.7 4.0 %collective-permute-start.10 = (bf16[32,3712]{1,0:T(8,128)(2,1)S(1)}, bf16[32,3712]{1,0:T(8,128)(2,1)S(1)}, u32[]{:S(2)}, u32[]{:S(2)}) collective-permute-start(bf16[32,3712]{1,0:T(8,128)(2,1)S(1)} %slice.7), channel_id=1, source_target_pairs={{0,64},{32,96},{64,0},{96,32},{4,68},{36,100},{68,4},{100,36},{1,6... | collective-permute-start | bytes 712712 | tf_op jit(solution)/shard_map/ppermute | solution.py:252
  23.6 2.6 %collective-permute-start.9 = (bf16[32,3712]{1,0:T(8,128)(2,1)S(1)}, bf16[32,3712]{1,0:T(8,128)(2,1)S(1)}, u32[]{:S(2)}, u32[]{:S(2)}) collective-permute-start(bf16[32,3712]{1,0:T(8,128)(2,1)S(1)} %slice.7), channel_id=1, source_target_pairs={{0,96},{32,0},{64,32},{96,64},{4,36},{36,68},{68,100},{100,4},{1,9... | collective-permute-start | bytes 712712 | tf_op jit(solution)/shard_map/ppermute | solution.py:252
  28.9 3.8 %collective-permute-done.8 = bf16[32,3712]{1,0:T(8,128)(2,1)S(1)} collective-permute-done((bf16[32,3712]{1,0:T(8,128)(2,1)S(1)}, bf16[32,3712]{1,0:T(8,128)(2,1)S(1)}, u32[]{:S(2)}, u32[]{:S(2)}) %collective-permute-start.8) | collective-permute-done | bytes 237600 | tf_op jit(solution)/shard_map/ppermute | solution.py:252
  39.1 2.3 %copy-done.2 = bf16[4096,576]{0,1:T(8,128)(2,1)S(1)} copy-done((bf16[4096,576]{0,1:T(8,128)(2,1)S(1)}, bf16[4096,576]{0,1:T(8,128)(2,1)}, u32[]{:S(2)}) %copy-start.2) | copy-done | bytes 4718616
  41.5 3.8 %attend.1 = bf16[1,128,512]{2,1,0:T(8,128)(2,1)} custom-call(s32[1]{0:T(128)} %dynamic_slice.3.length_ref, bf16[1,128,576]{2,1,0:T(8,128)(2,1)S(1)} %copy.13.query_ref, bf16[576,4096]{1,0:T(8,128)(2,1)S(1)} %bitcast.10), custom_call_target="tpu_custom_call" | custom-call | flops 1140850688 | bytes 4718592 | tf_op jit(solution)/shard_map/attend/pallas_call | solution.py:74
  47.4 8.5 %own.1 = (f32[128,1024]{1,0:T(8,128)S(1)}, f32[128,1024]{1,0:T(8,128)S(1)}, bf16[7168,1024]{1,0:T(8,128)(2,1)S(1)}, bf16[512,7168]{1,0:T(8,128)(2,1)S(1)}) custom-call(bf16[128,3584]{1,0:T(8,128)(2,1)} %pad_maximum_fusion.1.refs_0_, bf16[128,3712]{1,0:T(8,128)(2,1)S(1)} %pad_maximum_fusion.refs_1_.b0, bf16[7168,256]{1,0:T(8,128)(2,1)S(1)} %bitcast.5, ...), custom_call_target="tpu_custom_call" | custom-call | flops 1879048192 | bytes 23855104 | tf_op jit(solution)/shard_map/own/pallas_call | solution.py:129
  58.0 2.7 %collective-permute-start.16 = (bf16[128,3712]{1,0:T(8,128)(2,1)S(1)}, bf16[128,3712]{1,0:T(8,128)(2,1)S(1)}, u32[]{:S(2)}, u32[]{:S(2)}) collective-permute-start(bf16[128,3712]{1,0:T(8,128)(2,1)S(1)} %collective-permute-done.12.b1), channel_id=1, source_target_pairs={{0,8},{8,16},{16,24},{24,0},{4,28},{12,4},{20,12},{28,20},{1,9},{9... | collective-permute-start | bytes 2850824 | tf_op jit(solution)/shard_map/ppermute | solution.py:252
  61.3 5.4 %early.1 = (f32[256,1024]{1,0:T(8,128)S(1)}, f32[256,1024]{1,0:T(8,128)S(1)}, bf16[7168,1024]{1,0:T(8,128)(2,1)S(1)}) custom-call(bf16[128,3584]{1,0:T(8,128)(2,1)} %collective-permute-done.11.a1, bf16[128,3584]{1,0:T(8,128)(2,1)} %collective-permute-done.17.a2, bf16[128,3712]{1,0:T(8,128)(2,1)S(1)} %collective-permute-done.12.b1, ...), custom_call_target="tpu_custom_call", output_to_operand_aliasing={{2}: (4, {})} | custom-call | flops 3758096384 | tf_op jit(solution)/shard_map/early/pallas_call | solution.py:148
  66.7 8.8 %collective-permute-done.14.a3 = bf16[128,3584]{1,0:T(8,128)(2,1)S(1)} collective-permute-done((bf16[128,3584]{1,0:T(8,128)(2,1)}, bf16[128,3584]{1,0:T(8,128)(2,1)S(1)}, u32[]{:S(2)}, u32[]{:S(2)}) %collective-permute-start.14) | collective-permute-done | bytes 917536 | tf_op jit(solution)/shard_map/ppermute | solution.py:252
  75.5 2.3 %late.1 = (bf16[512,512]{1,0:T(8,128)(2,1)S(1)}, bf16[512,512]{1,0:T(8,128)(2,1)S(1)}) custom-call(bf16[128,3584]{1,0:T(8,128)(2,1)S(1)} %collective-permute-done.14.a3, bf16[128,3712]{1,0:T(8,128)(2,1)S(1)} %pad_maximum_fusion.refs_1_.b0, bf16[128,3712]{1,0:T(8,128)(2,1)S(1)} %collective-permute-done.12.b1, ...), custom_call_target="tpu_custom_call" | custom-call | flops 1879048192 | tf_op jit(solution)/shard_map/late/pallas_call | solution.py:148
  77.8 2.3 %down.2 = (bf16[128,3584]{1,0:T(8,128)(2,1)S(1)}, bf16[128,3584]{1,0:T(8,128)(2,1)S(1)}, bf16[128,3584]{1,0:T(8,128)(2,1)S(1)}, bf16[128,3584]{1,0:T(8,128)(2,1)S(1)}) custom-call(bf16[512,512]{1,0:T(8,128)(2,1)S(1)} %get-tuple-element.58.hidden, bf16[512,7168]{1,0:T(8,128)(2,1)S(1)} %get-tuple-element.59.down), custom_call_target="tpu_custom_call" | custom-call | flops 1879048192 | tf_op jit(solution)/shard_map/down/pallas_call | solution.py:148
  80.2 2.3 %down.3 = (bf16[128,3584]{1,0:T(8,128)(2,1)S(1)}, bf16[128,3584]{1,0:T(8,128)(2,1)S(1)}, bf16[128,3584]{1,0:T(8,128)(2,1)S(1)}, bf16[128,3584]{1,0:T(8,128)(2,1)S(1)}) custom-call(bf16[512,512]{1,0:T(8,128)(2,1)S(1)} %get-tuple-element.69.hidden, bf16[512,7168]{1,0:T(8,128)(2,1)S(1)} %get-tuple-element.59.down), custom_call_target="tpu_custom_call" | custom-call | flops 1879048192 | tf_op jit(solution)/shard_map/down/pallas_call | solution.py:148
  82.6 3.2 %collective-permute-start.24 = (bf16[128,3584]{1,0:T(8,128)(2,1)S(1)}, bf16[128,3584]{1,0:T(8,128)(2,1)S(1)}, u32[]{:S(2)}, u32[]{:S(2)}) collective-permute-start(bf16[128,3584]{1,0:T(8,128)(2,1)S(1)} %get-tuple-element.71), channel_id=1, source_target_pairs={{0,8},{8,16},{16,24},{24,0},{4,28},{12,4},{20,12},{28,20},{1,9},{9... | collective-permute-start | bytes 2752520 | tf_op jit(solution)/shard_map/ppermute | solution.py:252
  87.9 14.8 %collective-permute-done.25 = bf16[128,3584]{1,0:T(8,128)(2,1)S(1)} collective-permute-done((bf16[128,3584]{1,0:T(8,128)(2,1)S(1)}, bf16[128,3584]{1,0:T(8,128)(2,1)S(1)}, u32[]{:S(2)}, u32[]{:S(2)}) %collective-permute-start.25) | collective-permute-done | bytes 917536 | tf_op jit(solution)/shard_map/ppermute | solution.py:252
  103.9 3.8 %collective-permute-start.20 = (bf16[128,3584]{1,0:T(8,128)(2,1)S(1)}, bf16[128,3584]{1,0:T(8,128)(2,1)S(1)}, u32[]{:S(2)}, u32[]{:S(2)}) collective-permute-start(bf16[128,3584]{1,0:T(8,128)(2,1)S(1)} %add_convert_fusion.3), channel_id=1, source_target_pairs={{0,96},{32,0},{64,32},{96,64},{4,36},{36,68},{68,100},{100,4},{1,9... | collective-permute-start | bytes 2752520 | tf_op jit(solution)/shard_map/ppermute | solution.py:252
  107.6 9.9 %collective-permute-done.26 = bf16[128,3584]{1,0:T(8,128)(2,1)S(1)} collective-permute-done((bf16[128,3584]{1,0:T(8,128)(2,1)S(1)}, bf16[128,3584]{1,0:T(8,128)(2,1)S(1)}, u32[]{:S(2)}, u32[]{:S(2)}) %collective-permute-start.26) | collective-permute-done | bytes 917536 | tf_op jit(solution)/shard_map/ppermute | solution.py:252
  117.9 3.4 %collective-permute-start.28 = (bf16[32,3584]{1,0:T(8,128)(2,1)S(1)}, bf16[32,3584]{1,0:T(8,128)(2,1)S(1)}, u32[]{:S(2)}, u32[]{:S(2)}) collective-permute-start(bf16[32,3584]{1,0:T(8,128)(2,1)S(1)} %get-tuple-element.77), channel_id=1, source_target_pairs={{0,96},{32,0},{64,32},{96,64},{4,36},{36,68},{68,100},{100,4},{1,9... | collective-permute-start | bytes 688136 | tf_op jit(solution)/shard_map/ppermute | solution.py:252
  121.8 3.2 %collective-permute-start.21 = (bf16[32,3584]{1,0:T(8,128)(2,1)S(1)}, bf16[32,3584]{1,0:T(8,128)(2,1)S(1)}, u32[]{:S(2)}, u32[]{:S(2)}) collective-permute-start(bf16[32,3584]{1,0:T(8,128)(2,1)S(1)} %get-tuple-element.74), channel_id=1, source_target_pairs={{0,8},{8,16},{16,24},{24,0},{4,28},{12,4},{20,12},{28,20},{1,9},{9... | collective-permute-start | bytes 688136 | tf_op jit(solution)/shard_map/ppermute | solution.py:252
  125.1 3.6 %collective-permute-start.29 = (bf16[32,3584]{1,0:T(8,128)(2,1)S(1)}, bf16[32,3584]{1,0:T(8,128)(2,1)S(1)}, u32[]{:S(2)}, u32[]{:S(2)}) collective-permute-start(bf16[32,3584]{1,0:T(8,128)(2,1)S(1)} %add_convert_fusion.5), channel_id=1, source_target_pairs={{0,96},{32,0},{64,32},{96,64},{4,36},{36,68},{68,100},{100,4},{1,9... | collective-permute-start | bytes 688136 | tf_op jit(solution)/shard_map/ppermute | solution.py:252
  129.1 3.1 %collective-permute-done.29 = bf16[32,3584]{1,0:T(8,128)(2,1)S(1)} collective-permute-done((bf16[32,3584]{1,0:T(8,128)(2,1)S(1)}, bf16[32,3584]{1,0:T(8,128)(2,1)S(1)}, u32[]{:S(2)}, u32[]{:S(2)}) %collective-permute-start.29) | collective-permute-done | bytes 229408 | tf_op jit(solution)/shard_map/ppermute | solution.py:252
  132.3 4.1 %collective-permute-done.23 = bf16[32,3584]{1,0:T(8,128)(2,1)S(1)} collective-permute-done((bf16[32,3584]{1,0:T(8,128)(2,1)S(1)}, bf16[32,3584]{1,0:T(8,128)(2,1)S(1)}, u32[]{:S(2)}, u32[]{:S(2)}) %collective-permute-start.23) | collective-permute-done | bytes 229408 | tf_op jit(solution)/shard_map/ppermute | solution.py:252
  137.5 2.3 %collective-permute-start.31 = (bf16[8,7168]{1,0:T(8,128)(2,1)S(1)}, bf16[8,7168]{1,0:T(8,128)(2,1)S(1)}, u32[]{:S(2)}, u32[]{:S(2)}) collective-permute-start(bf16[8,7168]{1,0:T(8,128)(2,1)S(1)} %get-tuple-element.80), channel_id=1, source_target_pairs={{0,3},{1,0},{2,1},{3,2},{4,5},{5,6},{6,7},{7,4},{8,11},{9,8},{10,9... | collective-permute-start | bytes 344072 | tf_op jit(solution)/shard_map/ppermute | solution.py:252
  142.5 3.5 %collective-permute-done.32 = bf16[8,7168]{1,0:T(8,128)(2,1)S(1)} collective-permute-done((bf16[8,7168]{1,0:T(8,128)(2,1)S(1)}, bf16[8,7168]{1,0:T(8,128)(2,1)S(1)}, u32[]{:S(2)}, u32[]{:S(2)}) %collective-permute-start.32) | collective-permute-done | bytes 114720 | tf_op jit(solution)/shard_map/ppermute | solution.py:252
  (83 shorter events, 37.8 us)
Async XLA Ops:
  0.6 13.1 %collective-permute-start.3 = (bf16[7168,256]{1,0:T(8,128)(2,1)}, bf16[7168,256]{1,0:T(8,128)(2,1)}, u32[]{:S(2)}, u32[]{:S(2)}) collective-permute-start(bf16[7168,256]{1,0:T(8,128)(2,1)} %bitcast.4), channel_id=1, source_target_pairs={{0,4},{4,0},{1,5},{5,1},{2,6},{6,2},{3,7},{7,3},{8,12},{12,8},{9,1... | collective-permute-start | bytes 11010056 | tf_op jit(solution)/shard_map/ppermute | solution.py:238
  0.7 13.0 %collective-permute-start.4 = (bf16[7168,256]{1,0:T(8,128)(2,1)}, bf16[7168,256]{1,0:T(8,128)(2,1)}, u32[]{:S(2)}, u32[]{:S(2)}) collective-permute-start(bf16[7168,256]{1,0:T(8,128)(2,1)} %bitcast.7), channel_id=1, source_target_pairs={{0,4},{4,0},{1,5},{5,1},{2,6},{6,2},{3,7},{7,3},{8,12},{12,8},{9,1... | collective-permute-start | bytes 11010056 | tf_op jit(solution)/shard_map/ppermute | solution.py:238
  6.3 7.4 %collective-permute-start.2 = (bf16[8,7296]{1,0:T(8,128)(2,1)S(1)}, bf16[8,7296]{1,0:T(8,128)(2,1)S(1)}, u32[]{:S(2)}, u32[]{:S(2)}) collective-permute-start(bf16[8,7296]{1,0:T(8,128)(2,1)S(1)} %concatenate.18), channel_id=1, source_target_pairs={{0,2},{1,3},{2,0},{3,1},{4,6},{5,7},{6,4},{7,5},{8,10},{9,11},{10,... | collective-permute-start | bytes 350216 | tf_op jit(solution)/shard_map/ppermute | solution.py:252
  13.7 9.9 %collective-permute-start.5 = (bf16[32,3584]{1,0:T(8,128)(2,1)S(1)}, bf16[32,3584]{1,0:T(8,128)(2,1)S(1)}, u32[]{:S(2)}, u32[]{:S(2)}) collective-permute-start(bf16[32,3584]{1,0:T(8,128)(2,1)S(1)} %slice.6), channel_id=1, source_target_pairs={{0,8},{8,16},{16,24},{24,0},{4,28},{12,4},{20,12},{28,20},{1,9},{9... | collective-permute-start | bytes 688136 | tf_op jit(solution)/shard_map/ppermute | solution.py:252
  14.3 12.9 %collective-permute-start.6 = (bf16[32,3584]{1,0:T(8,128)(2,1)S(1)}, bf16[32,3584]{1,0:T(8,128)(2,1)S(1)}, u32[]{:S(2)}, u32[]{:S(2)}) collective-permute-start(bf16[32,3584]{1,0:T(8,128)(2,1)S(1)} %slice.6), channel_id=1, source_target_pairs={{0,24},{8,0},{16,8},{24,16},{4,12},{12,20},{20,28},{28,4},{1,25},{... | collective-permute-start | bytes 688136 | tf_op jit(solution)/shard_map/ppermute | solution.py:252
  15.8 11.4 %collective-permute-start.7 = (bf16[32,3584]{1,0:T(8,128)(2,1)S(1)}, bf16[32,3584]{1,0:T(8,128)(2,1)S(1)}, u32[]{:S(2)}, u32[]{:S(2)}) collective-permute-start(bf16[32,3584]{1,0:T(8,128)(2,1)S(1)} %slice.6), channel_id=1, source_target_pairs={{0,16},{8,24},{16,0},{24,8},{4,20},{12,28},{20,4},{28,12},{1,17},{... | collective-permute-start | bytes 688136 | tf_op jit(solution)/shard_map/ppermute | solution.py:252
  18.7 10.2 %collective-permute-start.10 = (bf16[32,3712]{1,0:T(8,128)(2,1)S(1)}, bf16[32,3712]{1,0:T(8,128)(2,1)S(1)}, u32[]{:S(2)}, u32[]{:S(2)}) collective-permute-start(bf16[32,3712]{1,0:T(8,128)(2,1)S(1)} %slice.7), channel_id=1, source_target_pairs={{0,64},{32,96},{64,0},{96,32},{4,68},{36,100},{68,4},{100,36},{1,6... | collective-permute-start | bytes 712712 | tf_op jit(solution)/shard_map/ppermute | solution.py:252
  22.6 10.1 %collective-permute-start.8 = (bf16[32,3712]{1,0:T(8,128)(2,1)S(1)}, bf16[32,3712]{1,0:T(8,128)(2,1)S(1)}, u32[]{:S(2)}, u32[]{:S(2)}) collective-permute-start(bf16[32,3712]{1,0:T(8,128)(2,1)S(1)} %slice.7), channel_id=1, source_target_pairs={{0,32},{32,64},{64,96},{96,0},{4,100},{36,4},{68,36},{100,68},{1,3... | collective-permute-start | bytes 712712 | tf_op jit(solution)/shard_map/ppermute | solution.py:252
  23.6 9.8 %collective-permute-start.9 = (bf16[32,3712]{1,0:T(8,128)(2,1)S(1)}, bf16[32,3712]{1,0:T(8,128)(2,1)S(1)}, u32[]{:S(2)}, u32[]{:S(2)}) collective-permute-start(bf16[32,3712]{1,0:T(8,128)(2,1)S(1)} %slice.7), channel_id=1, source_target_pairs={{0,96},{32,0},{64,32},{96,64},{4,36},{36,68},{68,100},{100,4},{1,9... | collective-permute-start | bytes 712712 | tf_op jit(solution)/shard_map/ppermute | solution.py:252
  33.5 11.8 %collective-permute-start.13 = (bf16[256,7168]{1,0:T(8,128)(2,1)}, bf16[256,7168]{1,0:T(8,128)(2,1)}, u32[]{:S(2)}, u32[]{:S(2)}) collective-permute-start(bf16[256,7168]{1,0:T(8,128)(2,1)} %bitcast.2.refs_10_), channel_id=1, source_target_pairs={{0,4},{4,0},{1,5},{5,1},{2,6},{6,2},{3,7},{7,3},{8,12},{12,8},{9,1... | collective-permute-start | bytes 11010056 | tf_op jit(solution)/shard_map/ppermute | solution.py:238
  33.6 24.3 %collective-permute-start.12 = (bf16[128,3712]{1,0:T(8,128)(2,1)S(1)}, bf16[128,3712]{1,0:T(8,128)(2,1)S(1)}, u32[]{:S(2)}, u32[]{:S(2)}) collective-permute-start(bf16[128,3712]{1,0:T(8,128)(2,1)S(1)} %pad_maximum_fusion.refs_1_.b0), channel_id=1, source_target_pairs={{0,8},{8,16},{16,24},{24,0},{4,28},{12,4},{20,12},{28,20},{1,9},{9... | collective-permute-start | bytes 2850824 | tf_op jit(solution)/shard_map/ppermute | solution.py:252
  35.7 22.2 %collective-permute-start.11 = (bf16[128,3584]{1,0:T(8,128)(2,1)}, bf16[128,3584]{1,0:T(8,128)(2,1)}, u32[]{:S(2)}, u32[]{:S(2)}) collective-permute-start(bf16[128,3584]{1,0:T(8,128)(2,1)} %pad_maximum_fusion.1.refs_0_), channel_id=1, source_target_pairs={{0,32},{32,64},{64,96},{96,0},{4,100},{36,4},{68,36},{100,68},{1,3... | collective-permute-start | bytes 2752520 | tf_op jit(solution)/shard_map/ppermute | solution.py:252
  36.7 24.6 %collective-permute-start.15 = (bf16[128,3712]{1,0:T(8,128)(2,1)S(1)}, bf16[128,3712]{1,0:T(8,128)(2,1)S(1)}, u32[]{:S(2)}, u32[]{:S(2)}) collective-permute-start(bf16[128,3712]{1,0:T(8,128)(2,1)S(1)} %pad_maximum_fusion.refs_1_.b0), channel_id=1, source_target_pairs={{0,24},{8,0},{16,8},{24,16},{4,12},{12,20},{20,28},{28,4},{1,25},{... | collective-permute-start | bytes 2850824 | tf_op jit(solution)/shard_map/ppermute | solution.py:252
  36.7 24.6 %collective-permute-start.17 = (bf16[128,3584]{1,0:T(8,128)(2,1)}, bf16[128,3584]{1,0:T(8,128)(2,1)}, u32[]{:S(2)}, u32[]{:S(2)}) collective-permute-start(bf16[128,3584]{1,0:T(8,128)(2,1)} %pad_maximum_fusion.1.refs_0_), channel_id=1, source_target_pairs={{0,96},{32,0},{64,32},{96,64},{4,36},{36,68},{68,100},{100,4},{1,9... | collective-permute-start | bytes 2752520 | tf_op jit(solution)/shard_map/ppermute | solution.py:252
  58.0 17.6 %collective-permute-start.16 = (bf16[128,3712]{1,0:T(8,128)(2,1)S(1)}, bf16[128,3712]{1,0:T(8,128)(2,1)S(1)}, u32[]{:S(2)}, u32[]{:S(2)}) collective-permute-start(bf16[128,3712]{1,0:T(8,128)(2,1)S(1)} %collective-permute-done.12.b1), channel_id=1, source_target_pairs={{0,8},{8,16},{16,24},{24,0},{4,28},{12,4},{20,12},{28,20},{1,9},{9... | collective-permute-start | bytes 2850824 | tf_op jit(solution)/shard_map/ppermute | solution.py:252
  60.7 14.8 %collective-permute-start.14 = (bf16[128,3584]{1,0:T(8,128)(2,1)}, bf16[128,3584]{1,0:T(8,128)(2,1)S(1)}, u32[]{:S(2)}, u32[]{:S(2)}) collective-permute-start(bf16[128,3584]{1,0:T(8,128)(2,1)} %collective-permute-done.11.a1), channel_id=1, source_target_pairs={{0,32},{32,64},{64,96},{96,0},{4,100},{36,4},{68,36},{100,68},{1,3... | collective-permute-start | bytes 2752520 | tf_op jit(solution)/shard_map/ppermute | solution.py:252
  82.5 20.2 %collective-permute-start.25 = (bf16[128,3584]{1,0:T(8,128)(2,1)S(1)}, bf16[128,3584]{1,0:T(8,128)(2,1)S(1)}, u32[]{:S(2)}, u32[]{:S(2)}) collective-permute-start(bf16[128,3584]{1,0:T(8,128)(2,1)S(1)} %get-tuple-element.73), channel_id=1, source_target_pairs={{0,24},{8,0},{16,8},{24,16},{4,12},{12,20},{20,28},{28,4},{1,25},{... | collective-permute-start | bytes 2752520 | tf_op jit(solution)/shard_map/ppermute | solution.py:252
  82.6 25.0 %collective-permute-start.24 = (bf16[128,3584]{1,0:T(8,128)(2,1)S(1)}, bf16[128,3584]{1,0:T(8,128)(2,1)S(1)}, u32[]{:S(2)}, u32[]{:S(2)}) collective-permute-start(bf16[128,3584]{1,0:T(8,128)(2,1)S(1)} %get-tuple-element.71), channel_id=1, source_target_pairs={{0,8},{8,16},{16,24},{24,0},{4,28},{12,4},{20,12},{28,20},{1,9},{9... | collective-permute-start | bytes 2752520 | tf_op jit(solution)/shard_map/ppermute | solution.py:252
  85.8 17.8 %collective-permute-start.19 = (bf16[128,3584]{1,0:T(8,128)(2,1)S(1)}, bf16[128,3584]{1,0:T(8,128)(2,1)S(1)}, u32[]{:S(2)}, u32[]{:S(2)}) collective-permute-start(bf16[128,3584]{1,0:T(8,128)(2,1)S(1)} %get-tuple-element.68), channel_id=1, source_target_pairs={{0,96},{32,0},{64,32},{96,64},{4,36},{36,68},{68,100},{100,4},{1,9... | collective-permute-start | bytes 2752520 | tf_op jit(solution)/shard_map/ppermute | solution.py:252
  86.9 34.4 %collective-permute-start.18 = (bf16[128,3584]{1,0:T(8,128)(2,1)S(1)}, bf16[128,3584]{1,0:T(8,128)(2,1)S(1)}, u32[]{:S(2)}, u32[]{:S(2)}) collective-permute-start(bf16[128,3584]{1,0:T(8,128)(2,1)S(1)} %get-tuple-element.66), channel_id=1, source_target_pairs={{0,32},{32,64},{64,96},{96,0},{4,100},{36,4},{68,36},{100,68},{1,3... | collective-permute-start | bytes 2752520 | tf_op jit(solution)/shard_map/ppermute | solution.py:252
  102.9 14.7 %collective-permute-start.26 = (bf16[128,3584]{1,0:T(8,128)(2,1)S(1)}, bf16[128,3584]{1,0:T(8,128)(2,1)S(1)}, u32[]{:S(2)}, u32[]{:S(2)}) collective-permute-start(bf16[128,3584]{1,0:T(8,128)(2,1)S(1)} %add_convert_fusion.1), channel_id=1, source_target_pairs={{0,24},{8,0},{16,8},{24,16},{4,12},{12,20},{20,28},{28,4},{1,25},{... | collective-permute-start | bytes 2752520 | tf_op jit(solution)/shard_map/ppermute | solution.py:252
  103.9 17.4 %collective-permute-start.20 = (bf16[128,3584]{1,0:T(8,128)(2,1)S(1)}, bf16[128,3584]{1,0:T(8,128)(2,1)S(1)}, u32[]{:S(2)}, u32[]{:S(2)}) collective-permute-start(bf16[128,3584]{1,0:T(8,128)(2,1)S(1)} %add_convert_fusion.3), channel_id=1, source_target_pairs={{0,96},{32,0},{64,32},{96,64},{4,36},{36,68},{68,100},{100,4},{1,9... | collective-permute-start | bytes 2752520 | tf_op jit(solution)/shard_map/ppermute | solution.py:252
  121.3 7.8 %collective-permute-start.27 = (bf16[32,3584]{1,0:T(8,128)(2,1)S(1)}, bf16[32,3584]{1,0:T(8,128)(2,1)S(1)}, u32[]{:S(2)}, u32[]{:S(2)}) collective-permute-start(bf16[32,3584]{1,0:T(8,128)(2,1)S(1)} %get-tuple-element.76), channel_id=1, source_target_pairs={{0,32},{32,64},{64,96},{96,0},{4,100},{36,4},{68,36},{100,68},{1,3... | collective-permute-start | bytes 688136 | tf_op jit(solution)/shard_map/ppermute | solution.py:252
  121.8 10.5 %collective-permute-start.21 = (bf16[32,3584]{1,0:T(8,128)(2,1)S(1)}, bf16[32,3584]{1,0:T(8,128)(2,1)S(1)}, u32[]{:S(2)}, u32[]{:S(2)}) collective-permute-start(bf16[32,3584]{1,0:T(8,128)(2,1)S(1)} %get-tuple-element.74), channel_id=1, source_target_pairs={{0,8},{8,16},{16,24},{24,0},{4,28},{12,4},{20,12},{28,20},{1,9},{9... | collective-permute-start | bytes 688136 | tf_op jit(solution)/shard_map/ppermute | solution.py:252
  (13 other events, 85.6 us)

commit v5 on v4

--- a/solution.py
+++ b/solution.py
@@ -23,8 +23,8 @@
 ATT_ROWS = 1024
 HALF = WIDTH // 2
 K_STEP = 512
-RETURN = (3584, 3584)
-N_TILE = 896
+RETURN = (3328, 3840)
+N_TILE = 1024
 VMEM_LIMIT = 8 * 2**20
 STEPS = HALF // K_STEP
 D_STEP = WIDTH // STEPS
@@ -48,7 +48,7 @@
     def _():
         rows = cache_ref[...]
         scores = QK_SCALE * lax.dot_general(
-            query_ref[0], rows, (((1,), (0,)), ((), ())), preferred_element_type=F32
+            query_ref[0], rows, (((0,), (0,)), ((), ())), preferred_element_type=F32
         )
         place = step * ATT_ROWS + lax.broadcasted_iota(jnp.int32, scores.shape, 1)
         scores = jnp.where(place < length, scores, FAR_LOW)
@@ -77,7 +77,7 @@
             num_scalar_prefetch=1,
             grid=(CTX // ATT_ROWS,),
             in_specs=[
-                pl.BlockSpec((1, HEADS, KEY_DIM), lambda step, length_ref: (0, 0, 0)),
+                pl.BlockSpec((1, KEY_DIM, HEADS), lambda step, length_ref: (0, 0, 0)),
                 pl.BlockSpec((KEY_DIM, ATT_ROWS), cache_block),
             ],
             out_specs=pl.BlockSpec((1, HEADS, LATENT), lambda step, length_ref: (0, 0, 0)),
@@ -91,16 +91,16 @@
         compiler_params=pltpu.CompilerParams(vmem_limit_bytes=VMEM_LIMIT),
         cost_estimate=pl.CostEstimate(
             flops=2 * HEADS * CTX * (KEY_DIM + LATENT),
-            bytes_accessed=CTX * KEY_DIM * 2,
+            bytes_accessed=4 * CTX * KEY_DIM * 2,
             transcendentals=HEADS * CTX,
         ),
         name="attend",
-    )(length, query_rows, cache_latent.T)
+    )(length, jnp.swapaxes(query_rows, 1, 2), cache_latent.T)
 
 
 def own_kernel(*refs):
-    a_ref, b_ref, weights_a, weights_b, d_own, d_other = *refs[:2], refs[2:6], refs[6:10], *refs[10:12]
-    out_a, out_b, held, down = refs[12:]
+    a_ref, b_ref, weights_a, weights_b = refs[0], refs[1], refs[2:6], refs[6:10]
+    out_a, out_b, held = refs[10:]
     step = pl.program_id(0)
 
     @pl.when(step == 0)
@@ -115,32 +115,50 @@
             value = weight[...]
             held[rows, lanes] = value
             out[:, lanes] += jnp.dot(block[...], value, preferred_element_type=F32)
+
+
+def keep_kernel(d_own, d_other, down):
+    step = pl.program_id(0)
     columns = pl.ds(pl.multiple_of(step * D_STEP, D_STEP), D_STEP)
     down[:UNITS, columns] = d_own[...]
     down[UNITS:, columns] = d_other[...]
 
 
-def own_part(a_block, b_block, weights, downs):
+def keep(downs):
+    return pl.pallas_call(
+        keep_kernel,
+        grid=(STEPS,),
+        in_specs=[pl.BlockSpec((UNITS, D_STEP), lambda step: (0, step))] * 2,
+        out_specs=pl.BlockSpec(memory_space=pltpu.VMEM),
+        out_shape=pltpu.VMEM((2 * UNITS, WIDTH), BF),
+        compiler_params=pltpu.CompilerParams(vmem_limit_bytes=VMEM_LIMIT),
+        cost_estimate=pl.CostEstimate(
+            flops=0, bytes_accessed=2 * 2 * UNITS * WIDTH, transcendentals=0
+        ),
+        name="keep",
+    )(*downs)
+
+
+def own_part(a_block, b_block, weights):
     block = pl.BlockSpec((PART, K_STEP), lambda step: (0, step))
     first = pl.BlockSpec((K_STEP, UNITS), lambda step: (step, 0))
     second = pl.BlockSpec((K_STEP, UNITS), lambda step: (step + STEPS, 0))
-    down = pl.BlockSpec((UNITS, D_STEP), lambda step: (0, step))
     sums = pl.BlockSpec((PART, 4 * UNITS), lambda step: (0, 0))
     return pl.pallas_call(
         own_kernel,
         grid=(STEPS,),
-        in_specs=[block] * 2 + [first] * 4 + [second] * 4 + [down] * 2,
-        out_specs=[sums] * 2 + [pl.BlockSpec(memory_space=pltpu.VMEM)] * 2,
+        in_specs=[block] * 2 + [first] * 4 + [second] * 4,
+        out_specs=[sums] * 2 + [pl.BlockSpec(memory_space=pltpu.VMEM)],
         out_shape=[jax.ShapeDtypeStruct((PART, 4 * UNITS), F32)] * 2
-        + [pltpu.VMEM((WIDTH, 4 * UNITS), BF), pltpu.VMEM((2 * UNITS, WIDTH), BF)],
+        + [pltpu.VMEM((WIDTH, 4 * UNITS), BF)],
         compiler_params=pltpu.CompilerParams(vmem_limit_bytes=VMEM_LIMIT),
         cost_estimate=pl.CostEstimate(
             flops=2 * PART * WIDTH * 4 * UNITS,
-            bytes_accessed=2 * (PART + 6 * UNITS) * WIDTH,
+            bytes_accessed=2 * (PART + 4 * UNITS) * WIDTH,
             transcendentals=0,
         ),
         name="own",
-    )(a_block, b_block, *weights, *weights, *downs)
+    )(a_block, b_block, *weights, *weights)
 
 
 def on_chip(kernel, name, operands, shapes, flops, aliases=()):
@@ -151,40 +169,36 @@
         out_specs=[spec] * len(shapes),
         out_shape=[pltpu.VMEM(*shape) for shape in shapes],
         compiler_params=pltpu.CompilerParams(vmem_limit_bytes=VMEM_LIMIT),
-        cost_estimate=pl.CostEstimate(flops=flops, bytes_accessed=0, transcendentals=0),
+        cost_estimate=pl.CostEstimate(
+            flops=flops, bytes_accessed=0, transcendentals=0
+        ),
         input_output_aliases=dict(aliases),
         name=name,
     )(*operands)
 
 
-def early_kernel(a1, a2, b1, b2, held, out_a, out_b, _):
-    for blocks, out, start in (((a1, a2), out_a, 0), ((b1, b2), out_b, HALF)):
-        stacked = jnp.concatenate([block[:, :HALF] for block in blocks], axis=0)
-        out[...] = jnp.dot(stacked, held[start : start + HALF], preferred_element_type=F32)
-
-
-def send_blocks(hidden, down, low, outs):
-    width = outs[0].shape[1]
-    for start in range(0, width, N_TILE):
-        made = jnp.dot(
-            hidden[...], down[:, low + start : low + start + N_TILE], preferred_element_type=F32
-        ).astype(BF)
-        for place, out in enumerate(outs):
-            out[:, start : start + N_TILE] = made[place * PART : (place + 1) * PART]
-
-
-def late_kernel(a3, b0, b1, b2, b3, held, pick, own_a, own_b, early_a, early_b, out_a, out_b):
-    last_a = jnp.dot(a3[...], held[:HALF], preferred_element_type=F32)
-    last_b = jnp.dot(b3[:, :HALF], held[HALF:], preferred_element_type=F32)
+def half_sums(blocks, held, start):
+    stacked = jnp.concatenate([block[:, :HALF] for block in blocks], axis=0)
+    return jnp.dot(stacked, held[start : start + HALF], preferred_element_type=F32)
+
+
+def early_kernel(a1, b1, held, out_a, out_b, _):
+    out_a[...] = half_sums([a1], held, 0)
+    out_b[...] = half_sums([b1], held, HALF)
+
+
+def late_kernel(a2, a3, b0, b1, b2, b3, held, pick, own_a, own_b, early_a, early_b, out_a, out_b):
+    last_a = half_sums([a2, a3], held, 0)
+    last_b = half_sums([b2, b3], held, HALF)
 
     def group(own, early, last, outer, inner):
         low = inner * GROUP
         if outer == 0:
             return own[low : low + GROUP]
-        if outer == 3:
-            return last[low : low + GROUP]
-        low = low + (outer - 1) * PART
-        return early[low : low + GROUP]
+        if outer == 1:
+            return early[low : low + GROUP]
+        low = low + (outer - 2) * PART
+        return last[low : low + GROUP]
 
     for kx, tail in enumerate((b0, b1, b2, b3)):
         share = jnp.dot(tail[:, HALF:], pick[...], preferred_element_type=F32)
@@ -198,40 +212,58 @@
             out_b[low_b : low_b + GROUP, :] = made
 
 
-def down_kernel(low, hidden, down, *outs):
-    send_blocks(hidden, down, low, outs)
-
-
-def sent_blocks(parts, own_sums, held, down, pick):
-    a_blocks, b_blocks = parts
-    sums = ((2 * PART, 4 * UNITS), F32)
-    *early_sums, held = on_chip(
+def down_kernel(low, high, hidden_a, hidden_b, down, *outs):
+    count = high - low
+    for half, hidden in enumerate((hidden_a, hidden_b)):
+        for start in range(0, RETURN[half], N_TILE):
+            stop = min(start + N_TILE, RETURN[half])
+            column = half * RETURN[0]
+            made = jnp.dot(
+                hidden[low * PART : high * PART],
+                down[:, column + start : column + stop],
+                preferred_element_type=F32,
+            ).astype(BF)
+            for place in range(count):
+                block = made[place * PART : (place + 1) * PART]
+                outs[half * count + place][:, start:stop] = block
+
+
+def early_part(a_block, b_block, held):
+    sums = ((PART, 4 * UNITS), F32)
+    return on_chip(
         early_kernel,
         "early",
-        (*a_blocks[1:3], *b_blocks[1:3], held),
+        (a_block, b_block, held),
         (sums, sums, ((WIDTH, 4 * UNITS), BF)),
-        2 * 2 * PART * WIDTH * 4 * UNITS,
-        {4: 2},
-    )
+        2 * PART * WIDTH * 4 * UNITS,
+        {2: 2},
+    )
+
+
+def sent_blocks(parts, own_sums, early_sums, held, down, pick):
+    a_blocks, b_blocks = parts
     made = ((ROWS, 2 * UNITS), BF)
     halves = on_chip(
         late_kernel,
         "late",
-        (a_blocks[3], *b_blocks, held, pick, *own_sums, *early_sums),
+        (*a_blocks[2:], *b_blocks, held, pick, *own_sums, *early_sums),
         (made, made),
-        2 * PART * WIDTH * 4 * UNITS,
-    )
-    def half(place, hidden):
-        return on_chip(
-            functools.partial(down_kernel, place * RETURN[0]),
+        2 * 2 * PART * WIDTH * 4 * UNITS,
+    )
+    def some(low, high, hidden):
+        count = high - low
+        blocks = on_chip(
+            functools.partial(down_kernel, low, high),
             "down",
-            (hidden, down),
-            [((PART, RETURN[place]), BF)] * 4,
-            2 * ROWS * 2 * UNITS * RETURN[place],
+            (*hidden, down),
+            [((PART, width), BF) for width in RETURN for _ in range(count)],
+            2 * count * PART * 2 * UNITS * WIDTH,
         )
-
-    first, hidden = lax.optimization_barrier((half(0, halves[0]), halves[1]))
-    return [first, half(1, hidden)]
+        return blocks[:count], blocks[count:]
+
+    (far_a, far_b), halves = lax.optimization_barrier((some(3, 4, halves), halves))
+    rest_a, rest_b = some(0, 3, halves)
+    return [[*rest_a, *far_a], [*rest_b, *far_b]]
 
 
 def swap(array):
@@ -331,21 +363,25 @@
     )
     plane = gather_stage([column[:, :HALF], column[:, HALF:]], ["x", "z"])
     both = [joined(blocks) for blocks in plane]
-    both, query_rows, down_own, pick, length = lax.optimization_barrier(
-        (both, query_rows, down_own, pick, length)
+    both, down_own, pick, length, query_rows = lax.optimization_barrier(
+        (both, down_own, pick, length, query_rows)
     )
     down_other = swap(down_own)
     first = [move(part, axis, 1) for part, axis in zip(both, "zx")]
-    second = [move(part, axis, -1) for part, axis in zip(both, "zx")]
     attn_out = attend(length, query_rows, cache_latent)
-    *own_sums, held, down = own_part(
-        both[0], both[1], (gate_own, gate_other, up_own, up_other), (down_own, down_other)
-    )
-    first, attn_out, own_sums = lax.optimization_barrier((first, attn_out, own_sums))
+    later, attn_out = lax.optimization_barrier((both, attn_out))
+    second = [move(part, axis, -1) for part, axis in zip(later, "zx")]
     third = [move(part, axis, 1) for part, axis in zip(first, "zx")]
     parts = [list(blocks) for blocks in zip(both, first, second, third)]
-
-    made = sent_blocks(parts, own_sums, held, down, pick)
+    (a_own, b_own), (a_first, b_first), down_other = lax.optimization_barrier(
+        (both, first, down_other)
+    )
+    *own_sums, held = own_part(a_own, b_own, (gate_own, gate_other, up_own, up_other))
+    *early_sums, held = early_part(a_first, b_first, held)
+    down = keep((down_own, down_other))
+    early_sums, down = lax.optimization_barrier((early_sums, down))
+
+    made = sent_blocks(parts, own_sums, early_sums, held, down, pick)
     sums = reduce_stage(made, ["z", "x"], True)
     sums = reduce_stage([quarters(part) for part in sums], ["x", "z"], True)
     moe_out = reduce_stage([quarters(jnp.concatenate(sums, axis=1))], ["y"], False)[0]

time: 148 us -> 150 us (1.014)
  waiting for transfers between devices: 59.5 us -> 63.8 us
    ppermute x30, waiting for transfers between devices: 59.5 us -> 63.8 us  [move(): return lax.ppermute(array, names, pairs)]
    pallas_call x4, Pallas kernels: 12.4 us -> 10.3 us  [on_chip(): pl.pallas_call(kernel, in_specs=[spec] * len(operands), out_specs=[spec]...]
    unnamed x8 -> x10, local copies, waits for them, and re-layouts: 4.38 us -> 4.39 us
  transfers between devices with their start and end apart: 33 -> 33, of which waited for: 17 -> 21; matrix products, arithmetic and copies ran while one was open for 4% -> 3% of each run, Pallas kernels for 12% -> 12%
where the time goes in v5:
time: 150 us; the launch traced here: 148 us
  waiting for transfers between devices  63.8 us (43%)
  starting transfers between devices  50.3 us (34%)
  Pallas kernels  23.3 us (16%)
  local copies, waits for them, and re-layouts  6.72 us (4%)
  other arithmetic  3.22 us (2%)
    ppermute x30, waiting for transfers between devices, move(): return lax.ppermute(array, names, pairs)  63.8 us
    ppermute x30, starting transfers between devices, move(): return lax.ppermute(array, names, pairs)  49.6 us
    pallas_call x4, Pallas kernels, on_chip(): pl.pallas_call(kernel, in_specs=[spec] * len(operands), out_specs=[spec]...  10.3 us
    pallas_call x1, Pallas kernels, own_part(): pl.pallas_call(own_kernel, grid=(STEPS,), in_specs=[block] * 2 + [first]...  7.07 us
    pallas_call x1, Pallas kernels, attend(): pl.pallas_call(attend_kernel, grid_spec=pltpu.PrefetchScalarGridSpec(num_...  4.84 us
    unnamed x10, local copies, waits for them, and re-layouts  4.39 us
  transfers between devices with their start and end apart: 33, of which 21 were waited for; matrix products, arithmetic and copies ran while one was open for 3% of the time, Pallas kernels for 12%

profile of v5, /device:TPU:6, one launch (start us, length us, event | category | flops | bytes accessed | tf_op | source)
XLA Modules:
  0.0 148.3 jit_solution(12742276006018495527)
XLA Ops:
  9.4 4.2 %collective-permute-done.2 = bf16[8,7296]{1,0:T(8,128)(2,1)S(1)} collective-permute-done((bf16[8,7296]{1,0:T(8,128)(2,1)S(1)}, bf16[8,7296]{1,0:T(8,128)(2,1)S(1)}, u32[]{:S(2)}, u32[]{:S(2)}) %collective-permute-start.2) | collective-permute-done | bytes 116768 | tf_op jit(solution)/shard_map/ppermute | solution.py:284
  18.7 4.0 %collective-permute-start.10 = (bf16[32,3712]{1,0:T(8,128)(2,1)S(1)}, bf16[32,3712]{1,0:T(8,128)(2,1)S(1)}, u32[]{:S(2)}, u32[]{:S(2)}) collective-permute-start(bf16[32,3712]{1,0:T(8,128)(2,1)S(1)} %slice.7), channel_id=1, source_target_pairs={{0,64},{32,96},{64,0},{96,32},{4,68},{36,100},{68,4},{100,36},{1,6... | collective-permute-start | bytes 712712 | tf_op jit(solution)/shard_map/ppermute | solution.py:284
  23.7 2.6 %collective-permute-start.9 = (bf16[32,3712]{1,0:T(8,128)(2,1)S(1)}, bf16[32,3712]{1,0:T(8,128)(2,1)S(1)}, u32[]{:S(2)}, u32[]{:S(2)}) collective-permute-start(bf16[32,3712]{1,0:T(8,128)(2,1)S(1)} %slice.7), channel_id=1, source_target_pairs={{0,96},{32,0},{64,32},{96,64},{4,36},{36,68},{68,100},{100,4},{1,9... | collective-permute-start | bytes 712712 | tf_op jit(solution)/shard_map/ppermute | solution.py:284
  28.9 3.8 %collective-permute-done.8 = bf16[32,3712]{1,0:T(8,128)(2,1)S(1)} collective-permute-done((bf16[32,3712]{1,0:T(8,128)(2,1)S(1)}, bf16[32,3712]{1,0:T(8,128)(2,1)S(1)}, u32[]{:S(2)}, u32[]{:S(2)}) %collective-permute-start.8) | collective-permute-done | bytes 237600 | tf_op jit(solution)/shard_map/ppermute | solution.py:284
  33.7 2.1 %collective-permute-start.14 = (bf16[128,3712]{1,0:T(8,128)(2,1)S(1)}, bf16[128,3712]{1,0:T(8,128)(2,1)S(1)}, u32[]{:S(2)}, u32[]{:S(2)}) collective-permute-start(bf16[128,3712]{1,0:T(8,128)(2,1)S(1)} %pad_maximum_fusion.refs_1_.b0), channel_id=1, source_target_pairs={{0,8},{8,16},{16,24},{24,0},{4,28},{12,4},{20,12},{28,20},{1,9},{9... | collective-permute-start | bytes 2850824 | tf_op jit(solution)/shard_map/ppermute | solution.py:284
  36.8 2.3 %copy-done.2 = bf16[4096,576]{0,1:T(8,128)(2,1)S(1)} copy-done((bf16[4096,576]{0,1:T(8,128)(2,1)S(1)}, bf16[4096,576]{0,1:T(8,128)(2,1)}, u32[]{:S(2)}) %copy-start.2) | copy-done | bytes 4718616
  39.1 4.8 %attend.1 = bf16[1,128,512]{2,1,0:T(8,128)(2,1)} custom-call(s32[1]{0:T(128)} %dynamic_slice.3.length_ref, bf16[1,576,128]{2,1,0:T(8,128)(2,1)S(1)} %bitcast.14, bf16[576,4096]{1,0:T(8,128)(2,1)S(1)} %bitcast.11), custom_call_target="tpu_custom_call" | custom-call | flops 1140850688 | bytes 18874368 | tf_op jit(solution)/shard_map/attend/pallas_call | solution.py:74
  43.9 5.7 %collective-permute-done.14.b1 = bf16[128,3712]{1,0:T(8,128)(2,1)S(1)} collective-permute-done((bf16[128,3712]{1,0:T(8,128)(2,1)S(1)}, bf16[128,3712]{1,0:T(8,128)(2,1)S(1)}, u32[]{:S(2)}, u32[]{:S(2)}) %collective-permute-start.14) | collective-permute-done | bytes 950304 | tf_op jit(solution)/shard_map/ppermute | solution.py:284
  50.7 7.1 %collective-permute-start.11 = (bf16[128,3584]{1,0:T(8,128)(2,1)S(1)}, bf16[128,3584]{1,0:T(8,128)(2,1)S(1)}, u32[]{:S(2)}, u32[]{:S(2)}) collective-permute-start(bf16[128,3584]{1,0:T(8,128)(2,1)S(1)} %pad_maximum_fusion.1.refs_0_), channel_id=1, source_target_pairs={{0,96},{32,0},{64,32},{96,64},{4,36},{36,68},{68,100},{100,4},{1,9... | collective-permute-start | bytes 2752520 | tf_op jit(solution)/shard_map/ppermute | solution.py:284
  61.0 7.1 %own.1 = (f32[128,1024]{1,0:T(8,128)S(1)}, f32[128,1024]{1,0:T(8,128)S(1)}, bf16[7168,1024]{1,0:T(8,128)(2,1)S(1)}) custom-call(bf16[128,3584]{1,0:T(8,128)(2,1)S(1)} %pad_maximum_fusion.1.refs_0_, bf16[128,3712]{1,0:T(8,128)(2,1)S(1)} %pad_maximum_fusion.refs_1_.b0, bf16[7168,256]{1,0:T(8,128)(2,1)S(1)} %bitcast.6, ...), custom_call_target="tpu_custom_call" | custom-call | flops 1879048192 | bytes 16515072 | tf_op jit(solution)/shard_map/own/pallas_call | solution.py:147
  70.2 3.4 %collective-permute-done.11.a2 = bf16[128,3584]{1,0:T(8,128)(2,1)S(1)} collective-permute-done((bf16[128,3584]{1,0:T(8,128)(2,1)S(1)}, bf16[128,3584]{1,0:T(8,128)(2,1)S(1)}, u32[]{:S(2)}, u32[]{:S(2)}) %collective-permute-start.11) | collective-permute-done | bytes 917536 | tf_op jit(solution)/shard_map/ppermute | solution.py:284
  73.6 4.1 %late.1 = (bf16[512,512]{1,0:T(8,128)(2,1)S(1)}, bf16[512,512]{1,0:T(8,128)(2,1)S(1)}) custom-call(bf16[128,3584]{1,0:T(8,128)(2,1)S(1)} %collective-permute-done.11.a2, bf16[128,3584]{1,0:T(8,128)(2,1)S(1)} %collective-permute-done.13.a3, bf16[128,3712]{1,0:T(8,128)(2,1)S(1)} %pad_maximum_fusion.refs_1_.b0, ...), custom_call_target="tpu_custom_call" | custom-call | flops 3758096384 | tf_op jit(solution)/shard_map/late/pallas_call | solution.py:166
  78.9 2.8 %collective-permute-start.19 = (bf16[128,3328]{1,0:T(8,128)(2,1)S(1)}, bf16[128,3328]{1,0:T(8,128)(2,1)S(1)}, u32[]{:S(2)}, u32[]{:S(2)}) collective-permute-start(bf16[128,3328]{1,0:T(8,128)(2,1)S(1)} %get-tuple-element.77), channel_id=1, source_target_pairs={{0,96},{32,0},{64,32},{96,64},{4,36},{36,68},{68,100},{100,4},{1,9... | collective-permute-start | bytes 2555912 | tf_op jit(solution)/shard_map/ppermute | solution.py:284
  81.7 2.5 %collective-permute-start.25 = (bf16[128,3840]{1,0:T(8,128)(2,1)S(1)}, bf16[128,3840]{1,0:T(8,128)(2,1)S(1)}, u32[]{:S(2)}, u32[]{:S(2)}) collective-permute-start(bf16[128,3840]{1,0:T(8,128)(2,1)S(1)} %get-tuple-element.81), channel_id=1, source_target_pairs={{0,24},{8,0},{16,8},{24,16},{4,12},{12,20},{20,28},{28,4},{1,25},{... | collective-permute-start | bytes 2949128 | tf_op jit(solution)/shard_map/ppermute | solution.py:284
  84.2 3.0 %down.3 = (bf16[128,3328]{1,0:T(8,128)(2,1)S(1)}, bf16[128,3328]{1,0:T(8,128)(2,1)S(1)}, bf16[128,3328]{1,0:T(8,128)(2,1)S(1)}, bf16[128,3840]{1,0:T(8,128)(2,1)...) custom-call(bf16[512,512]{1,0:T(8,128)(2,1)S(1)} %get-tuple-element.72.hidden_a, ...), custom_call_target="tpu_custom_call" | custom-call | flops 2818572288 | tf_op jit(solution)/shard_map/down/pallas_call | solution.py:166
  88.1 12.4 %collective-permute-done.19 = bf16[128,3328]{1,0:T(8,128)(2,1)S(1)} collective-permute-done((bf16[128,3328]{1,0:T(8,128)(2,1)S(1)}, bf16[128,3328]{1,0:T(8,128)(2,1)S(1)}, u32[]{:S(2)}, u32[]{:S(2)}) %collective-permute-start.19) | collective-permute-done | bytes 852000 | tf_op jit(solution)/shard_map/ppermute | solution.py:284
  100.7 3.8 %collective-permute-start.20 = (bf16[128,3328]{1,0:T(8,128)(2,1)S(1)}, bf16[128,3328]{1,0:T(8,128)(2,1)S(1)}, u32[]{:S(2)}, u32[]{:S(2)}) collective-permute-start(bf16[128,3328]{1,0:T(8,128)(2,1)S(1)} %add_convert_fusion.3), channel_id=1, source_target_pairs={{0,96},{32,0},{64,32},{96,64},{4,36},{36,68},{68,100},{100,4},{1,9... | collective-permute-start | bytes 2555912 | tf_op jit(solution)/shard_map/ppermute | solution.py:284
  104.4 2.4 %collective-permute-done.25 = bf16[128,3840]{1,0:T(8,128)(2,1)S(1)} collective-permute-done((bf16[128,3840]{1,0:T(8,128)(2,1)S(1)}, bf16[128,3840]{1,0:T(8,128)(2,1)S(1)}, u32[]{:S(2)}, u32[]{:S(2)}) %collective-permute-start.25) | collective-permute-done | bytes 983072 | tf_op jit(solution)/shard_map/ppermute | solution.py:284
  109.5 5.1 %collective-permute-done.20 = bf16[128,3328]{1,0:T(8,128)(2,1)S(1)} collective-permute-done((bf16[128,3328]{1,0:T(8,128)(2,1)S(1)}, bf16[128,3328]{1,0:T(8,128)(2,1)S(1)}, u32[]{:S(2)}, u32[]{:S(2)}) %collective-permute-start.20) | collective-permute-done | bytes 852000 | tf_op jit(solution)/shard_map/ppermute | solution.py:284
  118.3 6.6 %collective-permute-done.26 = bf16[128,3840]{1,0:T(8,128)(2,1)S(1)} collective-permute-done((bf16[128,3840]{1,0:T(8,128)(2,1)S(1)}, bf16[128,3840]{1,0:T(8,128)(2,1)S(1)}, u32[]{:S(2)}, u32[]{:S(2)}) %collective-permute-start.26) | collective-permute-done | bytes 983072 | tf_op jit(solution)/shard_map/ppermute | solution.py:284
  127.6 4.0 %collective-permute-done.28 = bf16[32,3840]{1,0:T(8,128)(2,1)S(1)} collective-permute-done((bf16[32,3840]{1,0:T(8,128)(2,1)S(1)}, bf16[32,3840]{1,0:T(8,128)(2,1)S(1)}, u32[]{:S(2)}, u32[]{:S(2)}) %collective-permute-start.28) | collective-permute-done | bytes 245792 | tf_op jit(solution)/shard_map/ppermute | solution.py:284
  134.8 3.1 %collective-permute-done.29 = bf16[32,3840]{1,0:T(8,128)(2,1)S(1)} collective-permute-done((bf16[32,3840]{1,0:T(8,128)(2,1)S(1)}, bf16[32,3840]{1,0:T(8,128)(2,1)S(1)}, u32[]{:S(2)}, u32[]{:S(2)}) %collective-permute-start.29) | collective-permute-done | bytes 245792 | tf_op jit(solution)/shard_map/ppermute | solution.py:284
  138.1 3.2 %collective-permute-start.31 = (bf16[8,7168]{1,0:T(8,128)(2,1)S(1)}, bf16[8,7168]{1,0:T(8,128)(2,1)S(1)}, u32[]{:S(2)}, u32[]{:S(2)}) collective-permute-start(bf16[8,7168]{1,0:T(8,128)(2,1)S(1)} %get-tuple-element.88), channel_id=1, source_target_pairs={{0,3},{1,0},{2,1},{3,2},{4,5},{5,6},{6,7},{7,4},{8,11},{9,8},{10,9... | collective-permute-start | bytes 344072 | tf_op jit(solution)/shard_map/ppermute | solution.py:284
  144.1 3.5 %collective-permute-done.32 = bf16[8,7168]{1,0:T(8,128)(2,1)S(1)} collective-permute-done((bf16[8,7168]{1,0:T(8,128)(2,1)S(1)}, bf16[8,7168]{1,0:T(8,128)(2,1)S(1)}, u32[]{:S(2)}, u32[]{:S(2)}) %collective-permute-start.32) | collective-permute-done | bytes 114720 | tf_op jit(solution)/shard_map/ppermute | solution.py:284
  (85 shorter events, 43.8 us)
Async XLA Ops:
  0.6 13.1 %collective-permute-start.3 = (bf16[7168,256]{1,0:T(8,128)(2,1)}, bf16[7168,256]{1,0:T(8,128)(2,1)}, u32[]{:S(2)}, u32[]{:S(2)}) collective-permute-start(bf16[7168,256]{1,0:T(8,128)(2,1)} %bitcast.5), channel_id=1, source_target_pairs={{0,4},{4,0},{1,5},{5,1},{2,6},{6,2},{3,7},{7,3},{8,12},{12,8},{9,1... | collective-permute-start | bytes 11010056 | tf_op jit(solution)/shard_map/ppermute | solution.py:270
  0.7 13.0 %collective-permute-start.4 = (bf16[7168,256]{1,0:T(8,128)(2,1)}, bf16[7168,256]{1,0:T(8,128)(2,1)}, u32[]{:S(2)}, u32[]{:S(2)}) collective-permute-start(bf16[7168,256]{1,0:T(8,128)(2,1)} %bitcast.8), channel_id=1, source_target_pairs={{0,4},{4,0},{1,5},{5,1},{2,6},{6,2},{3,7},{7,3},{8,12},{12,8},{9,1... | collective-permute-start | bytes 11010056 | tf_op jit(solution)/shard_map/ppermute | solution.py:270
  13.7 9.9 %collective-permute-start.5 = (bf16[32,3584]{1,0:T(8,128)(2,1)S(1)}, bf16[32,3584]{1,0:T(8,128)(2,1)S(1)}, u32[]{:S(2)}, u32[]{:S(2)}) collective-permute-start(bf16[32,3584]{1,0:T(8,128)(2,1)S(1)} %slice.6), channel_id=1, source_target_pairs={{0,8},{8,16},{16,24},{24,0},{4,28},{12,4},{20,12},{28,20},{1,9},{9... | collective-permute-start | bytes 688136 | tf_op jit(solution)/shard_map/ppermute | solution.py:284
  14.3 12.9 %collective-permute-start.6 = (bf16[32,3584]{1,0:T(8,128)(2,1)S(1)}, bf16[32,3584]{1,0:T(8,128)(2,1)S(1)}, u32[]{:S(2)}, u32[]{:S(2)}) collective-permute-start(bf16[32,3584]{1,0:T(8,128)(2,1)S(1)} %slice.6), channel_id=1, source_target_pairs={{0,24},{8,0},{16,8},{24,16},{4,12},{12,20},{20,28},{28,4},{1,25},{... | collective-permute-start | bytes 688136 | tf_op jit(solution)/shard_map/ppermute | solution.py:284
  15.8 11.4 %collective-permute-start.7 = (bf16[32,3584]{1,0:T(8,128)(2,1)S(1)}, bf16[32,3584]{1,0:T(8,128)(2,1)S(1)}, u32[]{:S(2)}, u32[]{:S(2)}) collective-permute-start(bf16[32,3584]{1,0:T(8,128)(2,1)S(1)} %slice.6), channel_id=1, source_target_pairs={{0,16},{8,24},{16,0},{24,8},{4,20},{12,28},{20,4},{28,12},{1,17},{... | collective-permute-start | bytes 688136 | tf_op jit(solution)/shard_map/ppermute | solution.py:284
  18.7 10.2 %collective-permute-start.10 = (bf16[32,3712]{1,0:T(8,128)(2,1)S(1)}, bf16[32,3712]{1,0:T(8,128)(2,1)S(1)}, u32[]{:S(2)}, u32[]{:S(2)}) collective-permute-start(bf16[32,3712]{1,0:T(8,128)(2,1)S(1)} %slice.7), channel_id=1, source_target_pairs={{0,64},{32,96},{64,0},{96,32},{4,68},{36,100},{68,4},{100,36},{1,6... | collective-permute-start | bytes 712712 | tf_op jit(solution)/shard_map/ppermute | solution.py:284
  22.6 10.1 %collective-permute-start.8 = (bf16[32,3712]{1,0:T(8,128)(2,1)S(1)}, bf16[32,3712]{1,0:T(8,128)(2,1)S(1)}, u32[]{:S(2)}, u32[]{:S(2)}) collective-permute-start(bf16[32,3712]{1,0:T(8,128)(2,1)S(1)} %slice.7), channel_id=1, source_target_pairs={{0,32},{32,64},{64,96},{96,0},{4,100},{36,4},{68,36},{100,68},{1,3... | collective-permute-start | bytes 712712 | tf_op jit(solution)/shard_map/ppermute | solution.py:284
  23.7 9.8 %collective-permute-start.9 = (bf16[32,3712]{1,0:T(8,128)(2,1)S(1)}, bf16[32,3712]{1,0:T(8,128)(2,1)S(1)}, u32[]{:S(2)}, u32[]{:S(2)}) collective-permute-start(bf16[32,3712]{1,0:T(8,128)(2,1)S(1)} %slice.7), channel_id=1, source_target_pairs={{0,96},{32,0},{64,32},{96,64},{4,36},{36,68},{68,100},{100,4},{1,9... | collective-permute-start | bytes 712712 | tf_op jit(solution)/shard_map/ppermute | solution.py:284
  33.6 24.3 %collective-permute-start.17 = (bf16[256,7168]{1,0:T(8,128)(2,1)S(1)}, bf16[256,7168]{1,0:T(8,128)(2,1)S(1)}, u32[]{:S(2)}, u32[]{:S(2)}) collective-permute-start(bf16[256,7168]{1,0:T(8,128)(2,1)S(1)} %bitcast.12), channel_id=1, source_target_pairs={{0,4},{4,0},{1,5},{5,1},{2,6},{6,2},{3,7},{7,3},{8,12},{12,8},{9,1... | collective-permute-start | bytes 11010056 | tf_op jit(solution)/shard_map/ppermute | solution.py:270
  33.7 15.9 %collective-permute-start.14 = (bf16[128,3712]{1,0:T(8,128)(2,1)S(1)}, bf16[128,3712]{1,0:T(8,128)(2,1)S(1)}, u32[]{:S(2)}, u32[]{:S(2)}) collective-permute-start(bf16[128,3712]{1,0:T(8,128)(2,1)S(1)} %pad_maximum_fusion.refs_1_.b0), channel_id=1, source_target_pairs={{0,8},{8,16},{16,24},{24,0},{4,28},{12,4},{20,12},{28,20},{1,9},{9... | collective-permute-start | bytes 2850824 | tf_op jit(solution)/shard_map/ppermute | solution.py:284
  35.7 22.1 %collective-permute-start.12 = (bf16[128,3584]{1,0:T(8,128)(2,1)S(1)}, bf16[128,3584]{1,0:T(8,128)(2,1)S(1)}, u32[]{:S(2)}, u32[]{:S(2)}) collective-permute-start(bf16[128,3584]{1,0:T(8,128)(2,1)S(1)} %pad_maximum_fusion.1.refs_0_), channel_id=1, source_target_pairs={{0,32},{32,64},{64,96},{96,0},{4,100},{36,4},{68,36},{100,68},{1,3... | collective-permute-start | bytes 2752520 | tf_op jit(solution)/shard_map/ppermute | solution.py:284
  43.9 29.7 %collective-permute-start.15 = (bf16[128,3712]{1,0:T(8,128)(2,1)S(1)}, bf16[128,3712]{1,0:T(8,128)(2,1)S(1)}, u32[]{:S(2)}, u32[]{:S(2)}) collective-permute-start(bf16[128,3712]{1,0:T(8,128)(2,1)S(1)} %pad_maximum_fusion.refs_1_.b0), channel_id=1, source_target_pairs={{0,24},{8,0},{16,8},{24,16},{4,12},{12,20},{20,28},{28,4},{1,25},{... | collective-permute-start | bytes 2850824 | tf_op jit(solution)/shard_map/ppermute | solution.py:284
  49.6 24.0 %collective-permute-start.16 = (bf16[128,3712]{1,0:T(8,128)(2,1)S(1)}, bf16[128,3712]{1,0:T(8,128)(2,1)S(1)}, u32[]{:S(2)}, u32[]{:S(2)}) collective-permute-start(bf16[128,3712]{1,0:T(8,128)(2,1)S(1)} %collective-permute-done.14.b1), channel_id=1, source_target_pairs={{0,8},{8,16},{16,24},{24,0},{4,28},{12,4},{20,12},{28,20},{1,9},{9... | collective-permute-start | bytes 2850824 | tf_op jit(solution)/shard_map/ppermute | solution.py:284
  50.7 22.9 %collective-permute-start.11 = (bf16[128,3584]{1,0:T(8,128)(2,1)S(1)}, bf16[128,3584]{1,0:T(8,128)(2,1)S(1)}, u32[]{:S(2)}, u32[]{:S(2)}) collective-permute-start(bf16[128,3584]{1,0:T(8,128)(2,1)S(1)} %pad_maximum_fusion.1.refs_0_), channel_id=1, source_target_pairs={{0,96},{32,0},{64,32},{96,64},{4,36},{36,68},{68,100},{100,4},{1,9... | collective-permute-start | bytes 2752520 | tf_op jit(solution)/shard_map/ppermute | solution.py:284
  57.8 15.8 %collective-permute-start.13 = (bf16[128,3584]{1,0:T(8,128)(2,1)S(1)}, bf16[128,3584]{1,0:T(8,128)(2,1)S(1)}, u32[]{:S(2)}, u32[]{:S(2)}) collective-permute-start(bf16[128,3584]{1,0:T(8,128)(2,1)S(1)} %collective-permute-done.12.a1), channel_id=1, source_target_pairs={{0,32},{32,64},{64,96},{96,0},{4,100},{36,4},{68,36},{100,68},{1,3... | collective-permute-start | bytes 2752520 | tf_op jit(solution)/shard_map/ppermute | solution.py:284
  78.9 21.6 %collective-permute-start.19 = (bf16[128,3328]{1,0:T(8,128)(2,1)S(1)}, bf16[128,3328]{1,0:T(8,128)(2,1)S(1)}, u32[]{:S(2)}, u32[]{:S(2)}) collective-permute-start(bf16[128,3328]{1,0:T(8,128)(2,1)S(1)} %get-tuple-element.77), channel_id=1, source_target_pairs={{0,96},{32,0},{64,32},{96,64},{4,36},{36,68},{68,100},{100,4},{1,9... | collective-permute-start | bytes 2555912 | tf_op jit(solution)/shard_map/ppermute | solution.py:284
  81.7 25.1 %collective-permute-start.25 = (bf16[128,3840]{1,0:T(8,128)(2,1)S(1)}, bf16[128,3840]{1,0:T(8,128)(2,1)S(1)}, u32[]{:S(2)}, u32[]{:S(2)}) collective-permute-start(bf16[128,3840]{1,0:T(8,128)(2,1)S(1)} %get-tuple-element.81), channel_id=1, source_target_pairs={{0,24},{8,0},{16,8},{24,16},{4,12},{12,20},{20,28},{28,4},{1,25},{... | collective-permute-start | bytes 2949128 | tf_op jit(solution)/shard_map/ppermute | solution.py:284
  87.2 22.3 %collective-permute-start.18 = (bf16[128,3328]{1,0:T(8,128)(2,1)S(1)}, bf16[128,3328]{1,0:T(8,128)(2,1)S(1)}, u32[]{:S(2)}, u32[]{:S(2)}) collective-permute-start(bf16[128,3328]{1,0:T(8,128)(2,1)S(1)} %get-tuple-element.75), channel_id=1, source_target_pairs={{0,32},{32,64},{64,96},{96,0},{4,100},{36,4},{68,36},{100,68},{1,3... | collective-permute-start | bytes 2555912 | tf_op jit(solution)/shard_map/ppermute | solution.py:284
  87.3 31.0 %collective-permute-start.24 = (bf16[128,3840]{1,0:T(8,128)(2,1)S(1)}, bf16[128,3840]{1,0:T(8,128)(2,1)S(1)}, u32[]{:S(2)}, u32[]{:S(2)}) collective-permute-start(bf16[128,3840]{1,0:T(8,128)(2,1)S(1)} %get-tuple-element.79), channel_id=1, source_target_pairs={{0,8},{8,16},{16,24},{24,0},{4,28},{12,4},{20,12},{28,20},{1,9},{9... | collective-permute-start | bytes 2949128 | tf_op jit(solution)/shard_map/ppermute | solution.py:284
  100.7 14.0 %collective-permute-start.20 = (bf16[128,3328]{1,0:T(8,128)(2,1)S(1)}, bf16[128,3328]{1,0:T(8,128)(2,1)S(1)}, u32[]{:S(2)}, u32[]{:S(2)}) collective-permute-start(bf16[128,3328]{1,0:T(8,128)(2,1)S(1)} %add_convert_fusion.3), channel_id=1, source_target_pairs={{0,96},{32,0},{64,32},{96,64},{4,36},{36,68},{68,100},{100,4},{1,9... | collective-permute-start | bytes 2555912 | tf_op jit(solution)/shard_map/ppermute | solution.py:284
  107.0 17.9 %collective-permute-start.26 = (bf16[128,3840]{1,0:T(8,128)(2,1)S(1)}, bf16[128,3840]{1,0:T(8,128)(2,1)S(1)}, u32[]{:S(2)}, u32[]{:S(2)}) collective-permute-start(bf16[128,3840]{1,0:T(8,128)(2,1)S(1)} %add_convert_fusion.1), channel_id=1, source_target_pairs={{0,24},{8,0},{16,8},{24,16},{4,12},{12,20},{20,28},{28,4},{1,25},{... | collective-permute-start | bytes 2949128 | tf_op jit(solution)/shard_map/ppermute | solution.py:284
  115.0 12.2 %collective-permute-start.22 = (bf16[32,3328]{1,0:T(8,128)(2,1)S(1)}, bf16[32,3328]{1,0:T(8,128)(2,1)S(1)}, u32[]{:S(2)}, u32[]{:S(2)}) collective-permute-start(bf16[32,3328]{1,0:T(8,128)(2,1)S(1)} %get-tuple-element.85), channel_id=1, source_target_pairs={{0,24},{8,0},{16,8},{24,16},{4,12},{12,20},{20,28},{28,4},{1,25},{... | collective-permute-start | bytes 638984 | tf_op jit(solution)/shard_map/ppermute | solution.py:284
  116.5 17.1 %collective-permute-start.21 = (bf16[32,3328]{1,0:T(8,128)(2,1)S(1)}, bf16[32,3328]{1,0:T(8,128)(2,1)S(1)}, u32[]{:S(2)}, u32[]{:S(2)}) collective-permute-start(bf16[32,3328]{1,0:T(8,128)(2,1)S(1)} %get-tuple-element.84), channel_id=1, source_target_pairs={{0,8},{8,16},{16,24},{24,0},{4,28},{12,4},{20,12},{28,20},{1,9},{9... | collective-permute-start | bytes 638984 | tf_op jit(solution)/shard_map/ppermute | solution.py:284
  127.3 7.5 %collective-permute-start.27 = (bf16[32,3840]{1,0:T(8,128)(2,1)S(1)}, bf16[32,3840]{1,0:T(8,128)(2,1)S(1)}, u32[]{:S(2)}, u32[]{:S(2)}) collective-permute-start(bf16[32,3840]{1,0:T(8,128)(2,1)S(1)} %get-tuple-element.82), channel_id=1, source_target_pairs={{0,32},{32,64},{64,96},{96,0},{4,100},{36,4},{68,36},{100,68},{1,3... | collective-permute-start | bytes 737288 | tf_op jit(solution)/shard_map/ppermute | solution.py:284
  (14 other events, 96.8 us)

commit v6 on v4

--- a/solution.py
+++ b/solution.py
@@ -23,8 +23,8 @@
 ATT_ROWS = 1024
 HALF = WIDTH // 2
 K_STEP = 512
-RETURN = (3584, 3584)
-N_TILE = 896
+RETURN = (3328, 3840)
+N_TILE = 1024
 VMEM_LIMIT = 8 * 2**20
 STEPS = HALF // K_STEP
 D_STEP = WIDTH // STEPS
@@ -163,16 +163,6 @@
         out[...] = jnp.dot(stacked, held[start : start + HALF], preferred_element_type=F32)
 
 
-def send_blocks(hidden, down, low, outs):
-    width = outs[0].shape[1]
-    for start in range(0, width, N_TILE):
-        made = jnp.dot(
-            hidden[...], down[:, low + start : low + start + N_TILE], preferred_element_type=F32
-        ).astype(BF)
-        for place, out in enumerate(outs):
-            out[:, start : start + N_TILE] = made[place * PART : (place + 1) * PART]
-
-
 def late_kernel(a3, b0, b1, b2, b3, held, pick, own_a, own_b, early_a, early_b, out_a, out_b):
     last_a = jnp.dot(a3[...], held[:HALF], preferred_element_type=F32)
     last_b = jnp.dot(b3[:, :HALF], held[HALF:], preferred_element_type=F32)
@@ -198,8 +188,20 @@
             out_b[low_b : low_b + GROUP, :] = made
 
 
-def down_kernel(low, hidden, down, *outs):
-    send_blocks(hidden, down, low, outs)
+def down_kernel(low, high, hidden_a, hidden_b, down, *outs):
+    count = high - low
+    for half, hidden in enumerate((hidden_a, hidden_b)):
+        for start in range(0, RETURN[half], N_TILE):
+            stop = min(start + N_TILE, RETURN[half])
+            column = half * RETURN[0]
+            made = jnp.dot(
+                hidden[low * PART : high * PART],
+                down[:, column + start : column + stop],
+                preferred_element_type=F32,
+            ).astype(BF)
+            for place in range(count):
+                block = made[place * PART : (place + 1) * PART]
+                outs[half * count + place][:, start:stop] = block
 
 
 def sent_blocks(parts, own_sums, held, down, pick):
@@ -221,17 +223,20 @@
         (made, made),
         2 * PART * WIDTH * 4 * UNITS,
     )
-    def half(place, hidden):
-        return on_chip(
-            functools.partial(down_kernel, place * RETURN[0]),
+    def some(low, high, hidden):
+        count = high - low
+        blocks = on_chip(
+            functools.partial(down_kernel, low, high),
             "down",
-            (hidden, down),
-            [((PART, RETURN[place]), BF)] * 4,
-            2 * ROWS * 2 * UNITS * RETURN[place],
+            (*hidden, down),
+            [((PART, width), BF) for width in RETURN for _ in range(count)],
+            2 * count * PART * 2 * UNITS * WIDTH,
         )
-
-    first, hidden = lax.optimization_barrier((half(0, halves[0]), halves[1]))
-    return [first, half(1, hidden)]
+        return blocks[:count], blocks[count:]
+
+    (far_a, far_b), halves = lax.optimization_barrier((some(3, 4, halves), halves))
+    rest_a, rest_b = some(0, 3, halves)
+    return [[*rest_a, *far_a], [*rest_b, *far_b]]
 
 
 def swap(array):

time: 148 us -> 147 us (level)
  waiting for transfers between devices: 59.5 us -> 67.2 us
  starting transfers between devices: 50.6 us -> 43.3 us
    ppermute x30, waiting for transfers between devices: 59.5 us -> 67.2 us  [move(): return lax.ppermute(array, names, pairs)]
    ppermute x30, starting transfers between devices: 49.9 us -> 42.6 us  [move(): return lax.ppermute(array, names, pairs)]
  transfers between devices with their start and end apart: 33 -> 33, of which waited for: 17 -> 20; matrix products, arithmetic and copies ran while one was open for 4% -> 4% of each run, Pallas kernels for 12% -> 14%
where the time goes in v6:
time: 147 us
  waiting for transfers between devices  67.2 us (46%)
  starting transfers between devices  43.3 us (29%)
  Pallas kernels  24.2 us (16%)
  local copies, waits for them, and re-layouts  6.87 us (5%)
  other arithmetic  4.19 us (3%)
    ppermute x30, waiting for transfers between devices, move(): return lax.ppermute(array, names, pairs)  67.2 us
    ppermute x30, starting transfers between devices, move(): return lax.ppermute(array, names, pairs)  42.6 us
    pallas_call x4, Pallas kernels, on_chip(): pl.pallas_call(kernel, in_specs=[spec] * len(operands), out_specs=[spec]...  11.8 us
    pallas_call x1, Pallas kernels, own_part(): pl.pallas_call(own_kernel, grid=(STEPS,), in_specs=[block] * 2 + [first]...  8.51 us
    unnamed x8, local copies, waits for them, and re-layouts  4.38 us
    pallas_call x1, Pallas kernels, attend(): pl.pallas_call(attend_kernel, grid_spec=pltpu.PrefetchScalarGridSpec(num_...  3.85 us
  transfers between devices with their start and end apart: 33, of which 20 were waited for; matrix products, arithmetic and copies ran while one was open for 4% of the time, Pallas kernels for 14%

profile of v6, /device:TPU:6, one launch (start us, length us, event | category | flops | bytes accessed | tf_op | source)
XLA Modules:
  0.0 146.6 jit_solution(2397192236791334087)
XLA Ops:
  9.4 4.2 %collective-permute-done.2 = bf16[8,7296]{1,0:T(8,128)(2,1)S(1)} collective-permute-done((bf16[8,7296]{1,0:T(8,128)(2,1)S(1)}, bf16[8,7296]{1,0:T(8,128)(2,1)S(1)}, u32[]{:S(2)}, u32[]{:S(2)}) %collective-permute-start.2) | collective-permute-done | bytes 116768 | tf_op jit(solution)/shard_map/ppermute | solution.py:257
  18.7 4.0 %collective-permute-start.10 = (bf16[32,3712]{1,0:T(8,128)(2,1)S(1)}, bf16[32,3712]{1,0:T(8,128)(2,1)S(1)}, u32[]{:S(2)}, u32[]{:S(2)}) collective-permute-start(bf16[32,3712]{1,0:T(8,128)(2,1)S(1)} %slice.7), channel_id=1, source_target_pairs={{0,64},{32,96},{64,0},{96,32},{4,68},{36,100},{68,4},{100,36},{1,6... | collective-permute-start | bytes 712712 | tf_op jit(solution)/shard_map/ppermute | solution.py:257
  23.6 2.6 %collective-permute-start.9 = (bf16[32,3712]{1,0:T(8,128)(2,1)S(1)}, bf16[32,3712]{1,0:T(8,128)(2,1)S(1)}, u32[]{:S(2)}, u32[]{:S(2)}) collective-permute-start(bf16[32,3712]{1,0:T(8,128)(2,1)S(1)} %slice.7), channel_id=1, source_target_pairs={{0,96},{32,0},{64,32},{96,64},{4,36},{36,68},{68,100},{100,4},{1,9... | collective-permute-start | bytes 712712 | tf_op jit(solution)/shard_map/ppermute | solution.py:257
  28.9 3.8 %collective-permute-done.8 = bf16[32,3712]{1,0:T(8,128)(2,1)S(1)} collective-permute-done((bf16[32,3712]{1,0:T(8,128)(2,1)S(1)}, bf16[32,3712]{1,0:T(8,128)(2,1)S(1)}, u32[]{:S(2)}, u32[]{:S(2)}) %collective-permute-start.8) | collective-permute-done | bytes 237600 | tf_op jit(solution)/shard_map/ppermute | solution.py:257
  36.7 2.2 %collective-permute-start.17 = (bf16[128,3584]{1,0:T(8,128)(2,1)}, bf16[128,3584]{1,0:T(8,128)(2,1)}, u32[]{:S(2)}, u32[]{:S(2)}) collective-permute-start(bf16[128,3584]{1,0:T(8,128)(2,1)} %pad_maximum_fusion.1.refs_0_), channel_id=1, source_target_pairs={{0,96},{32,0},{64,32},{96,64},{4,36},{36,68},{68,100},{100,4},{1,9... | collective-permute-start | bytes 2752520 | tf_op jit(solution)/shard_map/ppermute | solution.py:257
  39.1 2.3 %copy-done.2 = bf16[4096,576]{0,1:T(8,128)(2,1)S(1)} copy-done((bf16[4096,576]{0,1:T(8,128)(2,1)S(1)}, bf16[4096,576]{0,1:T(8,128)(2,1)}, u32[]{:S(2)}) %copy-start.2) | copy-done | bytes 4718616
  41.5 3.8 %attend.1 = bf16[1,128,512]{2,1,0:T(8,128)(2,1)} custom-call(s32[1]{0:T(128)} %dynamic_slice.3.length_ref, bf16[1,128,576]{2,1,0:T(8,128)(2,1)S(1)} %copy.13.query_ref, bf16[576,4096]{1,0:T(8,128)(2,1)S(1)} %bitcast.10), custom_call_target="tpu_custom_call" | custom-call | flops 1140850688 | bytes 4718592 | tf_op jit(solution)/shard_map/attend/pallas_call | solution.py:74
  47.4 8.5 %own.1 = (f32[128,1024]{1,0:T(8,128)S(1)}, f32[128,1024]{1,0:T(8,128)S(1)}, bf16[7168,1024]{1,0:T(8,128)(2,1)S(1)}, bf16[512,7168]{1,0:T(8,128)(2,1)S(1)}) custom-call(bf16[128,3584]{1,0:T(8,128)(2,1)} %pad_maximum_fusion.1.refs_0_, bf16[128,3712]{1,0:T(8,128)(2,1)S(1)} %pad_maximum_fusion.refs_1_.b0, bf16[7168,256]{1,0:T(8,128)(2,1)S(1)} %bitcast.5, ...), custom_call_target="tpu_custom_call" | custom-call | flops 1879048192 | bytes 23855104 | tf_op jit(solution)/shard_map/own/pallas_call | solution.py:129
  58.0 2.7 %collective-permute-start.16 = (bf16[128,3712]{1,0:T(8,128)(2,1)S(1)}, bf16[128,3712]{1,0:T(8,128)(2,1)S(1)}, u32[]{:S(2)}, u32[]{:S(2)}) collective-permute-start(bf16[128,3712]{1,0:T(8,128)(2,1)S(1)} %collective-permute-done.12.b1), channel_id=1, source_target_pairs={{0,8},{8,16},{16,24},{24,0},{4,28},{12,4},{20,12},{28,20},{1,9},{9... | collective-permute-start | bytes 2850824 | tf_op jit(solution)/shard_map/ppermute | solution.py:257
  61.3 5.4 %early.1 = (f32[256,1024]{1,0:T(8,128)S(1)}, f32[256,1024]{1,0:T(8,128)S(1)}, bf16[7168,1024]{1,0:T(8,128)(2,1)S(1)}) custom-call(bf16[128,3584]{1,0:T(8,128)(2,1)} %collective-permute-done.11.a1, bf16[128,3584]{1,0:T(8,128)(2,1)} %collective-permute-done.17.a2, bf16[128,3712]{1,0:T(8,128)(2,1)S(1)} %collective-permute-done.12.b1, ...), custom_call_target="tpu_custom_call", output_to_operand_aliasing={{2}: (4, {})} | custom-call | flops 3758096384 | tf_op jit(solution)/shard_map/early/pallas_call | solution.py:148
  66.7 8.8 %collective-permute-done.14.a3 = bf16[128,3584]{1,0:T(8,128)(2,1)S(1)} collective-permute-done((bf16[128,3584]{1,0:T(8,128)(2,1)}, bf16[128,3584]{1,0:T(8,128)(2,1)S(1)}, u32[]{:S(2)}, u32[]{:S(2)}) %collective-permute-start.14) | collective-permute-done | bytes 917536 | tf_op jit(solution)/shard_map/ppermute | solution.py:257
  75.5 2.3 %late.1 = (bf16[512,512]{1,0:T(8,128)(2,1)S(1)}, bf16[512,512]{1,0:T(8,128)(2,1)S(1)}) custom-call(bf16[128,3584]{1,0:T(8,128)(2,1)S(1)} %collective-permute-done.14.a3, bf16[128,3712]{1,0:T(8,128)(2,1)S(1)} %pad_maximum_fusion.refs_1_.b0, bf16[128,3712]{1,0:T(8,128)(2,1)S(1)} %collective-permute-done.12.b1, ...), custom_call_target="tpu_custom_call" | custom-call | flops 1879048192 | tf_op jit(solution)/shard_map/late/pallas_call | solution.py:148
  80.7 3.0 %down.3 = (bf16[128,3328]{1,0:T(8,128)(2,1)S(1)}, bf16[128,3328]{1,0:T(8,128)(2,1)S(1)}, bf16[128,3328]{1,0:T(8,128)(2,1)S(1)}, bf16[128,3840]{1,0:T(8,128)(2,1)...) custom-call(bf16[512,512]{1,0:T(8,128)(2,1)S(1)} %get-tuple-element.62.hidden_a, ...), custom_call_target="tpu_custom_call" | custom-call | flops 2818572288 | tf_op jit(solution)/shard_map/down/pallas_call | solution.py:148
  84.1 3.3 %collective-permute-start.24 = (bf16[128,3840]{1,0:T(8,128)(2,1)S(1)}, bf16[128,3840]{1,0:T(8,128)(2,1)S(1)}, u32[]{:S(2)}, u32[]{:S(2)}) collective-permute-start(bf16[128,3840]{1,0:T(8,128)(2,1)S(1)} %get-tuple-element.69), channel_id=1, source_target_pairs={{0,8},{8,16},{16,24},{24,0},{4,28},{12,4},{20,12},{28,20},{1,9},{9... | collective-permute-start | bytes 2949128 | tf_op jit(solution)/shard_map/ppermute | solution.py:257
  87.4 12.2 %collective-permute-done.19 = bf16[128,3328]{1,0:T(8,128)(2,1)S(1)} collective-permute-done((bf16[128,3328]{1,0:T(8,128)(2,1)S(1)}, bf16[128,3328]{1,0:T(8,128)(2,1)S(1)}, u32[]{:S(2)}, u32[]{:S(2)}) %collective-permute-start.19) | collective-permute-done | bytes 852000 | tf_op jit(solution)/shard_map/ppermute | solution.py:257
  99.8 2.6 %collective-permute-start.20 = (bf16[128,3328]{1,0:T(8,128)(2,1)S(1)}, bf16[128,3328]{1,0:T(8,128)(2,1)S(1)}, u32[]{:S(2)}, u32[]{:S(2)}) collective-permute-start(bf16[128,3328]{1,0:T(8,128)(2,1)S(1)} %add_convert_fusion.3), channel_id=1, source_target_pairs={{0,96},{32,0},{64,32},{96,64},{4,36},{36,68},{68,100},{100,4},{1,9... | collective-permute-start | bytes 2555912 | tf_op jit(solution)/shard_map/ppermute | solution.py:257
  102.4 2.9 %collective-permute-done.25 = bf16[128,3840]{1,0:T(8,128)(2,1)S(1)} collective-permute-done((bf16[128,3840]{1,0:T(8,128)(2,1)S(1)}, bf16[128,3840]{1,0:T(8,128)(2,1)S(1)}, u32[]{:S(2)}, u32[]{:S(2)}) %collective-permute-start.25) | collective-permute-done | bytes 983072 | tf_op jit(solution)/shard_map/ppermute | solution.py:257
  105.6 7.0 %collective-permute-done.20 = bf16[128,3328]{1,0:T(8,128)(2,1)S(1)} collective-permute-done((bf16[128,3328]{1,0:T(8,128)(2,1)S(1)}, bf16[128,3328]{1,0:T(8,128)(2,1)S(1)}, u32[]{:S(2)}, u32[]{:S(2)}) %collective-permute-start.20) | collective-permute-done | bytes 852000 | tf_op jit(solution)/shard_map/ppermute | solution.py:257
  113.1 3.1 %collective-permute-start.21 = (bf16[32,3328]{1,0:T(8,128)(2,1)S(1)}, bf16[32,3328]{1,0:T(8,128)(2,1)S(1)}, u32[]{:S(2)}, u32[]{:S(2)}) collective-permute-start(bf16[32,3328]{1,0:T(8,128)(2,1)S(1)} %get-tuple-element.74), channel_id=1, source_target_pairs={{0,8},{8,16},{16,24},{24,0},{4,28},{12,4},{20,12},{28,20},{1,9},{9... | collective-permute-start | bytes 638984 | tf_op jit(solution)/shard_map/ppermute | solution.py:257
  116.3 6.9 %collective-permute-done.26 = bf16[128,3840]{1,0:T(8,128)(2,1)S(1)} collective-permute-done((bf16[128,3840]{1,0:T(8,128)(2,1)S(1)}, bf16[128,3840]{1,0:T(8,128)(2,1)S(1)}, u32[]{:S(2)}, u32[]{:S(2)}) %collective-permute-start.26) | collective-permute-done | bytes 983072 | tf_op jit(solution)/shard_map/ppermute | solution.py:257
  125.9 4.0 %collective-permute-done.28 = bf16[32,3840]{1,0:T(8,128)(2,1)S(1)} collective-permute-done((bf16[32,3840]{1,0:T(8,128)(2,1)S(1)}, bf16[32,3840]{1,0:T(8,128)(2,1)S(1)}, u32[]{:S(2)}, u32[]{:S(2)}) %collective-permute-start.28) | collective-permute-done | bytes 245792 | tf_op jit(solution)/shard_map/ppermute | solution.py:257
  133.1 3.1 %collective-permute-done.29 = bf16[32,3840]{1,0:T(8,128)(2,1)S(1)} collective-permute-done((bf16[32,3840]{1,0:T(8,128)(2,1)S(1)}, bf16[32,3840]{1,0:T(8,128)(2,1)S(1)}, u32[]{:S(2)}, u32[]{:S(2)}) %collective-permute-start.29) | collective-permute-done | bytes 245792 | tf_op jit(solution)/shard_map/ppermute | solution.py:257
  137.5 2.1 %collective-permute-start.31 = (bf16[8,7168]{1,0:T(8,128)(2,1)S(1)}, bf16[8,7168]{1,0:T(8,128)(2,1)S(1)}, u32[]{:S(2)}, u32[]{:S(2)}) collective-permute-start(bf16[8,7168]{1,0:T(8,128)(2,1)S(1)} %get-tuple-element.78), channel_id=1, source_target_pairs={{0,3},{1,0},{2,1},{3,2},{4,5},{5,6},{6,7},{7,4},{8,11},{9,8},{10,9... | collective-permute-start | bytes 344072 | tf_op jit(solution)/shard_map/ppermute | solution.py:257
  142.4 3.5 %collective-permute-done.32 = bf16[8,7168]{1,0:T(8,128)(2,1)S(1)} collective-permute-done((bf16[8,7168]{1,0:T(8,128)(2,1)S(1)}, bf16[8,7168]{1,0:T(8,128)(2,1)S(1)}, u32[]{:S(2)}, u32[]{:S(2)}) %collective-permute-start.32) | collective-permute-done | bytes 114720 | tf_op jit(solution)/shard_map/ppermute | solution.py:257
  (83 shorter events, 41.3 us)
Async XLA Ops:
  0.6 13.1 %collective-permute-start.3 = (bf16[7168,256]{1,0:T(8,128)(2,1)}, bf16[7168,256]{1,0:T(8,128)(2,1)}, u32[]{:S(2)}, u32[]{:S(2)}) collective-permute-start(bf16[7168,256]{1,0:T(8,128)(2,1)} %bitcast.4), channel_id=1, source_target_pairs={{0,4},{4,0},{1,5},{5,1},{2,6},{6,2},{3,7},{7,3},{8,12},{12,8},{9,1... | collective-permute-start | bytes 11010056 | tf_op jit(solution)/shard_map/ppermute | solution.py:243
  0.7 13.0 %collective-permute-start.4 = (bf16[7168,256]{1,0:T(8,128)(2,1)}, bf16[7168,256]{1,0:T(8,128)(2,1)}, u32[]{:S(2)}, u32[]{:S(2)}) collective-permute-start(bf16[7168,256]{1,0:T(8,128)(2,1)} %bitcast.7), channel_id=1, source_target_pairs={{0,4},{4,0},{1,5},{5,1},{2,6},{6,2},{3,7},{7,3},{8,12},{12,8},{9,1... | collective-permute-start | bytes 11010056 | tf_op jit(solution)/shard_map/ppermute | solution.py:243
  13.7 9.9 %collective-permute-start.5 = (bf16[32,3584]{1,0:T(8,128)(2,1)S(1)}, bf16[32,3584]{1,0:T(8,128)(2,1)S(1)}, u32[]{:S(2)}, u32[]{:S(2)}) collective-permute-start(bf16[32,3584]{1,0:T(8,128)(2,1)S(1)} %slice.6), channel_id=1, source_target_pairs={{0,8},{8,16},{16,24},{24,0},{4,28},{12,4},{20,12},{28,20},{1,9},{9... | collective-permute-start | bytes 688136 | tf_op jit(solution)/shard_map/ppermute | solution.py:257
  14.3 12.9 %collective-permute-start.6 = (bf16[32,3584]{1,0:T(8,128)(2,1)S(1)}, bf16[32,3584]{1,0:T(8,128)(2,1)S(1)}, u32[]{:S(2)}, u32[]{:S(2)}) collective-permute-start(bf16[32,3584]{1,0:T(8,128)(2,1)S(1)} %slice.6), channel_id=1, source_target_pairs={{0,24},{8,0},{16,8},{24,16},{4,12},{12,20},{20,28},{28,4},{1,25},{... | collective-permute-start | bytes 688136 | tf_op jit(solution)/shard_map/ppermute | solution.py:257
  15.8 11.4 %collective-permute-start.7 = (bf16[32,3584]{1,0:T(8,128)(2,1)S(1)}, bf16[32,3584]{1,0:T(8,128)(2,1)S(1)}, u32[]{:S(2)}, u32[]{:S(2)}) collective-permute-start(bf16[32,3584]{1,0:T(8,128)(2,1)S(1)} %slice.6), channel_id=1, source_target_pairs={{0,16},{8,24},{16,0},{24,8},{4,20},{12,28},{20,4},{28,12},{1,17},{... | collective-permute-start | bytes 688136 | tf_op jit(solution)/shard_map/ppermute | solution.py:257
  18.7 10.2 %collective-permute-start.10 = (bf16[32,3712]{1,0:T(8,128)(2,1)S(1)}, bf16[32,3712]{1,0:T(8,128)(2,1)S(1)}, u32[]{:S(2)}, u32[]{:S(2)}) collective-permute-start(bf16[32,3712]{1,0:T(8,128)(2,1)S(1)} %slice.7), channel_id=1, source_target_pairs={{0,64},{32,96},{64,0},{96,32},{4,68},{36,100},{68,4},{100,36},{1,6... | collective-permute-start | bytes 712712 | tf_op jit(solution)/shard_map/ppermute | solution.py:257
  22.6 10.1 %collective-permute-start.8 = (bf16[32,3712]{1,0:T(8,128)(2,1)S(1)}, bf16[32,3712]{1,0:T(8,128)(2,1)S(1)}, u32[]{:S(2)}, u32[]{:S(2)}) collective-permute-start(bf16[32,3712]{1,0:T(8,128)(2,1)S(1)} %slice.7), channel_id=1, source_target_pairs={{0,32},{32,64},{64,96},{96,0},{4,100},{36,4},{68,36},{100,68},{1,3... | collective-permute-start | bytes 712712 | tf_op jit(solution)/shard_map/ppermute | solution.py:257
  23.6 9.8 %collective-permute-start.9 = (bf16[32,3712]{1,0:T(8,128)(2,1)S(1)}, bf16[32,3712]{1,0:T(8,128)(2,1)S(1)}, u32[]{:S(2)}, u32[]{:S(2)}) collective-permute-start(bf16[32,3712]{1,0:T(8,128)(2,1)S(1)} %slice.7), channel_id=1, source_target_pairs={{0,96},{32,0},{64,32},{96,64},{4,36},{36,68},{68,100},{100,4},{1,9... | collective-permute-start | bytes 712712 | tf_op jit(solution)/shard_map/ppermute | solution.py:257
  33.5 11.8 %collective-permute-start.13 = (bf16[256,7168]{1,0:T(8,128)(2,1)}, bf16[256,7168]{1,0:T(8,128)(2,1)}, u32[]{:S(2)}, u32[]{:S(2)}) collective-permute-start(bf16[256,7168]{1,0:T(8,128)(2,1)} %bitcast.2.refs_10_), channel_id=1, source_target_pairs={{0,4},{4,0},{1,5},{5,1},{2,6},{6,2},{3,7},{7,3},{8,12},{12,8},{9,1... | collective-permute-start | bytes 11010056 | tf_op jit(solution)/shard_map/ppermute | solution.py:243
  33.6 24.3 %collective-permute-start.12 = (bf16[128,3712]{1,0:T(8,128)(2,1)S(1)}, bf16[128,3712]{1,0:T(8,128)(2,1)S(1)}, u32[]{:S(2)}, u32[]{:S(2)}) collective-permute-start(bf16[128,3712]{1,0:T(8,128)(2,1)S(1)} %pad_maximum_fusion.refs_1_.b0), channel_id=1, source_target_pairs={{0,8},{8,16},{16,24},{24,0},{4,28},{12,4},{20,12},{28,20},{1,9},{9... | collective-permute-start | bytes 2850824 | tf_op jit(solution)/shard_map/ppermute | solution.py:257
  35.7 22.2 %collective-permute-start.11 = (bf16[128,3584]{1,0:T(8,128)(2,1)}, bf16[128,3584]{1,0:T(8,128)(2,1)}, u32[]{:S(2)}, u32[]{:S(2)}) collective-permute-start(bf16[128,3584]{1,0:T(8,128)(2,1)} %pad_maximum_fusion.1.refs_0_), channel_id=1, source_target_pairs={{0,32},{32,64},{64,96},{96,0},{4,100},{36,4},{68,36},{100,68},{1,3... | collective-permute-start | bytes 2752520 | tf_op jit(solution)/shard_map/ppermute | solution.py:257
  36.7 24.6 %collective-permute-start.15 = (bf16[128,3712]{1,0:T(8,128)(2,1)S(1)}, bf16[128,3712]{1,0:T(8,128)(2,1)S(1)}, u32[]{:S(2)}, u32[]{:S(2)}) collective-permute-start(bf16[128,3712]{1,0:T(8,128)(2,1)S(1)} %pad_maximum_fusion.refs_1_.b0), channel_id=1, source_target_pairs={{0,24},{8,0},{16,8},{24,16},{4,12},{12,20},{20,28},{28,4},{1,25},{... | collective-permute-start | bytes 2850824 | tf_op jit(solution)/shard_map/ppermute | solution.py:257
  36.7 24.6 %collective-permute-start.17 = (bf16[128,3584]{1,0:T(8,128)(2,1)}, bf16[128,3584]{1,0:T(8,128)(2,1)}, u32[]{:S(2)}, u32[]{:S(2)}) collective-permute-start(bf16[128,3584]{1,0:T(8,128)(2,1)} %pad_maximum_fusion.1.refs_0_), channel_id=1, source_target_pairs={{0,96},{32,0},{64,32},{96,64},{4,36},{36,68},{68,100},{100,4},{1,9... | collective-permute-start | bytes 2752520 | tf_op jit(solution)/shard_map/ppermute | solution.py:257
  58.0 17.6 %collective-permute-start.16 = (bf16[128,3712]{1,0:T(8,128)(2,1)S(1)}, bf16[128,3712]{1,0:T(8,128)(2,1)S(1)}, u32[]{:S(2)}, u32[]{:S(2)}) collective-permute-start(bf16[128,3712]{1,0:T(8,128)(2,1)S(1)} %collective-permute-done.12.b1), channel_id=1, source_target_pairs={{0,8},{8,16},{16,24},{24,0},{4,28},{12,4},{20,12},{28,20},{1,9},{9... | collective-permute-start | bytes 2850824 | tf_op jit(solution)/shard_map/ppermute | solution.py:257
  60.7 14.8 %collective-permute-start.14 = (bf16[128,3584]{1,0:T(8,128)(2,1)}, bf16[128,3584]{1,0:T(8,128)(2,1)S(1)}, u32[]{:S(2)}, u32[]{:S(2)}) collective-permute-start(bf16[128,3584]{1,0:T(8,128)(2,1)} %collective-permute-done.11.a1), channel_id=1, source_target_pairs={{0,32},{32,64},{64,96},{96,0},{4,100},{36,4},{68,36},{100,68},{1,3... | collective-permute-start | bytes 2752520 | tf_op jit(solution)/shard_map/ppermute | solution.py:257
  78.9 20.7 %collective-permute-start.19 = (bf16[128,3328]{1,0:T(8,128)(2,1)S(1)}, bf16[128,3328]{1,0:T(8,128)(2,1)S(1)}, u32[]{:S(2)}, u32[]{:S(2)}) collective-permute-start(bf16[128,3328]{1,0:T(8,128)(2,1)S(1)} %get-tuple-element.67), channel_id=1, source_target_pairs={{0,96},{32,0},{64,32},{96,64},{4,36},{36,68},{68,100},{100,4},{1,9... | collective-permute-start | bytes 2555912 | tf_op jit(solution)/shard_map/ppermute | solution.py:257
  80.1 25.2 %collective-permute-start.25 = (bf16[128,3840]{1,0:T(8,128)(2,1)S(1)}, bf16[128,3840]{1,0:T(8,128)(2,1)S(1)}, u32[]{:S(2)}, u32[]{:S(2)}) collective-permute-start(bf16[128,3840]{1,0:T(8,128)(2,1)S(1)} %get-tuple-element.71), channel_id=1, source_target_pairs={{0,24},{8,0},{16,8},{24,16},{4,12},{12,20},{20,28},{28,4},{1,25},{... | collective-permute-start | bytes 2949128 | tf_op jit(solution)/shard_map/ppermute | solution.py:257
  83.8 21.8 %collective-permute-start.18 = (bf16[128,3328]{1,0:T(8,128)(2,1)S(1)}, bf16[128,3328]{1,0:T(8,128)(2,1)S(1)}, u32[]{:S(2)}, u32[]{:S(2)}) collective-permute-start(bf16[128,3328]{1,0:T(8,128)(2,1)S(1)} %get-tuple-element.65), channel_id=1, source_target_pairs={{0,32},{32,64},{64,96},{96,0},{4,100},{36,4},{68,36},{100,68},{1,3... | collective-permute-start | bytes 2555912 | tf_op jit(solution)/shard_map/ppermute | solution.py:257
  84.1 32.1 %collective-permute-start.24 = (bf16[128,3840]{1,0:T(8,128)(2,1)S(1)}, bf16[128,3840]{1,0:T(8,128)(2,1)S(1)}, u32[]{:S(2)}, u32[]{:S(2)}) collective-permute-start(bf16[128,3840]{1,0:T(8,128)(2,1)S(1)} %get-tuple-element.69), channel_id=1, source_target_pairs={{0,8},{8,16},{16,24},{24,0},{4,28},{12,4},{20,12},{28,20},{1,9},{9... | collective-permute-start | bytes 2949128 | tf_op jit(solution)/shard_map/ppermute | solution.py:257
  99.8 12.8 %collective-permute-start.20 = (bf16[128,3328]{1,0:T(8,128)(2,1)S(1)}, bf16[128,3328]{1,0:T(8,128)(2,1)S(1)}, u32[]{:S(2)}, u32[]{:S(2)}) collective-permute-start(bf16[128,3328]{1,0:T(8,128)(2,1)S(1)} %add_convert_fusion.3), channel_id=1, source_target_pairs={{0,96},{32,0},{64,32},{96,64},{4,36},{36,68},{68,100},{100,4},{1,9... | collective-permute-start | bytes 2555912 | tf_op jit(solution)/shard_map/ppermute | solution.py:257
  105.5 17.7 %collective-permute-start.26 = (bf16[128,3840]{1,0:T(8,128)(2,1)S(1)}, bf16[128,3840]{1,0:T(8,128)(2,1)S(1)}, u32[]{:S(2)}, u32[]{:S(2)}) collective-permute-start(bf16[128,3840]{1,0:T(8,128)(2,1)S(1)} %add_convert_fusion.1), channel_id=1, source_target_pairs={{0,24},{8,0},{16,8},{24,16},{4,12},{12,20},{20,28},{28,4},{1,25},{... | collective-permute-start | bytes 2949128 | tf_op jit(solution)/shard_map/ppermute | solution.py:257
  113.0 12.5 %collective-permute-start.22 = (bf16[32,3328]{1,0:T(8,128)(2,1)S(1)}, bf16[32,3328]{1,0:T(8,128)(2,1)S(1)}, u32[]{:S(2)}, u32[]{:S(2)}) collective-permute-start(bf16[32,3328]{1,0:T(8,128)(2,1)S(1)} %get-tuple-element.75), channel_id=1, source_target_pairs={{0,24},{8,0},{16,8},{24,16},{4,12},{12,20},{20,28},{28,4},{1,25},{... | collective-permute-start | bytes 638984 | tf_op jit(solution)/shard_map/ppermute | solution.py:257
  113.1 18.0 %collective-permute-start.21 = (bf16[32,3328]{1,0:T(8,128)(2,1)S(1)}, bf16[32,3328]{1,0:T(8,128)(2,1)S(1)}, u32[]{:S(2)}, u32[]{:S(2)}) collective-permute-start(bf16[32,3328]{1,0:T(8,128)(2,1)S(1)} %get-tuple-element.74), channel_id=1, source_target_pairs={{0,8},{8,16},{16,24},{24,0},{4,28},{12,4},{20,12},{28,20},{1,9},{9... | collective-permute-start | bytes 638984 | tf_op jit(solution)/shard_map/ppermute | solution.py:257
  125.6 7.5 %collective-permute-start.27 = (bf16[32,3840]{1,0:T(8,128)(2,1)S(1)}, bf16[32,3840]{1,0:T(8,128)(2,1)S(1)}, u32[]{:S(2)}, u32[]{:S(2)}) collective-permute-start(bf16[32,3840]{1,0:T(8,128)(2,1)S(1)} %get-tuple-element.72), channel_id=1, source_target_pairs={{0,32},{32,64},{64,96},{96,0},{4,100},{36,4},{68,36},{100,68},{1,3... | collective-permute-start | bytes 737288 | tf_op jit(solution)/shard_map/ppermute | solution.py:257
  (13 other events, 83.7 us)
